TPU v7x, 32 devices: a whole 2x2x4 slice. The times are simulated.
32 devices in a mesh: groups: 2 (over y), fsdp: 4 (over x, core), dp: 4 (over z).
Axes of the slice: x: 2, y: 2, z: 4, core: 2. Of those that a mesh axis runs over, the one named last changes fastest.
Arguments:
- inputs: bfloat16 [4096, 8192], P(('groups', 'dp'), 'fsdp'), parts along dimension 0, may hold values from -6 to 6
- cotangent: bfloat16 [4096, 1024], P(('groups', 'dp'), 'fsdp'), parts along dimension 0, may hold values from -1.1953125 to 1.1953125
- frozen_key_weight: bfloat16 [8192, 1024], P(('fsdp', 'dp')), may hold values from -0.1875 to 0.1875
- adapter_down_weight: bfloat16 [128, 16, 8192], P(('groups', 'dp'), None, 'fsdp'), parts along dimension 0, may hold values from -0.119628906 to 0.119628906
- adapter_up_weight: bfloat16 [128, 16, 1024], P(('groups', 'dp')), parts along dimension 0, may hold values from -0.1875 to 0.1875
- row_adapter_index: int32 [4096, 1], P(('groups', 'dp')), parts along dimension 0, may hold values from 0 to 63; in each aligned block of 512 rows (0 to 511, 512 to 1023, ...) at most 16 rows name the same one
- adapter_slot_index: int32 [128], P('groups'), parts along dimension 0, may hold values from 0 to 63, each once
Outputs:
- input_grad: bfloat16 [4096, 8192], P(('groups', 'dp'), 'fsdp'), parts along dimension 0
- down_grad: bfloat16 [128, 16, 8192], P(('groups', 'dp'), None, 'fsdp'), parts along dimension 0
- up_grad: bfloat16 [128, 16, 1024], P(('groups', 'dp'), None, 'fsdp'), parts along dimension 0
There are 2 independent parts, one for each index of `groups`. A program takes and returns all parts, laid end to end along the dimension named above; an argument that names none is the same for every part. Nothing has to cross between parts.
Inputs may be any that keep to these rules, and one draw needn't show every extreme that they name: `row_adapter_index`: among the rows of one index of dp (aligned blocks of 512 rows) no adapter is named by more than 16 rows, a bound that some block reaches. `adapter_slot_index`: a permutation: each slot holds one adapter; slot s lies on index s // 16 of dp.
All inputs are finite; a program needn't handle non-finite values.
Results may differ from a plain program's by a relative error of at most 0.005.
Values may be sent and summed in bfloat16 or wider, within the bound.
No kernel may reach another device: no remote copies, remote signals or barrier semaphores. Data moves between devices by JAX's collectives and lax.ppermute only.
A program may use at most 128 MiB of HBM per device.

v0:
```python
import jax
import jax.numpy as jnp
from jax import lax
from jax.sharding import PartitionSpec as P

adapter_scale = 2.0


def shards(
    inputs,
    cotangent,
    frozen_key_weight,
    adapter_down_weight,
    adapter_up_weight,
    row_adapter_index,
    adapter_slot_index,
):
    tok_rows = inputs.shape[0]
    feat_width = inputs.shape[1]
    owned_rows_mask = adapter_down_weight.shape[0]
    data_count = lax.axis_size("dp")
    all_adapters = owned_rows_mask * data_count
    capacity = 2 * tok_rows // all_adapters
    key_feature_width = adapter_up_weight.shape[2]
    key_shard = cotangent.shape[1]
    full_dy = lax.all_gather(cotangent, "fsdp", axis=1, tiled=True)
    base = lax.dot_general(
        full_dy,
        lax.all_gather(frozen_key_weight, "dp", axis=0, tiled=True),
        (((1,), (1,)), ((), ())),
        preferred_element_type=jnp.float32,
    )
    ids = row_adapter_index[:, 0]
    every_id = lax.broadcasted_iota(jnp.int32, (1, all_adapters), 1)
    slot = jnp.sum(jnp.where(ids[:, None] == every_id, adapter_slot_index[None, :], 0), axis=1)
    row_index = lax.broadcasted_iota(jnp.int32, (tok_rows, tok_rows), 0)
    col_index = lax.broadcasted_iota(jnp.int32, (tok_rows, tok_rows), 1)
    earlier = (ids[:, None] == ids[None, :]) & (col_index < row_index)
    within = jnp.sum(earlier.astype(jnp.int32), axis=1)
    target = slot * capacity + within
    total_slots = all_adapters * capacity
    send_in = jnp.zeros((total_slots, feat_width), jnp.bfloat16).at[target].set(inputs)
    column = lax.axis_index("fsdp") * key_shard
    send_dy = jnp.zeros((total_slots, key_feature_width), jnp.bfloat16).at[target].set(full_dy)
    recv_in, recv_dy = (
        lax.all_to_all(send_in, "dp", split_axis=0, concat_axis=0, tiled=True),
        lax.all_to_all(send_dy, "dp", split_axis=0, concat_axis=0, tiled=True),
    )
    incoming_input = recv_in.reshape(data_count, owned_rows_mask, capacity, feat_width)
    incoming_gradient = recv_dy.reshape(data_count, owned_rows_mask, capacity, key_feature_width)
    partial_projection = jnp.einsum(
        "julg,uvg->julv", incoming_input, adapter_down_weight, preferred_element_type=jnp.float32
    )
    input_backward = jnp.einsum(
        "zmif,mgf->zmig", incoming_gradient, adapter_up_weight, preferred_element_type=jnp.float32
    )
    key_projection = lax.psum(partial_projection, "fsdp")
    mine_dy = lax.dynamic_slice_in_dim(incoming_gradient, column, key_shard, 3)
    proj_low = key_projection.astype(jnp.bfloat16)
    lowrank_backward = input_backward.astype(jnp.bfloat16)
    down_grad = (
        adapter_scale
        * jnp.einsum(
            "sacr,sacd->ard", lowrank_backward, incoming_input, preferred_element_type=jnp.float32
        )
    ).astype(jnp.bfloat16)
    up_grad = (
        adapter_scale
        * jnp.einsum("sacr,sack->ark", proj_low, mine_dy, preferred_element_type=jnp.float32)
    ).astype(jnp.bfloat16)
    low_part = (
        adapter_scale
        * jnp.einsum(
            "kwoe,wev->kwov",
            lowrank_backward,
            adapter_down_weight,
            preferred_element_type=jnp.float32,
        )
    ).astype(jnp.bfloat16)
    returned = lax.all_to_all(
        low_part.reshape(total_slots, feat_width), "dp", split_axis=0, concat_axis=0, tiled=True
    )
    low_rows = returned[target]
    input_grad = (base + low_rows.astype(jnp.float32)).astype(jnp.bfloat16)
    return (input_grad, down_grad, up_grad)


def solution(mesh):
    placed = (
        P(("groups", "dp"), "fsdp"),
        P(("groups", "dp"), "fsdp"),
        P(("fsdp", "dp"), None),
        P(("groups", "dp"), None, "fsdp"),
        P(("groups", "dp"), None, None),
        P(("groups", "dp"), None),
        P("groups"),
    )
    return jax.shard_map(
        shards,
        mesh=mesh,
        in_specs=placed,
        out_specs=(
            P(("groups", "dp"), "fsdp"),
            P(("groups", "dp"), None, "fsdp"),
            P(("groups", "dp"), None, "fsdp"),
        ),
        check_vma=False,
    )
```

profile of v0, /device:TPU:0, one launch (start us, length us, event | category | flops | bytes accessed | tf_op | source)
XLA Modules:
  0.0 371.4 jit_solution(11862377096071514070)
XLA Ops:
  8.0 0.0 all-gather.3.cloned.1.call-start
  8.1 0.7 all-gather.3.cloned.1.call-update
  8.7 0.8 select_reduce_fusion
  9.5 1.0 convert_reduce_fusion
  10.6 19.4 %all-gather.3.cloned.1.call-done = bf16[512,1024]{1,0:T(8,128)(2,1)} async-done(((bf16[512,256]{1,0:T(8,128)(2,1)}), bf16[512,1024]{1,0:T(8,128)(2,1)}) %all-gather.3.cloned.1.call-update) | async-done | bytes 1048592 | tf_op jit(solution)/shard_map/all_gather | solution.py:26
  30.0 4.8 %scatter_custom_fusion = bf16[1024,1024]{1,0:T(8,128)(2,1)} fusion(s32[512]{0:T(512)S(1)} %bitcast.52, bf16[512,1024]{1,0:T(8,128)(2,1)} %all-gather.3.cloned.1.call-done, bf16[]{:T(256)} %constant.8.clone.1), kind=kCustom, calls=%fused_computation.25 | custom fusion | bytes 2097664 | tf_op jit(solution)/shard_map/scatter | solution.py:44
  34.8 4.6 %all-to-all-start = ((bf16[4,256,1024]{2,1,0:T(8,128)(2,1)}), bf16[4,256,1024]{2,1,0:T(8,128)(2,1)S(1)}, u32[]{:S(2)}, u32[]{:S(2)}) async-start(bf16[4,256,1024]{2,1,0:T(8,128)(2,1)} %bitcast.3), calls=%async_computation | async-start | bytes 4194304 | tf_op jit(solution)/shard_map/all_to_all | solution.py:47
  39.4 7.2 %scatter_custom_fusion.1 = bf16[1024,2048]{1,0:T(8,128)(2,1)} fusion(s32[512]{0:T(512)S(1)} %bitcast.53, bf16[512,2048]{1,0:T(8,128)(2,1)} %param.7, bf16[]{:T(256)} %constant.8.clone.1), kind=kCustom, calls=%fused_computation.13 | custom fusion | bytes 4194816 | tf_op jit(solution)/shard_map/scatter | solution.py:42
  46.6 41.4 %all-to-all-done = bf16[4,256,1024]{2,1,0:T(8,128)(2,1)S(1)} async-done(((bf16[4,256,1024]{2,1,0:T(8,128)(2,1)}), bf16[4,256,1024]{2,1,0:T(8,128)(2,1)S(1)}, u32[]{:S(2)}, u32[]{:S(2)}) %all-to-all-start) | async-done | bytes 2097184 | tf_op jit(solution)/shard_map/all_to_all | solution.py:47
  88.0 4.9 %all-to-all-start.2 = ((bf16[4,256,2048]{2,1,0:T(8,128)(2,1)}), bf16[4,256,2048]{2,1,0:T(8,128)(2,1)}, u32[]{:S(2)}, u32[]{:S(2)}) async-start(bf16[4,256,2048]{2,1,0:T(8,128)(2,1)} %bitcast.47), calls=%async_computation.2 | async-start | bytes 8388608 | tf_op jit(solution)/shard_map/all_to_all | solution.py:46
  92.8 1.7 fusion.19
  94.6 1.2 fusion.4
  95.8 2.3 copy.17
  98.1 87.5 %all-to-all-done.2 = bf16[4,256,2048]{2,1,0:T(8,128)(2,1)} async-done(((bf16[4,256,2048]{2,1,0:T(8,128)(2,1)}), bf16[4,256,2048]{2,1,0:T(8,128)(2,1)}, u32[]{:S(2)}, u32[]{:S(2)}) %all-to-all-start.2) | async-done | bytes 4194336 | tf_op jit(solution)/shard_map/all_to_all | solution.py:46
  185.6 4.9 %all-to-all-start.1 = ((bf16[4,256,2048]{2,1,0:T(8,128)(2,1)}), bf16[4,256,2048]{2,1,0:T(8,128)(2,1)}, u32[]{:S(2)}, u32[]{:S(2)}) async-start(bf16[4,256,2048]{2,1,0:T(8,128)(2,1)} %bitcast.46), calls=%async_computation.1 | async-start | bytes 8388608 | tf_op jit(solution)/shard_map/all_to_all | solution.py:80
  190.5 0.2 all-gather.5.cloned.1.call-start
  190.7 0.3 all-gather.5.cloned.1.call-update
  191.1 4.2 %fusion.16 = f32[4,16,16,16]{3,2,0,1:T(8,128)} fusion(bf16[4,16,16,2048]{3,2,1,0:T(8,128)(2,1)} %bitcast.14, bf16[16,16,2048]{2,1,0:T(8,128)(2,1)S(1)} %copy-done), kind=kOutput, calls=%fused_computation.15 | convolution fusion | flops 67108864 | bytes 5308416 | tf_op jit(solution)/shard_map/julg,uvg->julv/dot_general | solution.py:51
  195.3 17.8 %psum.7 = bf16[4,16,16,16]{3,2,0,1:T(8,128)(2,1)} all-reduce(f32[4,16,16,16]{3,2,0,1:T(8,128)} %fusion.16), channel_id=1, replica_groups=mesh['groups'=2,'fsdp'=4,'dp'=4] {'fsdp'}, use_global_device_ids=true, to_apply=%region_4.5 | all-reduce | flops 16384 | bytes 98304 | tf_op jit(solution)/shard_map/psum | solution.py:57
  213.1 1.9 fusion.21
  215.0 3.9 %fusion.11 = bf16[16,16,2048]{2,1,0:T(8,128)(2,1)} fusion(bf16[4,16,16,16]{3,2,0,1:T(8,128)(2,1)S(1)} %fusion.19, bf16[4,16,16,2048]{3,2,1,0:T(8,128)(2,1)} %bitcast.14), kind=kOutput, calls=%fused_computation.12 | convolution fusion | flops 68157440 | bytes 5275648 | tf_op jit(solution)/shard_map/sacr,sacd->ard/dot_general | solution.py:63
  218.9 131.7 %all-to-all-done.1 = bf16[4,256,2048]{2,1,0:T(8,128)(2,1)} async-done(((bf16[4,256,2048]{2,1,0:T(8,128)(2,1)}), bf16[4,256,2048]{2,1,0:T(8,128)(2,1)}, u32[]{:S(2)}, u32[]{:S(2)}) %all-to-all-start.1) | async-done | bytes 4194336 | tf_op jit(solution)/shard_map/all_to_all | solution.py:80
  350.6 7.1 %gather_fusion = bf16[512,2048]{1,0:T(8,128)(2,1)S(1)} fusion(bf16[1024,2048]{1,0:T(8,128)(2,1)} %bitcast.12, s32[1024]{0:T(1024)S(1)} %pad_clamp_fusion), kind=kCustom, calls=%fused_computation | custom fusion | bytes 4196352 | tf_op jit(solution)/shard_map/gather | solution.py:83
  357.8 6.2 %add_convert_fusion = bf16[512,2048]{1,0:T(8,128)(2,1)} fusion(bf16[512,2048]{1,0:T(8,128)(2,1)S(1)} %gather_fusion, bf16[512,1024]{1,0:T(8,128)(2,1)} %all-gather.3.cloned.1.call-done, bf16[2048,1024]{1,0:T(8,128)(2,1)} %all-gather.5.cloned.1.call-done), kind=kOutput, calls=%fused_computation.4 | convolution fusion | flops 2150629376 | bytes 9437184 | tf_op jit(solution)/shard_map/dot_general | solution.py:27
  (6 shorter events, 0.1 us)
Async XLA Ops:
  8.0 86.6 %copy-start = (bf16[16,16,2048]{2,1,0:T(8,128)(2,1)S(1)}, bf16[16,16,2048]{2,1,0:T(8,128)(2,1)}, u32[]{:S(2)}) copy-start(bf16[16,16,2048]{2,1,0:T(8,128)(2,1)} %param.10) | copy-start | bytes 3145732
  8.0 22.0 %all-gather.3.cloned.1.call-start = ((), (), s32[]{:S(2)}) async-start(), calls=%async_computation.3 | async-start | bytes 1310720 | tf_op jit(solution)/shard_map/all_gather | solution.py:26
  34.8 53.2 %all-to-all-start = ((bf16[4,256,1024]{2,1,0:T(8,128)(2,1)}), bf16[4,256,1024]{2,1,0:T(8,128)(2,1)S(1)}, u32[]{:S(2)}, u32[]{:S(2)}) async-start(bf16[4,256,1024]{2,1,0:T(8,128)(2,1)} %bitcast.3), calls=%async_computation | async-start | bytes 4194304 | tf_op jit(solution)/shard_map/all_to_all | solution.py:47
  88.0 97.6 %all-to-all-start.2 = ((bf16[4,256,2048]{2,1,0:T(8,128)(2,1)}), bf16[4,256,2048]{2,1,0:T(8,128)(2,1)}, u32[]{:S(2)}, u32[]{:S(2)}) async-start(bf16[4,256,2048]{2,1,0:T(8,128)(2,1)} %bitcast.47), calls=%async_computation.2 | async-start | bytes 8388608 | tf_op jit(solution)/shard_map/all_to_all | solution.py:46
  185.6 165.0 %all-to-all-start.1 = ((bf16[4,256,2048]{2,1,0:T(8,128)(2,1)}), bf16[4,256,2048]{2,1,0:T(8,128)(2,1)}, u32[]{:S(2)}, u32[]{:S(2)}) async-start(bf16[4,256,2048]{2,1,0:T(8,128)(2,1)} %bitcast.46), calls=%async_computation.1 | async-start | bytes 8388608 | tf_op jit(solution)/shard_map/all_to_all | solution.py:80
  190.5 167.3 %all-gather.5.cloned.1.call-start = ((), (), s32[]{:S(2)}) async-start(), calls=%async_computation.4 | async-start | bytes 5242880 | tf_op jit(solution)/shard_map/all_gather | solution.py:29
Sparse Core Ops, SparseCore 0:
  10.4 19.5 all-gather.2
Sparse Core Ops, SparseCore 1:
  192.5 148.0 all-gather.4
where the time goes:
time: 372 us; the launch traced here: 371 us
  waiting for transfers between devices  281 us (76%)
  local copies, waits for them, and re-layouts  21.5 us (6%)
  matrix products  19.1 us (5%)
  blocking collectives  17.8 us (5%)
  between operations  15.6 us (4%)
  starting transfers between devices  14.6 us (4%)
    all_to_all x1, waiting for transfers between devices, shards(): lax.all_to_all(low_part.reshape(total_slots, feat_width), 'dp', split_axi...  132 us
    all_to_all x1, waiting for transfers between devices, shards(): lax.all_to_all(send_in, 'dp', split_axis=0, concat_axis=0, tiled=True)  87.5 us
    all_to_all x1, waiting for transfers between devices, shards(): lax.all_to_all(send_dy, 'dp', split_axis=0, concat_axis=0, tiled=True)  41.4 us
    all_gather x1, waiting for transfers between devices, shards(): full_dy = lax.all_gather(cotangent, 'fsdp', axis=1, tiled=True)  19.4 us
    psum x1, blocking collectives, shards(): key_projection = lax.psum(partial_projection, 'fsdp')  17.8 us
  transfers between devices with their start and end apart: 5, of which 4 were waited for; matrix products, arithmetic and copies ran while one was open for 8% of the time, Pallas kernels for 0%

commit v1 on v0

v1 whole, which is shorter than its diff:
```python
import jax
import jax.numpy as jnp
from jax import lax
from jax.sharding import PartitionSpec as P

adapter_scale = 2.0


def dot(a, b, ca, cb):
    return lax.dot_general(a, b, (((ca,), (cb,)), ((), ())), preferred_element_type=jnp.float32)


def shards(
    inputs,
    cotangent,
    frozen_key_weight,
    adapter_down_weight,
    adapter_up_weight,
    row_adapter_index,
    adapter_slot_index,
):
    tok_rows, feat_width = inputs.shape
    key_shard = cotangent.shape[1]
    owned, rank, _ = adapter_down_weight.shape
    slots = adapter_slot_index.shape[0]
    key_at = lax.axis_index("fsdp") * key_shard

    ids = row_adapter_index[:, 0]
    every = lax.broadcasted_iota(jnp.int32, (slots, tok_rows), 0)
    slot = jnp.sum(jnp.where(ids[None, :] == every, adapter_slot_index[:, None], 0), axis=0)
    mask = (slot[None, :] == every)[:, None, :]

    def own_rows(values):
        values = values.reshape(slots, rank, tok_rows)
        part = jnp.sum(jnp.where(mask, values, 0.0), axis=0)
        return lax.psum(part, "fsdp").astype(jnp.bfloat16)

    def spread(values):
        values = (adapter_scale * values)[None]
        return jnp.where(mask, values, jnp.bfloat16(0)).reshape(slots * rank, tok_rows)

    up_own = lax.dynamic_slice_in_dim(adapter_up_weight, key_at, key_shard, 2)
    up_all = lax.all_gather(up_own.reshape(owned * rank, key_shard), "dp", axis=0, tiled=True)
    down_all = lax.all_gather(
        adapter_down_weight.reshape(owned * rank, feat_width), "dp", axis=0, tiled=True
    )
    back = spread(own_rows(dot(up_all, cotangent, 1, 1)))
    down_part = dot(back, inputs, 1, 0).astype(jnp.bfloat16)
    down_grad = lax.psum_scatter(down_part, "dp", scatter_dimension=0, tiled=True)
    proj = spread(own_rows(dot(down_all, inputs, 1, 1)))
    up_part = dot(proj, cotangent, 1, 0).astype(jnp.bfloat16)
    up_grad = lax.psum_scatter(up_part, "dp", scatter_dimension=0, tiled=True)
    full_dy = lax.all_gather(cotangent, "fsdp", axis=1, tiled=True)
    weight = lax.all_gather(frozen_key_weight, "dp", axis=0, tiled=True)
    base = dot(full_dy, weight, 1, 1)
    low = dot(back, down_all, 0, 0).astype(jnp.bfloat16)
    input_grad = (base + low.astype(jnp.float32)).astype(jnp.bfloat16)
    return (
        input_grad,
        down_grad.reshape(owned, rank, feat_width),
        up_grad.reshape(owned, rank, key_shard),
    )


def solution(mesh):
    placed = (
        P(("groups", "dp"), "fsdp"),
        P(("groups", "dp"), "fsdp"),
        P(("fsdp", "dp"), None),
        P(("groups", "dp"), None, "fsdp"),
        P(("groups", "dp"), None, None),
        P(("groups", "dp"), None),
        P("groups"),
    )
    return jax.shard_map(
        shards,
        mesh=mesh,
        in_specs=placed,
        out_specs=(
            P(("groups", "dp"), "fsdp"),
            P(("groups", "dp"), None, "fsdp"),
            P(("groups", "dp"), None, "fsdp"),
        ),
        check_vma=False,
    )
```

time: 372 us -> 303 us (0.81)
  waiting for transfers between devices: 281 us -> 228 us
  local copies, waits for them, and re-layouts: 21.5 us -> 0.94 us
  blocking collectives: 17.8 us -> 34.1 us
  starting transfers between devices: 14.6 us -> 0.19 us
  matrix products: 19.1 us -> 24.8 us
    all_to_all x3 -> x0, waiting for transfers between devices: 261 us -> none  [the longest x1 132 us: shards(): lax.all_to_all(low_part.reshape(total_slots, feat_width), 'dp', split_axi...]
    all_gather x1 -> x2, waiting for transfers between devices: 0.03 us -> 132 us  [the longest x1 70.5 us: shards(): weight = lax.all_gather(frozen_key_weight, 'dp', axis=0, tiled=True)]
    reduce_scatter x0 -> x2, waiting for transfers between devices: none -> 93.9 us  [the longest x1 77.8 us: shards(): lax.psum_scatter(down_part, 'dp', scatter_dimension=0, tiled=True)]
    all_gather x0 -> x1, blocking collectives: none -> 21.1 us  [shards(): lax.all_gather(up_own.reshape(owned * rank, key_shard), 'dp', axis=0, til...]
    all_gather x1, waiting for transfers between devices: 19.4 us -> 0.01 us  [shards(): full_dy = lax.all_gather(cotangent, 'fsdp', axis=1, tiled=True)]
    all_to_all x3 -> x0, starting transfers between devices: 14.4 us -> none  [the longest x1 4.9 us: shards(): lax.all_to_all(low_part.reshape(total_slots, feat_width), 'dp', split_axi...]
    scatter x2 -> x0, local copies, waits for them, and re-layouts: 12 us -> none  [the longest x1 7.25 us: shards(): jnp.zeros((total_slots, feat_width), jnp.bfloat16).at[target].set(inputs)]
    gather x1 -> x0, local copies, waits for them, and re-layouts: 7.13 us -> none  [shards(): low_rows = returned[target]]
  transfers between devices with their start and end apart: 5 -> 5, of which waited for: 4 -> 4; matrix products, arithmetic and copies ran while one was open for 8% -> 9% of each run, Pallas kernels for 0% -> 0%
where the time goes in v1:
time: 303 us
  waiting for transfers between devices  228 us (75%)
  blocking collectives  34.1 us (11%)
  matrix products  24.8 us (8%)
  between operations  13.9 us (5%)
    reduce_scatter x1, waiting for transfers between devices, shards(): lax.psum_scatter(down_part, 'dp', scatter_dimension=0, tiled=True)  77.8 us
    all_gather x1, waiting for transfers between devices, shards(): weight = lax.all_gather(frozen_key_weight, 'dp', axis=0, tiled=True)  70.5 us
    all_gather x1, waiting for transfers between devices, shards(): lax.all_gather(adapter_down_weight.reshape(owned * rank, feat_width), 'dp...  61.9 us
    dot_general x6, matrix products, dot(): lax.dot_general(a, b, (((ca,), (cb,)), ((), ())), preferred_element_type=...  24.8 us
    all_gather x1, blocking collectives, shards(): lax.all_gather(up_own.reshape(owned * rank, key_shard), 'dp', axis=0, til...  21.1 us
    reduce_scatter x1, waiting for transfers between devices, shards(): up_grad = lax.psum_scatter(up_part, 'dp', scatter_dimension=0, tiled=True)  16.1 us
    psum x1, blocking collectives, own_rows(): return lax.psum(part, 'fsdp').astype(jnp.bfloat16)  13 us
  transfers between devices with their start and end apart: 5, of which 4 were waited for; matrix products, arithmetic and copies ran while one was open for 9% of the time, Pallas kernels for 0%

profile of v1, /device:TPU:0, one launch (start us, length us, event | category | flops | bytes accessed | tf_op | source)
XLA Modules:
  0.0 303.3 jit_solution(9537671145525473254)
XLA Ops:
  7.2 0.0 all-gather.8.cloned.1.call-start
  7.3 0.7 all-gather.8.cloned.1.call-update
  7.9 0.0 all-gather.4.cloned.1.call-start
  8.0 0.7 all-gather.4.cloned.1.call-update
  8.7 0.0 all-gather.6.cloned.1.call-start
  8.7 0.7 all-gather.6.cloned.1.call-update
  9.4 0.0 reduce-scatter.5.cloned.1.call-start
  9.5 0.9 constant_dynamic-slice_fusion
  10.4 0.1 select_reduce_fusion.2
  10.5 21.1 %all_gather.14 = bf16[1024,256]{1,0:T(8,128)(2,1)S(1)} all-gather(bf16[256,256]{1,0:T(8,128)(2,1)S(1)} %bitcast.27), channel_id=1, replica_groups=mesh['groups'=2,'fsdp'=4,'dp'=4] {'dp'}, dimensions={0}, use_global_device_ids=true | all-gather | bytes 655360 | tf_op jit(solution)/shard_map/all_gather | solution.py:43
  31.7 1.8 fusion
  33.5 61.9 %all-gather.8.cloned.1.call-done = bf16[1024,2048]{1,0:T(8,128)(2,1)} async-done(((bf16[256,2048]{1,0:T(8,128)(2,1)}), bf16[1024,2048]{1,0:T(8,128)(2,1)}) %all-gather.8.cloned.1.call-update) | async-done | bytes 4194320 | tf_op jit(solution)/shard_map/all_gather | solution.py:44
  95.4 4.7 %fusion.1 = f32[1024,512]{1,0:T(8,128)S(1)} fusion(bf16[1024,2048]{1,0:T(8,128)(2,1)} %all-gather.8.cloned.1.call-done, bf16[512,2048]{1,0:T(8,128)(2,1)S(1)} %copy-done), kind=kOutput, calls=%fused_computation.15 | convolution fusion | flops 2147483648 | bytes 8388608 | tf_op jit(solution)/shard_map/dot_general | solution.py:10
  100.1 0.7 select_reduce_fusion
  100.8 13.0 %all-reduce = (bf16[16,512]{1,0:T(8,128)(2,1)S(1)}, bf16[16,512]{1,0:T(8,128)(2,1)S(1)}) all-reduce(f32[16,512]{1,0:T(8,128)S(1)} %get-tuple-element.4, f32[16,512]{1,0:T(8,128)S(1)} %get-tuple-element.3), channel_id=1, replica_groups=mesh['groups'=2,'fsdp'=4,'dp'=4] {'fsdp'}, use_global_device_ids=true, to_apply=%region_2.3 | all-reduce | flops 16384 | bytes 98304 | tf_op jit(solution)/shard_map/psum | solution.py:36
  113.8 0.2 broadcast_select_fusion
  113.9 1.2 convolution_convert_fusion.2
  115.2 0.0 reduce-scatter.3.cloned.1.call-start
  115.2 4.3 %convolution_convert_fusion = bf16[1024,2048]{1,0:T(8,128)(2,1)} fusion(bf16[1024,512]{1,0:T(8,128)(2,1)S(1)} %bitcast.25, bf16[512,2048]{1,0:T(8,128)(2,1)S(1)} %copy-done), kind=kOutput, calls=%fused_computation.1 | convolution fusion | flops 2149580800 | bytes 7340032 | tf_op jit(solution)/shard_map/dot_general | solution.py:10
  119.6 5.9 %convolution_convert_fusion.1 = bf16[512,2048]{1,0:T(8,128)(2,1)} fusion(bf16[1024,512]{1,0:T(8,128)(2,1)S(1)} %bitcast.26, bf16[1024,2048]{1,0:T(8,128)(2,1)} %all-gather.8.cloned.1.call-done), kind=kOutput, calls=%fused_computation.2 | convolution fusion | flops 2148532224 | bytes 7340032 | tf_op jit(solution)/shard_map/dot_general | solution.py:10
  125.5 70.5 %all-gather.6.cloned.1.call-done = bf16[2048,1024]{1,0:T(8,128)(2,1)} async-done(((bf16[512,1024]{1,0:T(8,128)(2,1)}), bf16[2048,1024]{1,0:T(8,128)(2,1)}) %all-gather.6.cloned.1.call-update) | async-done | bytes 4194320 | tf_op jit(solution)/shard_map/all_gather | solution.py:54
  196.0 6.9 %add_convert_fusion = bf16[512,2048]{1,0:T(8,128)(2,1)} fusion(bf16[512,2048]{1,0:T(8,128)(2,1)} %convolution_convert_fusion.1, bf16[512,1024]{1,0:T(8,128)(2,1)} %all-gather.4.cloned.1.call-done, bf16[2048,1024]{1,0:T(8,128)(2,1)} %all-gather.6.cloned.1.call-done), kind=kOutput, calls=%fused_computation | convolution fusion | flops 2150629376 | bytes 9437184 | tf_op jit(solution)/shard_map/dot_general | solution.py:10
  202.9 16.1 %reduce-scatter.5.cloned.1.call-done = bf16[256,256]{1,0:T(8,128)(2,1)} async-done(((bf16[1024,256]{1,0:T(8,128)(2,1)}), bf16[256,256]{1,0:T(8,128)(2,1)}) %reduce-scatter.5.cloned.1.call-update) | async-done | bytes 131088 | tf_op jit(solution)/shard_map/reduce_scatter | solution.py:52
  219.0 77.8 %reduce-scatter.3.cloned.1.call-done = bf16[256,2048]{1,0:T(8,128)(2,1)} async-done(((bf16[1024,2048]{1,0:T(8,128)(2,1)}), bf16[256,2048]{1,0:T(8,128)(2,1)}) %reduce-scatter.3.cloned.1.call-update) | async-done | bytes 1048592 | tf_op jit(solution)/shard_map/reduce_scatter | solution.py:49
  (15 shorter events, 0.1 us)
Async XLA Ops:
  7.2 88.2 %copy-start = (bf16[512,2048]{1,0:T(8,128)(2,1)S(1)}, bf16[512,2048]{1,0:T(8,128)(2,1)}, u32[]{:S(2)}) copy-start(bf16[512,2048]{1,0:T(8,128)(2,1)} %param.7) | copy-start | bytes 6291460
  7.2 24.5 %copy-start.2 = (bf16[512,256]{1,0:T(8,128)(2,1)S(1)}, bf16[512,256]{1,0:T(8,128)(2,1)}, u32[]{:S(2)}) copy-start(bf16[512,256]{1,0:T(8,128)(2,1)} %param.8) | copy-start | bytes 786436
  7.2 3.2 %copy-start.3 = (s32[512,1]{0,1:T(1,128)S(1)}, s32[512,1]{0,1:T(1,128)}, u32[]{:S(2)}) copy-start(s32[512,1]{0,1:T(1,128)} %param.12) | copy-start | bytes 6148
  7.2 3.2 %copy-start.4 = (s32[64]{0:T(128)S(1)}, s32[64]{0:T(128)}, u32[]{:S(2)}) copy-start(s32[64]{0:T(128)} %param.13) | copy-start | bytes 772
  7.2 88.2 %all-gather.8.cloned.1.call-start = ((), (), s32[]{:S(2)}) async-start(), calls=%async_computation.4 | async-start | bytes 5242880 | tf_op jit(solution)/shard_map/all_gather | solution.py:44
  7.9 117.6 %all-gather.4.cloned.1.call-start = ((), (), s32[]{:S(2)}) async-start(), calls=%async_computation.2 | async-start | bytes 1310720 | tf_op jit(solution)/shard_map/all_gather | solution.py:53
  8.7 187.3 %all-gather.6.cloned.1.call-start = ((), (), s32[]{:S(2)}) async-start(), calls=%async_computation.3 | async-start | bytes 5242880 | tf_op jit(solution)/shard_map/all_gather | solution.py:54
  9.4 209.5 %reduce-scatter.5.cloned.1.call-start = ((), (), s32[]{:S(2)}) async-start(), calls=%async_computation.6 | async-start | bytes 655360 | tf_op jit(solution)/shard_map/reduce_scatter | solution.py:52
  95.4 4.7 %copy-start.1 = (f32[1024,512]{1,0:T(8,128)S(1)}, f32[1024,512]{1,0:T(8,128)}, u32[]{:S(2)}) copy-start(f32[1024,512]{1,0:T(8,128)} %fusion) | copy-start | bytes 6291460
  115.2 181.6 %reduce-scatter.3.cloned.1.call-start = ((), (), s32[]{:S(2)}) async-start(), calls=%async_computation.5 | async-start | bytes 5242880 | tf_op jit(solution)/shard_map/reduce_scatter | solution.py:49
Sparse Core Ops, SparseCore 0:
  9.6 85.7 all-gather.7
  96.9 16.4 all-gather.3
  115.1 80.9 all-gather.5
  198.7 20.1 reduce-scatter.4
  221.7 75.0 reduce-scatter.2

commit v2 on v1

v2 whole, which is shorter than its diff:
```python
import jax
import jax.numpy as jnp
from jax import lax
from jax.sharding import PartitionSpec as P

adapter_scale = 2.0


def dot(a, b, ca, cb):
    return lax.dot_general(a, b, (((ca,), (cb,)), ((), ())), preferred_element_type=jnp.float32)


def narrow(values):
    return values.astype(jnp.bfloat16)


def turns(value, axis):
    count = lax.axis_size(axis)
    return [
        lax.ppermute(value, axis, [(i, (i + step) % count) for i in range(count)])
        for step in range(1, count)
    ]


def add_over(value, axis):
    for other in turns(value, axis):
        value = value + other
    return value


def line_steps(value, axis):
    count = lax.axis_size(axis)
    below = above = value
    for step in range(1, count):
        below = lax.ppermute(below, axis, [(i, i + 1) for i in range(step - 1, count - 1)])
        above = lax.ppermute(above, axis, [(i + 1, i) for i in range(count - step)])
        yield step, below, above


def line_pieces(value, axis):
    count, place = lax.axis_size(axis), lax.axis_index(axis)
    for step, below, above in line_steps(value, axis):
        if 2 * step < count:
            yield place - step, below
            yield place + step, above
        else:
            yield jnp.where(place < count - step, place + step, place - step), below + above


def line_sums(part, axis):
    count, place = lax.axis_size(axis), lax.axis_index(axis)
    below = above = 0.0
    for step in range(1, count):
        far = count - step
        up = [(i, i + 1) for i in range(step)]
        down = [(i, i - 1) for i in range(far, count)]
        if 2 * step <= count:
            sent = narrow(part(jnp.where(place < step, place + far, place - far)) + below + above)
            if 2 * step < count - 1:
                below, above = lax.ppermute(sent, axis, up + down), 0.0
            else:
                below, above = lax.ppermute(sent, axis, up), lax.ppermute(sent, axis, down)
        else:
            to_up = narrow(part(place + far) + below)
            to_down = narrow(part(place - far) + above)
            below, above = lax.ppermute(to_up, axis, up), lax.ppermute(to_down, axis, down)
    return narrow(part(place) + below + above)


def shards(
    inputs,
    cotangent,
    frozen_key_weight,
    adapter_down_weight,
    adapter_up_weight,
    row_adapter_index,
    adapter_slot_index,
):
    tok_rows, feat_width = inputs.shape
    key_shard = cotangent.shape[1]
    owned, rank, _ = adapter_down_weight.shape
    slots = adapter_slot_index.shape[0]
    data_count, place = lax.axis_size("dp"), lax.axis_index("dp")
    weight_rows, key_width = frozen_key_weight.shape
    groups, group = lax.axis_size("groups"), lax.axis_index("groups")
    key_at = lax.axis_index("fsdp") * key_shard

    ids = row_adapter_index[:, 0]
    every = lax.broadcasted_iota(jnp.int32, (slots, tok_rows), 0)
    slot = jnp.sum(jnp.where(ids[None, :] == every, adapter_slot_index[:, None], 0), axis=0)
    owned_at = lax.broadcasted_iota(jnp.int32, (owned, tok_rows), 0)

    def named(block):
        return (slot[None, :] - block * owned == owned_at)[:, None, :]

    def pick(block, values):
        values = values.reshape(owned, rank, tok_rows)
        return jnp.sum(jnp.where(named(block), values, 0.0), axis=0)

    def spread(block, values):
        return jnp.where(named(block), values[None], jnp.bfloat16(0)).reshape(owned * rank, tok_rows)

    up_own = lax.dynamic_slice_in_dim(adapter_up_weight, key_at, key_shard, 2)
    up_own = up_own.reshape(owned * rank, key_shard)
    up_parts = [up_own] + turns(up_own, "dp")
    down_own = adapter_down_weight.reshape(owned * rank, feat_width)
    full_dy = lax.all_gather(cotangent, "fsdp", axis=1, tiled=True)

    back = sum(
        pick((place - turn) % data_count, dot(part, cotangent, 1, 1))
        for turn, part in enumerate(up_parts)
    )
    back = adapter_scale * narrow(add_over(back, "fsdp"))

    margin = (data_count - 1) // 2
    gathered = data_count + 2 * margin

    def put(whole, block, piece, within=0):
        return lax.dynamic_update_slice(
            whole, piece[None, None], (block + margin, within, 0, 0)
        )

    down_all = jnp.zeros((gathered, 1, owned * rank, feat_width), jnp.bfloat16)
    down_all = put(down_all, place, down_own)
    proj = pick(place, dot(down_own, inputs, 1, 1))
    for block, piece in line_pieces(down_own, "dp"):
        proj = proj + pick(block, dot(piece, inputs, 1, 1))
        down_all = put(down_all, block, piece)

    half_rows = weight_rows // groups
    halves = frozen_key_weight.reshape(groups, half_rows, key_width)
    weight = jnp.zeros((gathered, groups, half_rows, key_width), jnp.bfloat16)
    weight = lax.dynamic_update_slice(weight, halves[None], (place + margin, 0, 0, 0))
    mine = lax.dynamic_index_in_dim(halves, group, 0, False)
    for block, piece in line_pieces(mine, "dp"):
        weight = put(weight, block, piece, group)
        for turn, other in enumerate(turns(piece, "groups")):
            weight = put(weight, block, other, (group - turn - 1) % groups)

    down_grad = line_sums(lambda block: dot(spread(block, back), inputs, 1, 0), "dp")

    proj = adapter_scale * narrow(add_over(proj, "fsdp"))

    def up_part(block):
        return dot(spread(block, proj), cotangent, 1, 0)

    up_grad = up_part(place)
    for turn in range(1, data_count):
        pairs = [(i, (i + turn) % data_count) for i in range(data_count)]
        up_grad = up_grad + lax.ppermute(narrow(up_part((place + turn) % data_count)), "dp", pairs)

    def whole(array):
        return array[margin : margin + data_count].reshape(-1, array.shape[-1])

    every_back = jnp.concatenate([spread(block, back) for block in range(data_count)], axis=0)
    low = narrow(dot(every_back, whole(down_all), 0, 0))
    base = dot(full_dy, whole(weight), 1, 1)
    input_grad = narrow(base + low.astype(jnp.float32))
    return (
        input_grad,
        down_grad.reshape(owned, rank, feat_width),
        narrow(up_grad).reshape(owned, rank, key_shard),
    )


def solution(mesh):
    placed = (
        P(("groups", "dp"), "fsdp"),
        P(("groups", "dp"), "fsdp"),
        P(("fsdp", "dp"), None),
        P(("groups", "dp"), None, "fsdp"),
        P(("groups", "dp"), None, None),
        P(("groups", "dp"), None),
        P("groups"),
    )
    return jax.shard_map(
        shards,
        mesh=mesh,
        in_specs=placed,
        out_specs=(
            P(("groups", "dp"), "fsdp"),
            P(("groups", "dp"), None, "fsdp"),
            P(("groups", "dp"), None, "fsdp"),
        ),
        check_vma=False,
    )
```

time: 303 us -> 216 us (0.71)
  waiting for transfers between devices: 228 us -> 63.9 us
  starting transfers between devices: 0.19 us -> 64.7 us
  blocking collectives: 34.1 us -> 0 us
  local copies, waits for them, and re-layouts: 0.94 us -> 25.5 us
  other arithmetic: 0.98 us -> 13.8 us
  matrix products: 24.8 us -> 31.9 us
    all_gather x2 -> x0, waiting for transfers between devices: 132 us -> none  [the longest x1 70.5 us: shards(): weight = lax.all_gather(frozen_key_weight, 'dp', axis=0, tiled=True)]
    reduce_scatter x2 -> x0, waiting for transfers between devices: 93.9 us -> none  [the longest x1 77.8 us: shards(): lax.psum_scatter(down_part, 'dp', scatter_dimension=0, tiled=True)]
    ppermute x0 -> x33, starting transfers between devices: none -> 64.7 us  [the longest x1 21.3 us: line_sums(): lax.ppermute(to_up, axis, up)]
    ppermute x0 -> x33, waiting for transfers between devices: none -> 63.9 us  [the longest x13 35 us: turns(): lax.ppermute(value, axis, [(i, (i + step) % count) for i in range(count)])]
    all_gather x1 -> x0, blocking collectives: 21.1 us -> none  [shards(): lax.all_gather(up_own.reshape(owned * rank, key_shard), 'dp', axis=0, til...]
    psum x1 -> x0, blocking collectives: 13 us -> none  [own_rows(): return lax.psum(part, 'fsdp').astype(jnp.bfloat16)]
    dynamic_update_slice x0 -> x10, local copies, waits for them, and re-layouts: none -> 8.94 us  [the longest x9 7.8 us: put(): lax.dynamic_update_slice(whole, piece[None, None], (block + margin, withi...]
    dot_general x6 -> x20, matrix products: 24.8 us -> 31.9 us  [dot(): lax.dot_general(a, b, (((ca,), (cb,)), ((), ())), preferred_element_type=...]
  transfers between devices with their start and end apart: 5 -> 34, of which waited for: 4 -> 11; matrix products, arithmetic and copies ran while one was open for 9% -> 32% of each run, Pallas kernels for 0% -> 0%
where the time goes in v2:
time: 216 us; the launch traced here: 215 us
  starting transfers between devices  64.7 us (30%)
  waiting for transfers between devices  63.9 us (30%)
  matrix products  31.9 us (15%)
  local copies, waits for them, and re-layouts  25.5 us (12%)
  between operations  14.9 us (7%)
  other arithmetic  13.8 us (6%)
    ppermute x13, waiting for transfers between devices, turns(): lax.ppermute(value, axis, [(i, (i + step) % count) for i in range(count)])  35 us
    dot_general x20, matrix products, dot(): lax.dot_general(a, b, (((ca,), (cb,)), ((), ())), preferred_element_type=...  31.9 us
    ppermute x1, starting transfers between devices, line_sums(): lax.ppermute(to_up, axis, up)  21.3 us
    ppermute x13, starting transfers between devices, turns(): lax.ppermute(value, axis, [(i, (i + step) % count) for i in range(count)])  12.9 us
    ppermute x6, waiting for transfers between devices, line_steps(): above = lax.ppermute(above, axis, [(i + 1, i) for i in range(count - step)])  12.2 us
    ppermute x6, starting transfers between devices, line_steps(): lax.ppermute(below, axis, [(i, i + 1) for i in range(step - 1, count - 1)])  11.3 us
    ppermute x3, waiting for transfers between devices, shards(): lax.ppermute(narrow(up_part((place + turn) % data_count)), 'dp', pairs)  8.91 us
    ppermute x6, starting transfers between devices, line_steps(): above = lax.ppermute(above, axis, [(i + 1, i) for i in range(count - step)])  7.89 us
  transfers between devices with their start and end apart: 34, of which 11 were waited for; matrix products, arithmetic and copies ran while one was open for 32% of the time, Pallas kernels for 0%

profile of v2, /device:TPU:0, one launch (start us, length us, event | category | flops | bytes accessed | tf_op | source)
XLA Modules:
  0.0 214.8 jit_solution(432657305024138625)
XLA Ops:
  7.2 6.1 %collective-permute-start.16 = (bf16[256,2048]{1,0:T(8,128)(2,1)}, bf16[256,2048]{1,0:T(8,128)(2,1)}, u32[]{:S(2)}, u32[]{:S(2)}) collective-permute-start(bf16[256,2048]{1,0:T(8,128)(2,1)} %bitcast.121), channel_id=1, source_target_pairs={{0,1},{1,2},{2,3},{4,5},{5,6},{6,7},{8,9},{9,10},{10,11},{12,13},{... | collective-permute-start | bytes 3145736 | tf_op jit(solution)/shard_map/ppermute | solution.py:35
  16.1 4.7 %collective-permute-start.12 = (bf16[256,256]{1,0:T(8,128)(2,1)}, bf16[256,256]{1,0:T(8,128)(2,1)}, u32[]{:S(2)}, u32[]{:S(2)}) collective-permute-start(bf16[256,256]{1,0:T(8,128)(2,1)} %bitcast.15), channel_id=1, source_target_pairs={{0,3},{1,0},{2,1},{3,2},{4,7},{5,4},{6,5},{7,6},{8,11},{9,8},{10,9... | collective-permute-start | bytes 393224 | tf_op jit(solution)/shard_map/ppermute | solution.py:20
  29.1 2.6 %fusion.7 = f32[16,512]{1,0:T(8,128)} fusion(bf16[16,16,2048]{2,1,0:T(8,128)(2,1)} %param.10, bf16[512,2048]{1,0:T(8,128)(2,1)S(1)} %copy-done, pred[16,512]{1,0:T(8,128)(4,1)S(1)} %get-tuple-element.47), kind=kOutput, calls=%fused_computation.13 | convolution fusion | flops 537124864 | bytes 3186688 | tf_op jit(solution)/shard_map/dot_general | solution.py:10
  33.7 3.5 %broadcast_in_dim.290 = bf16[6,2,256,1024]{3,2,1,0:T(8,128)(2,1)} broadcast(bf16[]{:T(256)} %constant.91.clone.1), dimensions={} | broadcast | bytes 6291458 | tf_op jit(solution)/shard_map/broadcast_in_dim | solution.py:132
  39.4 4.3 %collective-permute-done.12 = bf16[256,256]{1,0:T(8,128)(2,1)} collective-permute-done((bf16[256,256]{1,0:T(8,128)(2,1)}, bf16[256,256]{1,0:T(8,128)(2,1)}, u32[]{:S(2)}, u32[]{:S(2)}) %collective-permute-start.12) | collective-permute-done | bytes 131104 | tf_op jit(solution)/shard_map/ppermute | solution.py:20
  45.0 6.3 %collective-permute-done.11 = bf16[256,256]{1,0:T(8,128)(2,1)} collective-permute-done((bf16[256,256]{1,0:T(8,128)(2,1)}, bf16[256,256]{1,0:T(8,128)(2,1)}, u32[]{:S(2)}, u32[]{:S(2)}) %collective-permute-start.11) | collective-permute-done | bytes 131104 | tf_op jit(solution)/shard_map/ppermute | solution.py:20
  54.9 2.5 %collective-permute-start = (bf16[256,1024]{1,0:T(8,128)(2,1)S(1)}, bf16[256,1024]{1,0:T(8,128)(2,1)S(1)}, u32[]{:S(2)}, u32[]{:S(2)}) collective-permute-start(bf16[256,1024]{1,0:T(8,128)(2,1)S(1)} %dynamic-slice_bitcast_fusion), channel_id=1, source_target_pairs={{0,1},{1,2},{2,3},{4,5},{5,6},{6,7},{8,9},{9,10},{10,11},{12,13},{... | collective-permute-start | bytes 1572872 | tf_op jit(solution)/shard_map/ppermute | solution.py:35
  61.2 7.8 %collective-permute-done = bf16[256,1024]{1,0:T(8,128)(2,1)S(1)} collective-permute-done((bf16[256,1024]{1,0:T(8,128)(2,1)S(1)}, bf16[256,1024]{1,0:T(8,128)(2,1)S(1)}, u32[]{:S(2)}, u32[]{:S(2)}) %collective-permute-start) | collective-permute-done | bytes 524320 | tf_op jit(solution)/shard_map/ppermute | solution.py:35
  76.1 7.7 %collective-permute-done.1 = bf16[256,1024]{1,0:T(8,128)(2,1)S(1)} collective-permute-done((bf16[256,1024]{1,0:T(8,128)(2,1)S(1)}, bf16[256,1024]{1,0:T(8,128)(2,1)S(1)}, u32[]{:S(2)}, u32[]{:S(2)}) %collective-permute-start.1) | collective-permute-done | bytes 524320 | tf_op jit(solution)/shard_map/ppermute | solution.py:20
  86.8 8.0 %collective-permute-done.3 = bf16[256,1024]{1,0:T(8,128)(2,1)S(1)} collective-permute-done((bf16[256,1024]{1,0:T(8,128)(2,1)S(1)}, bf16[256,1024]{1,0:T(8,128)(2,1)S(1)}, u32[]{:S(2)}, u32[]{:S(2)}) %collective-permute-start.3) | collective-permute-done | bytes 524320 | tf_op jit(solution)/shard_map/ppermute | solution.py:20
  94.8 4.4 %collective-permute-start.22 = (bf16[256,2048]{1,0:T(8,128)(2,1)S(1)}, bf16[256,2048]{1,0:T(8,128)(2,1)S(1)}, u32[]{:S(2)}, u32[]{:S(2)}) collective-permute-start(bf16[256,2048]{1,0:T(8,128)(2,1)S(1)} %convolution_convert_fusion.1), channel_id=1, source_target_pairs={{0,1},{3,2},{4,5},{7,6},{8,9},{11,10},{12,13},{15,14},{16,17},{19,... | collective-permute-start | bytes 3145736 | tf_op jit(solution)/shard_map/ppermute | solution.py:60
  112.0 2.5 %collective-permute-done.6 = bf16[256,1024]{1,0:T(8,128)(2,1)S(1)} collective-permute-done((bf16[256,1024]{1,0:T(8,128)(2,1)S(1)}, bf16[256,1024]{1,0:T(8,128)(2,1)S(1)}, u32[]{:S(2)}, u32[]{:S(2)}) %collective-permute-start.6) | collective-permute-done | bytes 524320 | tf_op jit(solution)/shard_map/ppermute | solution.py:20
  116.7 7.2 %collective-permute-done.8 = bf16[256,1024]{1,0:T(8,128)(2,1)S(1)} collective-permute-done((bf16[256,1024]{1,0:T(8,128)(2,1)S(1)}, bf16[256,1024]{1,0:T(8,128)(2,1)S(1)}, u32[]{:S(2)}, u32[]{:S(2)}) %collective-permute-start.8) | collective-permute-done | bytes 524320 | tf_op jit(solution)/shard_map/ppermute | solution.py:36
  127.1 2.1 collective-permute-start.23
  129.2 6.1 %collective-permute-done.9 = bf16[256,1024]{1,0:T(8,128)(2,1)S(1)} collective-permute-done((bf16[256,1024]{1,0:T(8,128)(2,1)S(1)}, bf16[256,1024]{1,0:T(8,128)(2,1)S(1)}, u32[]{:S(2)}, u32[]{:S(2)}) %collective-permute-start.9) | collective-permute-done | bytes 524320 | tf_op jit(solution)/shard_map/ppermute | solution.py:20
  136.1 4.6 %slice.8 = bf16[4,2,256,1024]{3,2,1,0:T(8,128)(2,1)} slice(bf16[6,2,256,1024]{3,2,1,0:T(8,128)(2,1)} %bitcast_dynamic-update-slice_fusion.4), slice={[1:5], [0:2], [0:256], [0:1024]} | slice | bytes 8388608 | tf_op jit(solution)/shard_map/slice | solution.py:153
  141.5 3.2 %collective-permute-done.19 = bf16[256,2048]{1,0:T(8,128)(2,1)S(1)} collective-permute-done((bf16[256,2048]{1,0:T(8,128)(2,1)}, bf16[256,2048]{1,0:T(8,128)(2,1)S(1)}, u32[]{:S(2)}, u32[]{:S(2)}) %collective-permute-start.19) | collective-permute-done | bytes 1048608 | tf_op jit(solution)/shard_map/ppermute | solution.py:36
  152.2 21.3 %collective-permute-start.24 = (bf16[256,2048]{1,0:T(8,128)(2,1)}, bf16[256,2048]{1,0:T(8,128)(2,1)}, u32[]{:S(2)}, u32[]{:S(2)}) collective-permute-start(bf16[256,2048]{1,0:T(8,128)(2,1)} %add_convert_fusion.2), channel_id=1, source_target_pairs={{0,1},{1,2},{2,3},{4,5},{5,6},{6,7},{8,9},{9,10},{10,11},{12,13},{... | collective-permute-start | bytes 3145736 | tf_op jit(solution)/shard_map/ppermute | solution.py:66
  176.1 3.8 %convolution_convert_fusion = bf16[512,2048]{0,1:T(8,128)(2,1)} fusion(bf16[1024,2048]{1,0:T(8,128)(2,1)S(1)} %bitcast.108, bf16[256,512]{1,0:T(8,128)(2,1)S(1)} %bitcast.133, bf16[256,512]{1,0:T(8,128)(2,1)S(1)} %bitcast.132, bf16[256,512]{1,0:T(8,128)(2,1)S(1)} %bitcast.131, bf16[256,512]{1,0:T(8,128)(2,1)S(1)} %bitcast.134), kind=kOutput, calls=%fused_computation.2 | convolution fusion | flops 2152726528 | bytes 7340032 | tf_op jit(solution)/shard_map/dot_general | solution.py:10
  179.9 6.9 %fusion = bf16[512,2048]{0,1:T(8,128)(2,1)} fusion(bf16[512,2048]{0,1:T(8,128)(2,1)} %convolution_convert_fusion, bf16[2048,1024]{1,0:T(8,128)(2,1)} %bitcast.107, bf16[512,1024]{1,0:T(8,128)(2,1)} %all-gather.2.cloned.1.call-done), kind=kOutput, calls=%fused_computation.1 | convolution fusion | flops 2150629376 | bytes 9437184 | tf_op jit(solution)/shard_map/dot_general | solution.py:10
  186.8 3.9 %copy.13 = bf16[512,2048]{1,0:T(8,128)(2,1)} copy(bf16[512,2048]{0,1:T(8,128)(2,1)} %fusion) | data formatting | bytes 4194304
  192.5 2.6 %collective-permute-start.31 = (bf16[256,256]{1,0:T(8,128)(2,1)S(1)}, bf16[256,256]{1,0:T(8,128)(2,1)S(1)}, u32[]{:S(2)}, u32[]{:S(2)}) collective-permute-start(bf16[256,256]{1,0:T(8,128)(2,1)S(1)} %convolution_convert_fusion.3), channel_id=1, source_target_pairs={{0,2},{1,3},{2,0},{3,1},{4,6},{5,7},{6,4},{7,5},{8,10},{9,11},{10,... | collective-permute-start | bytes 393224 | tf_op jit(solution)/shard_map/ppermute | solution.py:150
  195.4 2.7 %add_convert_fusion = bf16[256,2048]{1,0:T(8,128)(2,1)} fusion(bf16[256,2048]{1,0:T(8,128)(2,1)S(1)} %collective-permute-done.26, f32[256,2048]{1,0:T(8,128)S(1)} %copy-done.3, bf16[256,2048]{1,0:T(8,128)(2,1)} %collective-permute-done.24), kind=kLoop, calls=%fused_computation.6 | loop fusion | flops 2621440 | bytes 5242880 | tf_op jit(solution)/shard_map/convert_element_type | solution.py:14
  198.1 8.9 %collective-permute-done.31 = bf16[256,256]{1,0:T(8,128)(2,1)S(1)} collective-permute-done((bf16[256,256]{1,0:T(8,128)(2,1)S(1)}, bf16[256,256]{1,0:T(8,128)(2,1)S(1)}, u32[]{:S(2)}, u32[]{:S(2)}) %collective-permute-start.31) | collective-permute-done | bytes 131104 | tf_op jit(solution)/shard_map/ppermute | solution.py:150
  (158 shorter events, 66.1 us)
Async XLA Ops:
  7.2 172.7 %all-gather.2.cloned.1.call-start = ((), (), s32[]{:S(2)}) async-start(), calls=%async_computation | async-start | bytes 1310720 | tf_op jit(solution)/shard_map/all_gather | solution.py:107
  7.2 96.1 %collective-permute-start.16 = (bf16[256,2048]{1,0:T(8,128)(2,1)}, bf16[256,2048]{1,0:T(8,128)(2,1)}, u32[]{:S(2)}, u32[]{:S(2)}) collective-permute-start(bf16[256,2048]{1,0:T(8,128)(2,1)} %bitcast.121), channel_id=1, source_target_pairs={{0,1},{1,2},{2,3},{4,5},{5,6},{6,7},{8,9},{9,10},{10,11},{12,13},{... | collective-permute-start | bytes 3145736 | tf_op jit(solution)/shard_map/ppermute | solution.py:35
  13.3 92.2 %collective-permute-start.17 = (bf16[256,2048]{1,0:T(8,128)(2,1)}, bf16[256,2048]{1,0:T(8,128)(2,1)}, u32[]{:S(2)}, u32[]{:S(2)}) collective-permute-start(bf16[256,2048]{1,0:T(8,128)(2,1)} %bitcast.122), channel_id=1, source_target_pairs={{1,0},{2,1},{3,2},{5,4},{6,5},{7,6},{9,8},{10,9},{11,10},{13,12},{... | collective-permute-start | bytes 3145736 | tf_op jit(solution)/shard_map/ppermute | solution.py:36
  16.1 27.6 %collective-permute-start.12 = (bf16[256,256]{1,0:T(8,128)(2,1)}, bf16[256,256]{1,0:T(8,128)(2,1)}, u32[]{:S(2)}, u32[]{:S(2)}) collective-permute-start(bf16[256,256]{1,0:T(8,128)(2,1)} %bitcast.15), channel_id=1, source_target_pairs={{0,3},{1,0},{2,1},{3,2},{4,7},{5,4},{6,5},{7,6},{8,11},{9,8},{10,9... | collective-permute-start | bytes 393224 | tf_op jit(solution)/shard_map/ppermute | solution.py:20
  20.8 30.6 %collective-permute-start.11 = (bf16[256,256]{1,0:T(8,128)(2,1)}, bf16[256,256]{1,0:T(8,128)(2,1)}, u32[]{:S(2)}, u32[]{:S(2)}) collective-permute-start(bf16[256,256]{1,0:T(8,128)(2,1)} %bitcast.15), channel_id=1, source_target_pairs={{0,2},{1,3},{2,0},{3,1},{4,6},{5,7},{6,4},{7,5},{8,10},{9,11},{10,... | collective-permute-start | bytes 393224 | tf_op jit(solution)/shard_map/ppermute | solution.py:20
  20.8 31.8 %collective-permute-start.10 = (bf16[256,256]{1,0:T(8,128)(2,1)}, bf16[256,256]{1,0:T(8,128)(2,1)S(1)}, u32[]{:S(2)}, u32[]{:S(2)}) collective-permute-start(bf16[256,256]{1,0:T(8,128)(2,1)} %bitcast.15), channel_id=1, source_target_pairs={{0,1},{1,2},{2,3},{3,0},{4,5},{5,6},{6,7},{7,4},{8,9},{9,10},{10,1... | collective-permute-start | bytes 393224 | tf_op jit(solution)/shard_map/ppermute | solution.py:20
  57.4 16.4 %collective-permute-start.2 = (bf16[256,1024]{1,0:T(8,128)(2,1)S(1)}, bf16[256,1024]{1,0:T(8,128)(2,1)S(1)}, u32[]{:S(2)}, u32[]{:S(2)}) collective-permute-start(bf16[256,1024]{1,0:T(8,128)(2,1)S(1)} %dynamic-slice_bitcast_fusion), channel_id=1, source_target_pairs={{1,0},{2,1},{3,2},{5,4},{6,5},{7,6},{9,8},{10,9},{11,10},{13,12},{... | collective-permute-start | bytes 1572872 | tf_op jit(solution)/shard_map/ppermute | solution.py:36
  69.0 14.8 %collective-permute-start.1 = (bf16[256,1024]{1,0:T(8,128)(2,1)S(1)}, bf16[256,1024]{1,0:T(8,128)(2,1)S(1)}, u32[]{:S(2)}, u32[]{:S(2)}) collective-permute-start(bf16[256,1024]{1,0:T(8,128)(2,1)S(1)} %collective-permute-done), channel_id=1, source_target_pairs={{0,16},{16,0},{1,17},{17,1},{2,18},{18,2},{3,19},{19,3},{4,20},{20... | collective-permute-start | bytes 1572872 | tf_op jit(solution)/shard_map/ppermute | solution.py:20
  71.3 28.8 %collective-permute-start.4 = (bf16[256,1024]{1,0:T(8,128)(2,1)S(1)}, bf16[256,1024]{1,0:T(8,128)(2,1)S(1)}, u32[]{:S(2)}, u32[]{:S(2)}) collective-permute-start(bf16[256,1024]{1,0:T(8,128)(2,1)S(1)} %collective-permute-done), channel_id=1, source_target_pairs={{1,2},{2,3},{5,6},{6,7},{9,10},{10,11},{13,14},{14,15},{17,18},{18... | collective-permute-start | bytes 1572872 | tf_op jit(solution)/shard_map/ppermute | solution.py:35
  73.8 21.0 %collective-permute-start.3 = (bf16[256,1024]{1,0:T(8,128)(2,1)S(1)}, bf16[256,1024]{1,0:T(8,128)(2,1)S(1)}, u32[]{:S(2)}, u32[]{:S(2)}) collective-permute-start(bf16[256,1024]{1,0:T(8,128)(2,1)S(1)} %collective-permute-done.2), channel_id=1, source_target_pairs={{0,16},{16,0},{1,17},{17,1},{2,18},{18,2},{3,19},{19,3},{4,20},{20... | collective-permute-start | bytes 1572872 | tf_op jit(solution)/shard_map/ppermute | solution.py:20
  83.8 16.3 %collective-permute-start.5 = (bf16[256,1024]{1,0:T(8,128)(2,1)S(1)}, bf16[256,1024]{1,0:T(8,128)(2,1)S(1)}, u32[]{:S(2)}, u32[]{:S(2)}) collective-permute-start(bf16[256,1024]{1,0:T(8,128)(2,1)S(1)} %collective-permute-done.2), channel_id=1, source_target_pairs={{1,0},{2,1},{5,4},{6,5},{9,8},{10,9},{13,12},{14,13},{17,16},{18,1... | collective-permute-start | bytes 1572872 | tf_op jit(solution)/shard_map/ppermute | solution.py:36
  94.8 30.8 %collective-permute-start.22 = (bf16[256,2048]{1,0:T(8,128)(2,1)S(1)}, bf16[256,2048]{1,0:T(8,128)(2,1)S(1)}, u32[]{:S(2)}, u32[]{:S(2)}) collective-permute-start(bf16[256,2048]{1,0:T(8,128)(2,1)S(1)} %convolution_convert_fusion.1), channel_id=1, source_target_pairs={{0,1},{3,2},{4,5},{7,6},{8,9},{11,10},{12,13},{15,14},{16,17},{19,... | collective-permute-start | bytes 3145736 | tf_op jit(solution)/shard_map/ppermute | solution.py:60
  103.4 37.4 %collective-permute-start.18 = (bf16[256,2048]{1,0:T(8,128)(2,1)}, bf16[256,2048]{1,0:T(8,128)(2,1)S(1)}, u32[]{:S(2)}, u32[]{:S(2)}) collective-permute-start(bf16[256,2048]{1,0:T(8,128)(2,1)} %collective-permute-done.16), channel_id=1, source_target_pairs={{1,2},{2,3},{5,6},{6,7},{9,10},{10,11},{13,14},{14,15},{17,18},{18... | collective-permute-start | bytes 3145736 | tf_op jit(solution)/shard_map/ppermute | solution.py:35
  105.5 18.5 %collective-permute-start.8 = (bf16[256,1024]{1,0:T(8,128)(2,1)S(1)}, bf16[256,1024]{1,0:T(8,128)(2,1)S(1)}, u32[]{:S(2)}, u32[]{:S(2)}) collective-permute-start(bf16[256,1024]{1,0:T(8,128)(2,1)S(1)} %collective-permute-done.5), channel_id=1, source_target_pairs={{1,0},{5,4},{9,8},{13,12},{17,16},{21,20},{25,24},{29,28}} | collective-permute-start | bytes 1572872 | tf_op jit(solution)/shard_map/ppermute | solution.py:36
  114.5 30.1 %collective-permute-start.19 = (bf16[256,2048]{1,0:T(8,128)(2,1)}, bf16[256,2048]{1,0:T(8,128)(2,1)S(1)}, u32[]{:S(2)}, u32[]{:S(2)}) collective-permute-start(bf16[256,2048]{1,0:T(8,128)(2,1)} %collective-permute-done.17), channel_id=1, source_target_pairs={{1,0},{2,1},{5,4},{6,5},{9,8},{10,9},{13,12},{14,13},{17,16},{18,1... | collective-permute-start | bytes 3145736 | tf_op jit(solution)/shard_map/ppermute | solution.py:36
  126.4 21.0 %collective-permute-start.25 = (bf16[256,2048]{1,0:T(8,128)(2,1)S(1)}, bf16[256,2048]{1,0:T(8,128)(2,1)S(1)}, u32[]{:S(2)}, u32[]{:S(2)}) collective-permute-start(bf16[256,2048]{1,0:T(8,128)(2,1)S(1)} %add_convert_fusion.3), channel_id=1, source_target_pairs={{2,1},{3,2},{6,5},{7,6},{10,9},{11,10},{14,13},{15,14},{18,17},{19... | collective-permute-start | bytes 3145736 | tf_op jit(solution)/shard_map/ppermute | solution.py:62
  127.1 23.2 %collective-permute-start.23 = (bf16[256,2048]{1,0:T(8,128)(2,1)S(1)}, bf16[256,2048]{1,0:T(8,128)(2,1)S(1)}, u32[]{:S(2)}, u32[]{:S(2)}) collective-permute-start(bf16[256,2048]{1,0:T(8,128)(2,1)S(1)} %add_convert_fusion.3), channel_id=1, source_target_pairs={{0,1},{1,2},{4,5},{5,6},{8,9},{9,10},{12,13},{13,14},{16,17},{17,1... | collective-permute-start | bytes 3145736 | tf_op jit(solution)/shard_map/ppermute | solution.py:62
  140.7 32.7 %collective-permute-start.20 = (bf16[256,2048]{1,0:T(8,128)(2,1)S(1)}, bf16[256,2048]{1,0:T(8,128)(2,1)S(1)}, u32[]{:S(2)}, u32[]{:S(2)}) collective-permute-start(bf16[256,2048]{1,0:T(8,128)(2,1)S(1)} %collective-permute-done.18), channel_id=1, source_target_pairs={{2,3},{6,7},{10,11},{14,15},{18,19},{22,23},{26,27},{30,31}} | collective-permute-start | bytes 3145736 | tf_op jit(solution)/shard_map/ppermute | solution.py:35
  144.6 28.9 %collective-permute-start.21 = (bf16[256,2048]{1,0:T(8,128)(2,1)S(1)}, bf16[256,2048]{1,0:T(8,128)(2,1)S(1)}, u32[]{:S(2)}, u32[]{:S(2)}) collective-permute-start(bf16[256,2048]{1,0:T(8,128)(2,1)S(1)} %collective-permute-done.19), channel_id=1, source_target_pairs={{1,0},{5,4},{9,8},{13,12},{17,16},{21,20},{25,24},{29,28}} | collective-permute-start | bytes 3145736 | tf_op jit(solution)/shard_map/ppermute | solution.py:36
  149.1 46.3 %collective-permute-start.26 = (bf16[256,2048]{1,0:T(8,128)(2,1)}, bf16[256,2048]{1,0:T(8,128)(2,1)S(1)}, u32[]{:S(2)}, u32[]{:S(2)}) collective-permute-start(bf16[256,2048]{1,0:T(8,128)(2,1)} %add_convert_fusion.1), channel_id=1, source_target_pairs={{1,0},{2,1},{3,2},{5,4},{6,5},{7,6},{9,8},{10,9},{11,10},{13,12},{... | collective-permute-start | bytes 3145736 | tf_op jit(solution)/shard_map/ppermute | solution.py:66
  152.2 43.2 %collective-permute-start.24 = (bf16[256,2048]{1,0:T(8,128)(2,1)}, bf16[256,2048]{1,0:T(8,128)(2,1)}, u32[]{:S(2)}, u32[]{:S(2)}) collective-permute-start(bf16[256,2048]{1,0:T(8,128)(2,1)} %add_convert_fusion.2), channel_id=1, source_target_pairs={{0,1},{1,2},{2,3},{4,5},{5,6},{6,7},{8,9},{9,10},{10,11},{12,13},{... | collective-permute-start | bytes 3145736 | tf_op jit(solution)/shard_map/ppermute | solution.py:66
  174.3 16.4 %collective-permute-start.29 = (f32[16,512]{1,0:T(8,128)S(1)}, f32[16,512]{1,0:T(8,128)S(1)}, u32[]{:S(2)}, u32[]{:S(2)}) collective-permute-start(f32[16,512]{1,0:T(8,128)S(1)} %add_add_fusion), channel_id=1, source_target_pairs={{0,12},{4,0},{8,4},{12,8},{1,13},{5,1},{9,5},{13,9},{2,14},{6,2},{... | collective-permute-start | bytes 98312 | tf_op jit(solution)/shard_map/ppermute | solution.py:20
  174.4 16.4 %collective-permute-start.28 = (f32[16,512]{1,0:T(8,128)S(1)}, f32[16,512]{1,0:T(8,128)}, u32[]{:S(2)}, u32[]{:S(2)}) collective-permute-start(f32[16,512]{1,0:T(8,128)S(1)} %add_add_fusion), channel_id=1, source_target_pairs={{0,8},{4,12},{8,0},{12,4},{1,9},{5,13},{9,1},{13,5},{2,10},{6,14},... | collective-permute-start | bytes 98312 | tf_op jit(solution)/shard_map/ppermute | solution.py:20
  174.9 15.9 %collective-permute-start.27 = (f32[16,512]{1,0:T(8,128)S(1)}, f32[16,512]{1,0:T(8,128)}, u32[]{:S(2)}, u32[]{:S(2)}) collective-permute-start(f32[16,512]{1,0:T(8,128)S(1)} %add_add_fusion), channel_id=1, source_target_pairs={{0,4},{4,8},{8,12},{12,0},{1,5},{5,9},{9,13},{13,1},{2,6},{6,10},{... | collective-permute-start | bytes 98312 | tf_op jit(solution)/shard_map/ppermute | solution.py:20
  (33 other events, 396.5 us)
Sparse Core Ops, SparseCore 0:
  21.5 17.7 all-gather.1

commit v3 on v1

v3 whole, which is shorter than its diff:
```python
import functools

import jax
import jax.numpy as jnp
from jax import lax
from jax.experimental import pallas as pl
from jax.experimental.pallas import tpu as pltpu
from jax.sharding import PartitionSpec as P

adapter_scale = 2.0
vmem_bytes = 24 * 1024 * 1024


def dot(a, b, ca, cb):
    return lax.dot_general(a, b, (((ca,), (cb,)), ((), ())), preferred_element_type=jnp.float32)


def narrow(values):
    return values.astype(jnp.bfloat16)


def turns(value, axis):
    count = lax.axis_size(axis)
    return [
        lax.ppermute(value, axis, [(i, (i + step) % count) for i in range(count)])
        for step in range(1, count)
    ]


def halving(value, axis):
    count = lax.axis_size(axis)
    if count & (count - 1):
        return [value] + turns(value, axis)
    step = 1
    while True:
        other = lax.ppermute(value, axis, [(i, i ^ step) for i in range(count)])
        step *= 2
        if step >= count:
            return [value, other]
        value = value + other


def after(value, *others):
    return lax.optimization_barrier((value, others))[0]


def halving(value, axis):
    count = lax.axis_size(axis)
    if count & (count - 1):
        return [value] + turns(value, axis)
    step = 1
    while True:
        other = lax.ppermute(value, axis, [(i, i ^ step) for i in range(count)])
        step *= 2
        if step >= count:
            return [value, other]
        value = value + other


def after(value, *others):
    return lax.optimization_barrier((value, others))[0]


def line_pass(below, above, axis, step):
    count = lax.axis_size(axis)
    up = [(i, i + 1) for i in range(step - 1, count - 1)]
    down = [(i + 1, i) for i in range(count - step)]
    return lax.ppermute(below, axis, up), lax.ppermute(above, axis, down)


def pairs(count, odd):
    swaps = [(i, i + 1) for i in range(odd, count - 1, 2)]
    return swaps + [(b, a) for a, b in swaps]


def going_up(place, odd):
    return lax.rem(place, 2) == odd


def arrived(count, place, step, odd):
    return jnp.where(going_up(place, odd), place + step, place - step)


def within(count, block):
    return (block >= 0) & (block < count)


def one_sided(count, step):
    return 2 * step >= count


def only_sums(count, step, odd):
    return step >= count - odd


def only_blocks(step, odd):
    return step <= 1 + odd


def named(slot, block, owned, rank):
    shape = (owned * rank, slot.shape[1])
    return (slot - block * owned) == lax.broadcasted_iota(jnp.int32, shape, 0) // rank


def pick(slot, block, values, owned, rank):
    values = jnp.where(named(slot, block, owned, rank), values, 0.0)
    total = values[:rank]
    for at in range(1, owned):
        total = total + values[at * rank : (at + 1) * rank]
    return total


def spread(slot, block, values, owned, rank):
    values = jnp.concatenate([values.astype(jnp.float32)] * owned, axis=0)
    return narrow(jnp.where(named(slot, block, owned, rank), values, 0.0))


def full(shape):
    return pl.BlockSpec(shape, lambda *at: (0,) * len(shape))


def call(body, grid, in_specs, out_specs, out_shape, *operands):
    return pl.pallas_call(
        body,
        grid=grid,
        in_specs=in_specs,
        out_specs=out_specs,
        out_shape=out_shape,
        compiler_params=pltpu.CompilerParams(vmem_limit_bytes=vmem_bytes),
        cost_estimate=pl.CostEstimate(flops=1, bytes_accessed=1, transcendentals=0),
    )(*operands)


def back_sum(slot, cotangent, parts, owned, rank):
    count, rows = len(parts), slot.shape[1]

    def body(slot_ref, cot_ref, *refs):
        place = lax.axis_index("dp")
        slots, cots = slot_ref[...], cot_ref[...]
        total = jnp.zeros((rank, rows), jnp.float32)
        for turn in range(count):
            block = lax.rem(place + count - turn, count)
            total = total + pick(slots, block, dot(refs[turn][...], cots, 1, 1), owned, rank)
        refs[count][...] = total

    return call(
        body,
        (1,),
        [full(slot.shape), full(cotangent.shape)] + [full(part.shape) for part in parts],
        full((rank, rows)),
        jax.ShapeDtypeStruct((rank, rows), jnp.float32),
        slot,
        cotangent,
        *parts,
    )


def scaled_sum(parts):
    def body(*refs):
        total = refs[0][...]
        for ref in refs[1:-1]:
            total = total + ref[...]
        refs[-1][...] = narrow(adapter_scale * narrow(total).astype(jnp.float32))

    shape = parts[0].shape
    return call(
        body,
        (1,),
        [full(shape)] * len(parts),
        full(shape),
        jax.ShapeDtypeStruct(shape, jnp.bfloat16),
        *parts,
    )


def message(step, count, odd, slot, back, inputs, received, owned, rank):
    rows, width = inputs.shape
    tile = 512 if width % 512 == 0 else width
    down_rows = owned * rank
    height = down_rows if only_sums(count, step, odd) else received.shape[0]

    def body(slot_ref, back_ref, in_ref, got_ref, out_ref):
        place = lax.axis_index("dp")
        up = going_up(place, odd)
        along = jnp.where(up, place, count - 1 - place)

        def add():
            target = along + count - step + 1
            block = jnp.where(up, target, count - 1 - target)
            factor = spread(slot_ref[...], block, back_ref[...], owned, rank)
            value = dot(factor, in_ref[...], 1, 0) + got_ref[:down_rows, :].astype(jnp.float32)
            out_ref[:down_rows, :] = narrow(value)
            if height > down_rows:
                out_ref[down_rows:, :] = jnp.zeros((height - down_rows, tile), jnp.bfloat16)

        def pass_on():
            out_ref[...] = got_ref[...]

        if height == down_rows:
            add()
        else:
            pl.when(along < step - 1)(add)
            pl.when(along >= step - 1)(pass_on)

    def moving(height):
        return pl.BlockSpec((height, tile), lambda at: (0, at))

    return call(
        body,
        (width // tile,),
        [full(slot.shape), full(back.shape), moving(rows), moving(height)],
        moving(height),
        jax.ShapeDtypeStruct((height, width), jnp.bfloat16),
        slot,
        back,
        inputs,
        received,
    )


def own_sum(count, slot, back, inputs, received, owned, rank):
    rows, width = inputs.shape
    tile = 512 if width % 512 == 0 else width
    down_rows = owned * rank

    def body(slot_ref, back_ref, in_ref, *refs):
        factor = spread(slot_ref[...], lax.axis_index("dp"), back_ref[...], owned, rank)
        value = dot(factor, in_ref[...], 1, 0)
        for ref in refs[:-1]:
            value = value + ref[...].astype(jnp.float32)
        refs[-1][...] = narrow(value)

    def moving(height):
        return pl.BlockSpec((height, tile), lambda at: (0, at))

    return call(
        body,
        (width // tile,),
        [full(slot.shape), full(back.shape), moving(rows)] + [moving(down_rows)] * len(received),
        moving(down_rows),
        jax.ShapeDtypeStruct((down_rows, width), jnp.bfloat16),
        slot,
        back,
        inputs,
        *received,
    )


def use_pieces(step, count, slot, back, inputs, pieces, held, owned, rank):
    rows, width = inputs.shape
    tile = 512 if width % 512 == 0 else width
    down_rows = owned * rank
    total = len(pieces)
    share = pieces[0].shape[0] - down_rows
    merged = one_sided(count, step) and total > 1
    shared = share * (1 if merged else total)

    def body(slot_ref, back_ref, in_ref, *refs):
        place = lax.axis_index("dp")
        slots, backs, ins = slot_ref[...], back_ref[...], in_ref[...]
        if share:
            proj_ref, low_ref, share_ref = refs[-3:]
            share_refs = refs[total : 2 * total]
            if merged:
                even_came = within(count, arrived(count, place, step, 0))
                share_ref[...] = jnp.where(even_came, share_refs[0][...], share_refs[1][...])
            else:
                for at, ref in enumerate(share_refs):
                    share_ref[at * share : (at + 1) * share, :] = ref[...]
        else:
            proj_ref, low_ref = refs[-2:]
        proj, low = None, None
        for odd, ref in enumerate(refs[:total]):
            block = arrived(count, place, step, odd) if step else place
            value = ref[...]
            term = pick(slots, block, dot(value, ins, 1, 1), owned, rank)
            proj = term if proj is None else proj + term
            term = narrow(dot(spread(slots, block, backs, owned, rank), value, 0, 0))
            low = term if low is None else low + term
        low_ref[...] = low if held is None else low + refs[total * (2 if share else 1)][...]

        @pl.when(pl.program_id(0) == 0)
        def first():
            proj_ref[...] = proj

        @pl.when(pl.program_id(0) > 0)
        def later():
            proj_ref[...] = proj_ref[...] + proj

    def moving(height, at_row=0):
        return pl.BlockSpec((height, tile), lambda at: (at_row, at))

    return call(
        body,
        (width // tile,),
        [full(slot.shape), full(back.shape), moving(rows)]
        + [moving(down_rows)] * total
        + ([moving(share, down_rows // share)] * total if share else [])
        + ([] if held is None else [moving(rows)]),
        [full((rank, rows)), moving(rows)] + ([moving(shared)] if share else []),
        [
            jax.ShapeDtypeStruct((rank, rows), jnp.float32),
            jax.ShapeDtypeStruct((rows, width), jnp.bfloat16),
        ]
        + ([jax.ShapeDtypeStruct((shared, width), jnp.bfloat16)] if share else []),
        slot,
        back,
        inputs,
        *pieces,
        *(pieces if share else []),
        *([] if held is None else [held]),
    )


def up_parts(blocks, slot, proj, cotangent, owned, rank):
    keys = cotangent.shape[1]

    def body(block_ref, slot_ref, proj_ref, cot_ref, *outs):
        slots, projs, cots = slot_ref[...], proj_ref[...], cot_ref[...]
        for at, out in enumerate(outs):
            out[...] = narrow(dot(spread(slots, block_ref[at], projs, owned, rank), cots, 1, 0))

    shape = (owned * rank, keys)
    return call(
        body,
        (1,),
        [pl.BlockSpec(memory_space=pltpu.SMEM)]
        + [full(slot.shape), full(proj.shape), full(cotangent.shape)],
        [full(shape)] * len(blocks),
        [jax.ShapeDtypeStruct(shape, jnp.bfloat16)] * len(blocks),
        jnp.stack(blocks),
        slot,
        proj,
        cotangent,
    )


def pack(down_own, weight):
    down_rows, width = down_own.shape
    half = weight.shape[0] // lax.axis_size("groups")
    keys = weight.shape[1]
    chunks = width // keys
    chunk = half // chunks

    def body(down_ref, weight_ref, out_ref):
        group = lax.axis_index("groups")
        out_ref[:down_rows, :] = down_ref[...]
        for at in range(chunks):
            rows = pl.ds(pl.multiple_of(group * half + at * chunk, chunk), chunk)
            out_ref[down_rows:, at * keys : (at + 1) * keys] = weight_ref[rows, :]

    shape = (down_rows + chunk, width)
    return call(
        body,
        (1,),
        [full(down_own.shape), full(weight.shape)],
        full(shape),
        jax.ShapeDtypeStruct(shape, jnp.bfloat16),
        down_own,
        weight,
    )


def finish(cotangents, weight_own, steps, pieces, low):
    rows, width = low.shape
    weight_rows, keys = weight_own.shape
    shard = cotangents[0].shape[1]
    count, groups, parts = lax.axis_size("dp"), lax.axis_size("groups"), len(cotangents)
    half = weight_rows // groups
    chunks = width // keys
    chunk = half // chunks
    some = max(1, 512 // weight_rows)
    tile = some * weight_rows

    def body(*refs):
        cot_refs, own_ref, refs = refs[:parts], refs[parts], refs[parts + 1 :]
        piece_refs, (low_ref, out_ref, dy_ref, weight_ref) = refs[:-4], refs[-4:]

        @pl.when(pl.program_id(0) == 0)
        def arrange():
            place, group, part = (lax.axis_index(axis) for axis in ("dp", "groups", "fsdp"))
            for turn, ref in enumerate(cot_refs):
                at = lax.rem(part + parts - turn, parts) * shard
                dy_ref[:, pl.ds(pl.multiple_of(at, shard), shard)] = ref[...]
            weight_ref[place] = own_ref[...]
            for at, ref in enumerate(piece_refs):
                step, odds = steps[at // groups]
                owner = lax.rem(group + groups - at % groups, groups)
                for odd in odds:
                    block = arrived(count, place, step, odd)
                    number = 0 if one_sided(count, step) else odd

                    def store(number=number, block=block):
                        for part in range(chunks):
                            row = pl.multiple_of(owner * half + part * chunk, chunk)
                            weight_ref[block, pl.ds(row, chunk), :] = ref[
                                number * chunk : (number + 1) * chunk,
                                part * keys : (part + 1) * keys,
                            ]

                    pl.when(within(count, block))(store)

        for block in range(some):
            at = slice(block * weight_rows, (block + 1) * weight_rows)
            base = dot(dy_ref[...], weight_ref[pl.program_id(0) * some + block], 1, 1)
            out_ref[:, at] = narrow(base + low_ref[:, at].astype(jnp.float32))

    columns = pl.BlockSpec((rows, tile), lambda at: (0, at))
    fixed = [*cotangents, weight_own, *pieces]
    return pl.pallas_call(
        body,
        grid=(width // tile,),
        in_specs=[full(array.shape) for array in fixed] + [columns],
        out_specs=columns,
        out_shape=jax.ShapeDtypeStruct((rows, width), jnp.bfloat16),
        scratch_shapes=[
            pltpu.VMEM((rows, keys), jnp.bfloat16),
            pltpu.VMEM((count, weight_rows, keys), jnp.bfloat16),
        ],
        compiler_params=pltpu.CompilerParams(vmem_limit_bytes=vmem_bytes),
        cost_estimate=pl.CostEstimate(flops=1, bytes_accessed=1, transcendentals=0),
    )(*fixed, low)


def shards(
    inputs,
    cotangent,
    frozen_key_weight,
    adapter_down_weight,
    adapter_up_weight,
    row_adapter_index,
    adapter_slot_index,
):
    tok_rows, feat_width = inputs.shape
    key_shard = cotangent.shape[1]
    owned, rank, _ = adapter_down_weight.shape
    slots = adapter_slot_index.shape[0]
    data_count, place = lax.axis_size("dp"), lax.axis_index("dp")
    down_rows = owned * rank
    key_at = lax.axis_index("fsdp") * key_shard

    up_own = lax.dynamic_slice_in_dim(adapter_up_weight, key_at, key_shard, 2)
    up_own = up_own.reshape(down_rows, key_shard)
    ups = [up_own] + turns(up_own, "dp")
    down_own = adapter_down_weight.reshape(down_rows, feat_width)
    packed = pack(down_own, frozen_key_weight)

    ids = row_adapter_index[:, 0]
    every = lax.broadcasted_iota(jnp.int32, (slots, tok_rows), 0)
    slot = jnp.sum(jnp.where(ids[None, :] == every, adapter_slot_index[:, None], 0), axis=0)
    slot = slot[None, :]

    back = back_sum(slot, cotangent, ups, owned, rank)
    back = scaled_sum([back] + turns(back, "fsdp"))
    cotangents = [cotangent] + turns(after(cotangent, back), "fsdp")
    proj, low = use_pieces(0, data_count, slot, back, inputs, [down_own], None, owned, rank)

    def up_swaps(steps, proj):
        routes = []
        for step in steps:
            for odd in (0, 1):
                ends = [i for i in range(data_count - step) if i // step % 2 == odd]
                if ends:
                    other = jnp.where(place // step % 2 == odd, place + step, place - step)
                    swaps = [(i, i + step) for i in ends] + [(i + step, i) for i in ends]
                    routes.append((other, swaps))
        parts = up_parts(
            [place] + [other for other, _ in routes], slot, proj, cotangent, owned, rank
        )
        return parts, [lax.ppermute(part, "dp", way) for part, (_, way) in zip(parts[1:], routes)]

    early = data_count // 2
    received = [after(packed, *ups)] * 2
    steps, shares, up_grads, waited = [], [], [], [[], [cotangents]]
    for step in range(1, data_count + 1):
        sent = []
        for odd, other in enumerate(reversed(received)):
            other = after(other, waited[step - 1])
            if not only_blocks(step, odd):
                other = message(step, data_count, odd, slot, back, inputs, other, owned, rank)
            sent.append(other)
        if step > 1:
            got = after(got, sent)
            term, low, share = use_pieces(
                step - 1, data_count, slot, back, inputs, got, low, owned, rank
            )
            proj = proj + term
            share = [share] + turns(share, "groups")
            shares += share
            waited.append([low, share])
            if step - 1 == early:
                near = scaled_sum(halving(proj, "fsdp"))
                parts, up_grads = up_swaps(range(1, early + 1), near)
                up_grads.append(parts[0])
                waited[-1].append(parts)
                proj = 0.0
        received = [lax.ppermute(sent[odd], "dp", pairs(data_count, odd)) for odd in (0, 1)]
        odds = [odd for odd in (0, 1) if not only_sums(data_count, step, odd)]
        got = [received[odd] for odd in odds]
        steps.append((step, odds))

    far = scaled_sum(halving(proj, "fsdp"))
    up_grads += up_swaps(range(early + 1, data_count), far)[1]
    up_grad = sum(part.astype(jnp.float32) for part in up_grads)

    input_grad = finish(cotangents, frozen_key_weight, steps[:-1], shares, low)
    received = after(received, input_grad)
    down_grad = own_sum(data_count, slot, back, inputs, received, owned, rank)
    return (
        input_grad,
        down_grad.reshape(owned, rank, feat_width),
        narrow(up_grad).reshape(owned, rank, key_shard),
    )


def solution(mesh):
    placed = (
        P(("groups", "dp"), "fsdp"),
        P(("groups", "dp"), "fsdp"),
        P(("fsdp", "dp"), None),
        P(("groups", "dp"), None, "fsdp"),
        P(("groups", "dp"), None, None),
        P(("groups", "dp"), None),
        P("groups"),
    )
    return jax.shard_map(
        shards,
        mesh=mesh,
        in_specs=placed,
        out_specs=(
            P(("groups", "dp"), "fsdp"),
            P(("groups", "dp"), None, "fsdp"),
            P(("groups", "dp"), None, "fsdp"),
        ),
        check_vma=False,
    )
```

time: 303 us -> 189 us (0.62)
  waiting for transfers between devices: 228 us -> 76.3 us
  starting transfers between devices: 0.19 us -> 50.3 us
  Pallas kernels: 0 us -> 43.8 us
  blocking collectives: 34.1 us -> 0 us
  matrix products: 24.8 us -> 0 us
  local copies, waits for them, and re-layouts: 0.94 us -> 14.4 us
  between operations: 13.9 us -> 0.95 us
    all_gather x3 -> x0, waiting for transfers between devices: 132 us -> none  [the longest x1 70.5 us: shards(): weight = lax.all_gather(frozen_key_weight, 'dp', axis=0, tiled=True)]
    reduce_scatter x2 -> x0, waiting for transfers between devices: 93.9 us -> none  [the longest x1 77.8 us: shards(): lax.psum_scatter(down_part, 'dp', scatter_dimension=0, tiled=True)]
    ppermute x0 -> x28, waiting for transfers between devices: none -> 76.3 us  [the longest x12 41.2 us: turns(): lax.ppermute(value, axis, [(i, (i + step) % count) for i in range(count)])]
    ppermute x0 -> x28, starting transfers between devices: none -> 50.3 us  [the longest x8 20.3 us: shards(): lax.ppermute(sent[odd], 'dp', pairs(data_count, odd))]
    pallas_call x0 -> x18, Pallas kernels: none -> 43.8 us  [the longest x17 38 us: call(): pl.pallas_call(body, grid=grid, in_specs=in_specs, out_specs=out_specs, o...]
    dot_general x6 -> x0, matrix products: 24.8 us -> none  [dot(): lax.dot_general(a, b, (((ca,), (cb,)), ((), ())), preferred_element_type=...]
    all_gather x1 -> x0, blocking collectives: 21.1 us -> none  [shards(): lax.all_gather(up_own.reshape(owned * rank, key_shard), 'dp', axis=0, til...]
    unnamed x10 -> x50, local copies, waits for them, and re-layouts: 0.03 us -> 14.4 us
  transfers between devices with their start and end apart: 5 -> 28, of which waited for: 4 -> 16; matrix products, arithmetic and copies ran while one was open for 9% -> 1% of each run, Pallas kernels for 0% -> 21%
where the time goes in v3:
time: 189 us; the launch traced here: 188 us
  waiting for transfers between devices  76.3 us (40%)
  starting transfers between devices  50.3 us (27%)
  Pallas kernels  43.8 us (23%)
  local copies, waits for them, and re-layouts  14.4 us (8%)
  other arithmetic  2.04 us (1%)
    ppermute x12, waiting for transfers between devices, turns(): lax.ppermute(value, axis, [(i, (i + step) % count) for i in range(count)])  41.2 us
    pallas_call x17, Pallas kernels, call(): pl.pallas_call(body, grid=grid, in_specs=in_specs, out_specs=out_specs, o...  38 us
    ppermute x8, starting transfers between devices, shards(): lax.ppermute(sent[odd], 'dp', pairs(data_count, odd))  20.3 us
    ppermute x8, waiting for transfers between devices, shards(): lax.ppermute(sent[odd], 'dp', pairs(data_count, odd))  18.9 us
    ppermute x12, starting transfers between devices, turns(): lax.ppermute(value, axis, [(i, (i + step) % count) for i in range(count)])  17.1 us
    unnamed x50, local copies, waits for them, and re-layouts  14.4 us
    ppermute x4, waiting for transfers between devices, up_swaps(): lax.ppermute(part, 'dp', way)  11.5 us
    ppermute x4, starting transfers between devices, up_swaps(): lax.ppermute(part, 'dp', way)  9.82 us
  transfers between devices with their start and end apart: 28, of which 16 were waited for; matrix products, arithmetic and copies ran while one was open for 1% of the time, Pallas kernels for 21%

profile of v3, /device:TPU:0, one launch (start us, length us, event | category | flops | bytes accessed | tf_op | source)
XLA Modules:
  0.0 187.8 jit_solution(17646848676050505590)
XLA Ops:
  1.7 3.1 %collective-permute-start = (bf16[256,256]{1,0:T(8,128)(2,1)S(1)}, bf16[256,256]{1,0:T(8,128)(2,1)S(1)}, u32[]{:S(2)}, u32[]{:S(2)}) collective-permute-start(bf16[256,256]{1,0:T(8,128)(2,1)S(1)} %bitcast.13), channel_id=1, source_target_pairs={{0,1},{1,2},{2,3},{3,0},{4,5},{5,6},{6,7},{7,4},{8,9},{9,10},{10,1... | collective-permute-start | bytes 393224 | tf_op jit(solution)/shard_map/ppermute | solution.py:25
  4.8 2.6 %collective-permute-start.1 = (bf16[256,256]{1,0:T(8,128)(2,1)S(1)}, bf16[256,256]{1,0:T(8,128)(2,1)S(1)}, u32[]{:S(2)}, u32[]{:S(2)}) collective-permute-start(bf16[256,256]{1,0:T(8,128)(2,1)S(1)} %bitcast.14), channel_id=1, source_target_pairs={{0,2},{1,3},{2,0},{3,1},{4,6},{5,7},{6,4},{7,5},{8,10},{9,11},{10,... | collective-permute-start | bytes 393224 | tf_op jit(solution)/shard_map/ppermute | solution.py:25
  11.3 4.7 %collective-permute-done.1.refs_2_ = bf16[256,256]{1,0:T(8,128)(2,1)S(1)} collective-permute-done((bf16[256,256]{1,0:T(8,128)(2,1)S(1)}, bf16[256,256]{1,0:T(8,128)(2,1)S(1)}, u32[]{:S(2)}, u32[]{:S(2)}) %collective-permute-start.1) | collective-permute-done | bytes 131104 | tf_op jit(solution)/shard_map/ppermute | solution.py:25
  16.0 3.3 %collective-permute-start.9 = (bf16[384,2048]{1,0:T(8,128)(2,1)S(1)}, bf16[384,2048]{1,0:T(8,128)(2,1)S(1)}, u32[]{:S(2)}, u32[]{:S(2)}) collective-permute-start(bf16[384,2048]{1,0:T(8,128)(2,1)S(1)} %shard_map.96), channel_id=1, source_target_pairs={{0,1},{2,3},{1,0},{3,2},{4,5},{6,7},{5,4},{7,6},{8,9},{10,11},{9,8... | collective-permute-start | bytes 4718600 | tf_op jit(solution)/shard_map/ppermute | solution.py:497
  27.8 5.2 %collective-permute-done.6.refs_1_ = bf16[512,256]{1,0:T(8,128)(2,1)S(1)} collective-permute-done((bf16[512,256]{1,0:T(8,128)(2,1)S(1)}, bf16[512,256]{1,0:T(8,128)(2,1)S(1)}, u32[]{:S(2)}, u32[]{:S(2)}) %collective-permute-start.6) | collective-permute-done | bytes 262176 | tf_op jit(solution)/shard_map/ppermute | solution.py:25
  33.0 2.5 %collective-permute-done.7.refs_2_ = bf16[512,256]{1,0:T(8,128)(2,1)S(1)} collective-permute-done((bf16[512,256]{1,0:T(8,128)(2,1)S(1)}, bf16[512,256]{1,0:T(8,128)(2,1)S(1)}, u32[]{:S(2)}, u32[]{:S(2)}) %collective-permute-start.7) | collective-permute-done | bytes 262176 | tf_op jit(solution)/shard_map/ppermute | solution.py:25
  35.5 2.6 %collective-permute-done.8.refs_3_ = bf16[512,256]{1,0:T(8,128)(2,1)S(1)} collective-permute-done((bf16[512,256]{1,0:T(8,128)(2,1)S(1)}, bf16[512,256]{1,0:T(8,128)(2,1)S(1)}, u32[]{:S(2)}, u32[]{:S(2)}) %collective-permute-start.8) | collective-permute-done | bytes 262176 | tf_op jit(solution)/shard_map/ppermute | solution.py:25
  38.1 15.8 %collective-permute-done.9.refs_0_.refs_2_ = bf16[384,2048]{1,0:T(8,128)(2,1)S(1)} collective-permute-done((bf16[384,2048]{1,0:T(8,128)(2,1)S(1)}, bf16[384,2048]{1,0:T(8,128)(2,1)S(1)}, u32[]{:S(2)}, u32[]{:S(2)}) %collective-permute-start.9) | collective-permute-done | bytes 1572896 | tf_op jit(solution)/shard_map/ppermute | solution.py:497
  60.7 3.9 %shard_map.99 = (f32[16,512]{1,0:T(8,128)S(1)}, bf16[512,2048]{1,0:T(8,128)(2,1)S(1)}, bf16[256,2048]{1,0:T(8,128)(2,1)S(1)}) custom-call(s32[1,512]{1,0:T(1,128)S(1)} %bitcast.20, bf16[16,512]{1,0:T(8,128)(2,1)S(1)} %shard_map.95.back_ref, bf16[512,2048]{1,0:T(8,128)(2,1)S(1)} %copy-done.1, bf16[384,2048]{1,0:T(8,128)(2,1)S(1)} %collective-permute-done.9.refs_0_.refs_2_, ...), custom_call_target="tpu_custom_call" | custom-call | flops 1 | bytes 1 | tf_op jit(solution)/shard_map/pallas_call | solution.py:123
  66.2 22.4 %collective-permute-done.11.refs_6_ = bf16[256,2048]{1,0:T(8,128)(2,1)S(1)} collective-permute-done((bf16[256,2048]{1,0:T(8,128)(2,1)S(1)}, bf16[256,2048]{1,0:T(8,128)(2,1)S(1)}, u32[]{:S(2)}, u32[]{:S(2)}) %collective-permute-start.11) | collective-permute-done | bytes 1048608 | tf_op jit(solution)/shard_map/ppermute | solution.py:25
  88.6 2.8 %shard_map.100 = bf16[384,2048]{1,0:T(8,128)(2,1)} custom-call(s32[1,512]{1,0:T(1,128)S(1)} %bitcast.21, bf16[16,512]{1,0:T(8,128)(2,1)S(1)} %shard_map.95.back_ref, bf16[512,2048]{1,0:T(8,128)(2,1)S(1)} %copy-done.1, bf16[384,2048]{1,0:T(8,128)(2,1)S(1)} %collective-permute-done.13.got_ref.refs_1_.refs_3_), custom_call_target="tpu_custom_call" | custom-call | flops 1 | bytes 1 | tf_op jit(solution)/shard_map/pallas_call | solution.py:123
  91.4 3.5 %collective-permute-start.15 = (bf16[384,2048]{1,0:T(8,128)(2,1)}, bf16[384,2048]{1,0:T(8,128)(2,1)}, u32[]{:S(2)}, u32[]{:S(2)}) collective-permute-start(bf16[384,2048]{1,0:T(8,128)(2,1)} %shard_map.100), channel_id=1, source_target_pairs={{0,1},{2,3},{1,0},{3,2},{4,5},{6,7},{5,4},{7,6},{8,9},{10,11},{9,8... | collective-permute-start | bytes 4718600 | tf_op jit(solution)/shard_map/ppermute | solution.py:497
  95.0 2.6 %shard_map.101 = bf16[256,2048]{1,0:T(8,128)(2,1)} custom-call(s32[1,512]{1,0:T(1,128)S(1)} %bitcast.22, bf16[16,512]{1,0:T(8,128)(2,1)S(1)} %shard_map.95.back_ref, bf16[512,2048]{1,0:T(8,128)(2,1)S(1)} %copy-done.1, bf16[384,2048]{1,0:T(8,128)(2,1)S(1)} %collective-permute-done.12.got_ref.refs_0_.refs_2_), custom_call_target="tpu_custom_call" | custom-call | flops 1 | bytes 1 | tf_op jit(solution)/shard_map/pallas_call | solution.py:123
  99.3 3.8 %shard_map.102 = (f32[16,512]{1,0:T(8,128)S(1)}, bf16[512,2048]{1,0:T(8,128)(2,1)S(1)}, bf16[128,2048]{1,0:T(8,128)(2,1)S(1)}) custom-call(s32[1,512]{1,0:T(1,128)S(1)} %bitcast.23, bf16[16,512]{1,0:T(8,128)(2,1)S(1)} %shard_map.95.back_ref, bf16[512,2048]{1,0:T(8,128)(2,1)S(1)} %copy-done.1, ...), custom_call_target="tpu_custom_call" | custom-call | flops 1 | bytes 1 | tf_op jit(solution)/shard_map/pallas_call | solution.py:123
  116.4 4.1 %shard_map.105 = bf16[256,2048]{1,0:T(8,128)(2,1)} custom-call(s32[1,512]{1,0:T(1,128)S(1)} %bitcast.25, bf16[16,512]{1,0:T(8,128)(2,1)S(1)} %shard_map.95.back_ref, bf16[512,2048]{1,0:T(8,128)(2,1)S(1)} %copy-done.1, bf16[256,2048]{1,0:T(8,128)(2,1)} %collective-permute-done.16.got_ref), custom_call_target="tpu_custom_call" | custom-call | flops 1 | bytes 1 | tf_op jit(solution)/shard_map/pallas_call | solution.py:123
  120.5 6.8 %collective-permute-start.20 = (bf16[256,2048]{1,0:T(8,128)(2,1)}, bf16[256,2048]{1,0:T(8,128)(2,1)}, u32[]{:S(2)}, u32[]{:S(2)}) collective-permute-start(bf16[256,2048]{1,0:T(8,128)(2,1)} %shard_map.105), channel_id=1, source_target_pairs={{0,1},{2,3},{1,0},{3,2},{4,5},{6,7},{5,4},{7,6},{8,9},{10,11},{9,8... | collective-permute-start | bytes 3145736 | tf_op jit(solution)/shard_map/ppermute | solution.py:497
  127.3 3.0 %collective-permute-done.15.got_ref.refs_0_.refs_1_ = bf16[384,2048]{1,0:T(8,128)(2,1)} collective-permute-done((bf16[384,2048]{1,0:T(8,128)(2,1)}, bf16[384,2048]{1,0:T(8,128)(2,1)}, u32[]{:S(2)}, u32[]{:S(2)}) %collective-permute-start.15) | collective-permute-done | bytes 1572896 | tf_op jit(solution)/shard_map/ppermute | solution.py:497
  130.4 4.1 %shard_map.106 = bf16[256,2048]{1,0:T(8,128)(2,1)} custom-call(s32[1,512]{1,0:T(1,128)S(1)} %bitcast.26, bf16[16,512]{1,0:T(8,128)(2,1)S(1)} %shard_map.95.back_ref, bf16[512,2048]{1,0:T(8,128)(2,1)S(1)} %copy-done.1, bf16[384,2048]{1,0:T(8,128)(2,1)} %collective-permute-done.15.got_ref.refs_0_.refs_1_), custom_call_target="tpu_custom_call" | custom-call | flops 1 | bytes 1 | tf_op jit(solution)/shard_map/pallas_call | solution.py:123
  136.1 4.5 %shard_map.107 = (f32[16,512]{1,0:T(8,128)S(1)}, bf16[512,2048]{1,0:T(8,128)(2,1)S(1)}, bf16[128,2048]{1,0:T(8,128)(2,1)}) custom-call(s32[1,512]{1,0:T(1,128)S(1)} %bitcast.27, bf16[16,512]{1,0:T(8,128)(2,1)S(1)} %shard_map.95.back_ref, bf16[512,2048]{1,0:T(8,128)(2,1)S(1)} %copy-done.1, bf16[384,2048]{1,0:T(8,128)(2,1)} %collective-permute-done.15.got_ref.refs_0_.refs_1_, ...), custom_call_target="tpu_custom_call" | custom-call | flops 1 | bytes 1 | tf_op jit(solution)/shard_map/pallas_call | solution.py:123
  146.2 2.5 %collective-permute-start.22 = (bf16[256,256]{1,0:T(8,128)(2,1)}, bf16[256,256]{1,0:T(8,128)(2,1)}, u32[]{:S(2)}, u32[]{:S(2)}) collective-permute-start(bf16[256,256]{1,0:T(8,128)(2,1)} %get-tuple-element.53), channel_id=1, source_target_pairs={{0,1},{2,3},{1,0},{3,2},{4,5},{6,7},{5,4},{7,6},{8,9},{10,11},{9,8... | collective-permute-start | bytes 393224 | tf_op jit(solution)/shard_map/ppermute | solution.py:470
  155.1 4.2 %collective-permute-start.27 = (bf16[256,256]{1,0:T(8,128)(2,1)S(1)}, bf16[256,256]{1,0:T(8,128)(2,1)S(1)}, u32[]{:S(2)}, u32[]{:S(2)}) collective-permute-start(bf16[256,256]{1,0:T(8,128)(2,1)S(1)} %get-tuple-element.64), channel_id=1, source_target_pairs={{0,3},{3,0},{4,7},{7,4},{8,11},{11,8},{12,15},{15,12},{16,19},{19,... | collective-permute-start | bytes 393224 | tf_op jit(solution)/shard_map/ppermute | solution.py:470
  159.4 9.7 %collective-permute-done.24 = bf16[256,256]{1,0:T(8,128)(2,1)S(1)} collective-permute-done((bf16[256,256]{1,0:T(8,128)(2,1)}, bf16[256,256]{1,0:T(8,128)(2,1)S(1)}, u32[]{:S(2)}, u32[]{:S(2)}) %collective-permute-start.24) | collective-permute-done | bytes 131104 | tf_op jit(solution)/shard_map/ppermute | solution.py:470
  177.8 5.8 %shard_map.108 = bf16[512,2048]{1,0:T(8,128)(2,1)} custom-call(bf16[512,256]{1,0:T(8,128)(2,1)S(1)} %copy-done.4, bf16[512,256]{1,0:T(8,128)(2,1)S(1)} %copy-done.16, bf16[512,256]{1,0:T(8,128)(2,1)S(1)} %copy-done.18, bf16[512,256]{1,0:T(8,128)(2,1)S(1)} %copy-done.20, bf16[512,1024]{1,0:T(8,128)(2,1)S(1)} %copy-done.3, bf16[256,2048]{1,0:T(8,128)(2,1)S(1)} %copy-done.12, ...), custom_call_target="tpu_custom_call" | custom-call | flops 1 | bytes 1 | tf_op jit(solution)/shard_map/pallas_call | solution.py:410
  183.6 4.2 %shard_map.109 = bf16[256,2048]{1,0:T(8,128)(2,1)} custom-call(s32[1,512]{1,0:T(1,128)S(1)} %bitcast.29, bf16[16,512]{1,0:T(8,128)(2,1)S(1)} %shard_map.95.back_ref, bf16[512,2048]{1,0:T(8,128)(2,1)S(1)} %copy-done.1, bf16[256,2048]{1,0:T(8,128)(2,1)} %collective-permute-done.20.refs_0_, bf16[256,2048]{1,0:T(8,128)(2,1)} %collective-permute-done.21.refs_1_), custom_call_target="tpu_custom_call" | custom-call | flops 1 | bytes 1 | tf_op jit(solution)/shard_map/pallas_call | solution.py:123
  (108 shorter events, 58.9 us)
Async XLA Ops:
  1.7 9.6 %collective-permute-start = (bf16[256,256]{1,0:T(8,128)(2,1)S(1)}, bf16[256,256]{1,0:T(8,128)(2,1)S(1)}, u32[]{:S(2)}, u32[]{:S(2)}) collective-permute-start(bf16[256,256]{1,0:T(8,128)(2,1)S(1)} %bitcast.13), channel_id=1, source_target_pairs={{0,1},{1,2},{2,3},{3,0},{4,5},{5,6},{6,7},{7,4},{8,9},{9,10},{10,1... | collective-permute-start | bytes 393224 | tf_op jit(solution)/shard_map/ppermute | solution.py:25
  4.8 11.2 %collective-permute-start.1 = (bf16[256,256]{1,0:T(8,128)(2,1)S(1)}, bf16[256,256]{1,0:T(8,128)(2,1)S(1)}, u32[]{:S(2)}, u32[]{:S(2)}) collective-permute-start(bf16[256,256]{1,0:T(8,128)(2,1)S(1)} %bitcast.14), channel_id=1, source_target_pairs={{0,2},{1,3},{2,0},{3,1},{4,6},{5,7},{6,4},{7,5},{8,10},{9,11},{10,... | collective-permute-start | bytes 393224 | tf_op jit(solution)/shard_map/ppermute | solution.py:25
  7.4 8.6 %collective-permute-start.2 = (bf16[256,256]{1,0:T(8,128)(2,1)S(1)}, bf16[256,256]{1,0:T(8,128)(2,1)S(1)}, u32[]{:S(2)}, u32[]{:S(2)}) collective-permute-start(bf16[256,256]{1,0:T(8,128)(2,1)S(1)} %bitcast.15), channel_id=1, source_target_pairs={{0,3},{1,0},{2,1},{3,2},{4,7},{5,4},{6,5},{7,6},{8,11},{9,8},{10,9... | collective-permute-start | bytes 393224 | tf_op jit(solution)/shard_map/ppermute | solution.py:25
  16.0 37.8 %collective-permute-start.9 = (bf16[384,2048]{1,0:T(8,128)(2,1)S(1)}, bf16[384,2048]{1,0:T(8,128)(2,1)S(1)}, u32[]{:S(2)}, u32[]{:S(2)}) collective-permute-start(bf16[384,2048]{1,0:T(8,128)(2,1)S(1)} %shard_map.96), channel_id=1, source_target_pairs={{0,1},{2,3},{1,0},{3,2},{4,5},{6,7},{5,4},{7,6},{8,9},{10,11},{9,8... | collective-permute-start | bytes 4718600 | tf_op jit(solution)/shard_map/ppermute | solution.py:497
  19.3 35.3 %collective-permute-start.10 = (bf16[384,2048]{1,0:T(8,128)(2,1)S(1)}, bf16[384,2048]{1,0:T(8,128)(2,1)S(1)}, u32[]{:S(2)}, u32[]{:S(2)}) collective-permute-start(bf16[384,2048]{1,0:T(8,128)(2,1)S(1)} %shard_map.96), channel_id=1, source_target_pairs={{1,2},{2,1},{5,6},{6,5},{9,10},{10,9},{13,14},{14,13},{17,18},{18,... | collective-permute-start | bytes 4718600 | tf_op jit(solution)/shard_map/ppermute | solution.py:497
  20.7 4.0 %collective-permute-start.4 = (f32[16,512]{1,0:T(8,128)S(1)}, f32[16,512]{1,0:T(8,128)S(1)}, u32[]{:S(2)}, u32[]{:S(2)}) collective-permute-start(f32[16,512]{1,0:T(8,128)S(1)} %shard_map.94.refs_0_), channel_id=1, source_target_pairs={{0,8},{4,12},{8,0},{12,4},{1,9},{5,13},{9,1},{13,5},{2,10},{6,14},... | collective-permute-start | bytes 98312 | tf_op jit(solution)/shard_map/ppermute | solution.py:25
  25.3 7.7 %collective-permute-start.6 = (bf16[512,256]{1,0:T(8,128)(2,1)S(1)}, bf16[512,256]{1,0:T(8,128)(2,1)S(1)}, u32[]{:S(2)}, u32[]{:S(2)}) collective-permute-start(bf16[512,256]{1,0:T(8,128)(2,1)S(1)} %copy-done.4), channel_id=1, source_target_pairs={{0,4},{4,8},{8,12},{12,0},{1,5},{5,9},{9,13},{13,1},{2,6},{6,10},{... | collective-permute-start | bytes 786440 | tf_op jit(solution)/shard_map/ppermute | solution.py:25
  26.3 9.2 %collective-permute-start.7 = (bf16[512,256]{1,0:T(8,128)(2,1)S(1)}, bf16[512,256]{1,0:T(8,128)(2,1)S(1)}, u32[]{:S(2)}, u32[]{:S(2)}) collective-permute-start(bf16[512,256]{1,0:T(8,128)(2,1)S(1)} %copy-done.4), channel_id=1, source_target_pairs={{0,8},{4,12},{8,0},{12,4},{1,9},{5,13},{9,1},{13,5},{2,10},{6,14},... | collective-permute-start | bytes 786440 | tf_op jit(solution)/shard_map/ppermute | solution.py:25
  27.8 10.3 %collective-permute-start.8 = (bf16[512,256]{1,0:T(8,128)(2,1)S(1)}, bf16[512,256]{1,0:T(8,128)(2,1)S(1)}, u32[]{:S(2)}, u32[]{:S(2)}) collective-permute-start(bf16[512,256]{1,0:T(8,128)(2,1)S(1)} %copy-done.4), channel_id=1, source_target_pairs={{0,12},{4,0},{8,4},{12,8},{1,13},{5,1},{9,5},{13,9},{2,14},{6,2},{... | collective-permute-start | bytes 786440 | tf_op jit(solution)/shard_map/ppermute | solution.py:25
  53.9 34.8 %collective-permute-start.13 = (bf16[384,2048]{1,0:T(8,128)(2,1)S(1)}, bf16[384,2048]{1,0:T(8,128)(2,1)S(1)}, u32[]{:S(2)}, u32[]{:S(2)}) collective-permute-start(bf16[384,2048]{1,0:T(8,128)(2,1)S(1)} %collective-permute-done.9.refs_0_.refs_2_), channel_id=1, source_target_pairs={{1,2},{2,1},{5,6},{6,5},{9,10},{10,9},{13,14},{14,13},{17,18},{18,... | collective-permute-start | bytes 4718600 | tf_op jit(solution)/shard_map/ppermute | solution.py:497
  56.4 38.6 %collective-permute-start.12 = (bf16[384,2048]{1,0:T(8,128)(2,1)S(1)}, bf16[384,2048]{1,0:T(8,128)(2,1)S(1)}, u32[]{:S(2)}, u32[]{:S(2)}) collective-permute-start(bf16[384,2048]{1,0:T(8,128)(2,1)S(1)} %shard_map.97), channel_id=1, source_target_pairs={{0,1},{2,3},{1,0},{3,2},{4,5},{6,7},{5,4},{7,6},{8,9},{10,11},{9,8... | collective-permute-start | bytes 4718600 | tf_op jit(solution)/shard_map/ppermute | solution.py:497
  64.6 24.0 %collective-permute-start.11 = (bf16[256,2048]{1,0:T(8,128)(2,1)S(1)}, bf16[256,2048]{1,0:T(8,128)(2,1)S(1)}, u32[]{:S(2)}, u32[]{:S(2)}) collective-permute-start(bf16[256,2048]{1,0:T(8,128)(2,1)S(1)} %get-tuple-element.41.refs_5_), channel_id=1, source_target_pairs={{0,16},{16,0},{1,17},{17,1},{2,18},{18,2},{3,19},{19,3},{4,20},{20... | collective-permute-start | bytes 3145736 | tf_op jit(solution)/shard_map/ppermute | solution.py:25
  91.4 38.9 %collective-permute-start.15 = (bf16[384,2048]{1,0:T(8,128)(2,1)}, bf16[384,2048]{1,0:T(8,128)(2,1)}, u32[]{:S(2)}, u32[]{:S(2)}) collective-permute-start(bf16[384,2048]{1,0:T(8,128)(2,1)} %shard_map.100), channel_id=1, source_target_pairs={{0,1},{2,3},{1,0},{3,2},{4,5},{6,7},{5,4},{7,6},{8,9},{10,11},{9,8... | collective-permute-start | bytes 4718600 | tf_op jit(solution)/shard_map/ppermute | solution.py:497
  97.6 18.7 %collective-permute-start.16 = (bf16[256,2048]{1,0:T(8,128)(2,1)}, bf16[256,2048]{1,0:T(8,128)(2,1)}, u32[]{:S(2)}, u32[]{:S(2)}) collective-permute-start(bf16[256,2048]{1,0:T(8,128)(2,1)} %shard_map.101), channel_id=1, source_target_pairs={{1,2},{2,1},{5,6},{6,5},{9,10},{10,9},{13,14},{14,13},{17,18},{18,... | collective-permute-start | bytes 3145736 | tf_op jit(solution)/shard_map/ppermute | solution.py:497
  104.5 11.9 %collective-permute-start.14 = (bf16[128,2048]{1,0:T(8,128)(2,1)S(1)}, bf16[128,2048]{1,0:T(8,128)(2,1)}, u32[]{:S(2)}, u32[]{:S(2)}) collective-permute-start(bf16[128,2048]{1,0:T(8,128)(2,1)S(1)} %get-tuple-element.47.refs_7_), channel_id=1, source_target_pairs={{0,16},{16,0},{1,17},{17,1},{2,18},{18,2},{3,19},{19,3},{4,20},{20... | collective-permute-start | bytes 1572872 | tf_op jit(solution)/shard_map/ppermute | solution.py:25
  107.3 3.9 %collective-permute-start.18 = (f32[16,512]{1,0:T(8,128)S(1)}, f32[16,512]{1,0:T(8,128)S(1)}, u32[]{:S(2)}, u32[]{:S(2)}) collective-permute-start(f32[16,512]{1,0:T(8,128)S(1)} %add.61.refs_0_), channel_id=1, source_target_pairs={{0,8},{4,12},{8,0},{12,4},{1,9},{5,13},{9,1},{13,5},{2,10},{6,14},... | collective-permute-start | bytes 98312 | tf_op jit(solution)/shard_map/ppermute | solution.py:53
  120.5 63.1 %collective-permute-start.20 = (bf16[256,2048]{1,0:T(8,128)(2,1)}, bf16[256,2048]{1,0:T(8,128)(2,1)}, u32[]{:S(2)}, u32[]{:S(2)}) collective-permute-start(bf16[256,2048]{1,0:T(8,128)(2,1)} %shard_map.105), channel_id=1, source_target_pairs={{0,1},{2,3},{1,0},{3,2},{4,5},{6,7},{5,4},{7,6},{8,9},{10,11},{9,8... | collective-permute-start | bytes 3145736 | tf_op jit(solution)/shard_map/ppermute | solution.py:497
  134.5 49.1 %collective-permute-start.21 = (bf16[256,2048]{1,0:T(8,128)(2,1)}, bf16[256,2048]{1,0:T(8,128)(2,1)}, u32[]{:S(2)}, u32[]{:S(2)}) collective-permute-start(bf16[256,2048]{1,0:T(8,128)(2,1)} %shard_map.106), channel_id=1, source_target_pairs={{1,2},{2,1},{5,6},{6,5},{9,10},{10,9},{13,14},{14,13},{17,18},{18,... | collective-permute-start | bytes 3145736 | tf_op jit(solution)/shard_map/ppermute | solution.py:497
  143.1 5.5 %collective-permute-start.26 = (f32[16,512]{1,0:T(8,128)S(1)}, f32[16,512]{1,0:T(8,128)S(1)}, u32[]{:S(2)}, u32[]{:S(2)}) collective-permute-start(f32[16,512]{1,0:T(8,128)S(1)} %add.67.refs_0_), channel_id=1, source_target_pairs={{0,8},{4,12},{8,0},{12,4},{1,9},{5,13},{9,1},{13,5},{2,10},{6,14},... | collective-permute-start | bytes 98312 | tf_op jit(solution)/shard_map/ppermute | solution.py:53
  144.6 26.2 %collective-permute-start.19 = (bf16[128,2048]{1,0:T(8,128)(2,1)}, bf16[128,2048]{1,0:T(8,128)(2,1)}, u32[]{:S(2)}, u32[]{:S(2)}) collective-permute-start(bf16[128,2048]{1,0:T(8,128)(2,1)} %get-tuple-element.59.refs_9_), channel_id=1, source_target_pairs={{0,16},{16,0},{1,17},{17,1},{2,18},{18,2},{3,19},{19,3},{4,20},{20... | collective-permute-start | bytes 1572872 | tf_op jit(solution)/shard_map/ppermute | solution.py:25
  146.2 7.2 %collective-permute-start.22 = (bf16[256,256]{1,0:T(8,128)(2,1)}, bf16[256,256]{1,0:T(8,128)(2,1)}, u32[]{:S(2)}, u32[]{:S(2)}) collective-permute-start(bf16[256,256]{1,0:T(8,128)(2,1)} %get-tuple-element.53), channel_id=1, source_target_pairs={{0,1},{2,3},{1,0},{3,2},{4,5},{6,7},{5,4},{7,6},{8,9},{10,11},{9,8... | collective-permute-start | bytes 393224 | tf_op jit(solution)/shard_map/ppermute | solution.py:470
  148.7 6.5 %collective-permute-start.23 = (bf16[256,256]{1,0:T(8,128)(2,1)}, bf16[256,256]{1,0:T(8,128)(2,1)}, u32[]{:S(2)}, u32[]{:S(2)}) collective-permute-start(bf16[256,256]{1,0:T(8,128)(2,1)} %get-tuple-element.54), channel_id=1, source_target_pairs={{1,2},{2,1},{5,6},{6,5},{9,10},{10,9},{13,14},{14,13},{17,18},{18,... | collective-permute-start | bytes 393224 | tf_op jit(solution)/shard_map/ppermute | solution.py:470
  153.4 15.7 %collective-permute-start.24 = (bf16[256,256]{1,0:T(8,128)(2,1)}, bf16[256,256]{1,0:T(8,128)(2,1)S(1)}, u32[]{:S(2)}, u32[]{:S(2)}) collective-permute-start(bf16[256,256]{1,0:T(8,128)(2,1)} %copy-done.22), channel_id=1, source_target_pairs={{0,2},{1,3},{2,0},{3,1},{4,6},{5,7},{6,4},{7,5},{8,10},{9,11},{10,... | collective-permute-start | bytes 393224 | tf_op jit(solution)/shard_map/ppermute | solution.py:470
  155.1 14.0 %collective-permute-start.27 = (bf16[256,256]{1,0:T(8,128)(2,1)S(1)}, bf16[256,256]{1,0:T(8,128)(2,1)S(1)}, u32[]{:S(2)}, u32[]{:S(2)}) collective-permute-start(bf16[256,256]{1,0:T(8,128)(2,1)S(1)} %get-tuple-element.64), channel_id=1, source_target_pairs={{0,3},{3,0},{4,7},{7,4},{8,11},{11,8},{12,15},{15,12},{16,19},{19,... | collective-permute-start | bytes 393224 | tf_op jit(solution)/shard_map/ppermute | solution.py:470
  (29 other events, 255.2 us)

commit v4 on v3

v4 whole, which is shorter than its diff:
```python
import functools

import jax
import jax.numpy as jnp
from jax import lax
from jax.experimental import pallas as pl
from jax.experimental.pallas import tpu as pltpu
from jax.sharding import PartitionSpec as P

adapter_scale = 2.0
piece_flops = 1
vmem_bytes = 24 * 1024 * 1024


def dot(a, b, ca, cb):
    return lax.dot_general(a, b, (((ca,), (cb,)), ((), ())), preferred_element_type=jnp.float32)


def narrow(values):
    return values.astype(jnp.bfloat16)


def turns(value, axis):
    count = lax.axis_size(axis)
    return [
        lax.ppermute(value, axis, [(i, (i + step) % count) for i in range(count)])
        for step in range(1, count)
    ]


def after(value, *others):
    return lax.optimization_barrier((value, others))[0]


def halving(value, axis):
    count = lax.axis_size(axis)
    if count & (count - 1):
        return [value] + turns(value, axis)
    step = 1
    while True:
        other = lax.ppermute(value, axis, [(i, i ^ step) for i in range(count)])
        step *= 2
        if step >= count:
            return [value, other]
        value = value + other


def after(value, *others):
    return lax.optimization_barrier((value, others))[0]


def line_pass(below, above, axis, step):
    count = lax.axis_size(axis)
    up = [(i, i + 1) for i in range(step - 1, count - 1)]
    down = [(i + 1, i) for i in range(count - step)]
    return lax.ppermute(below, axis, up), lax.ppermute(above, axis, down)


def pairs(count, odd):
    swaps = [(i, i + 1) for i in range(odd, count - 1, 2)]
    return swaps + [(b, a) for a, b in swaps]


def going_up(place, odd):
    return lax.rem(place, 2) == odd


def arrived(count, place, step, odd):
    return jnp.where(going_up(place, odd), place + step, place - step)


def within(count, block):
    return (block >= 0) & (block < count)


def one_sided(count, step):
    return 2 * step >= count


def only_sums(count, step, odd):
    return step >= count - odd


def only_blocks(step, odd):
    return step <= 1 + odd


def named(slot, block, owned, rank):
    shape = (owned * rank, slot.shape[1])
    return (slot - block * owned) == lax.broadcasted_iota(jnp.int32, shape, 0) // rank


def pick(slot, block, values, owned, rank):
    values = jnp.where(named(slot, block, owned, rank), values, 0.0)
    total = values[:rank]
    for at in range(1, owned):
        total = total + values[at * rank : (at + 1) * rank]
    return total


def spread(slot, block, values, owned, rank):
    values = jnp.concatenate([values.astype(jnp.float32)] * owned, axis=0)
    return narrow(jnp.where(named(slot, block, owned, rank), values, 0.0))


def columns(height, tile, at_tile=0, at_row=0):
    return pl.BlockSpec((height, tile), lambda at: (at_row, at_tile + at))


def tile_of(width):
    return 512 if width % 512 == 0 else width


def full(shape):
    return pl.BlockSpec(shape, lambda *at: (0,) * len(shape))


def call(body, grid, in_specs, out_specs, out_shape, *operands, scratch=(), aliases=None, flops=1):
    return pl.pallas_call(
        body,
        grid=grid,
        in_specs=in_specs,
        out_specs=out_specs,
        out_shape=out_shape,
        scratch_shapes=scratch,
        input_output_aliases=aliases or {},
        compiler_params=pltpu.CompilerParams(vmem_limit_bytes=vmem_bytes),
        cost_estimate=pl.CostEstimate(flops=flops, bytes_accessed=1, transcendentals=0),
    )(*operands)


def back_sum(slot, cotangent, parts, owned, rank):
    count, rows = len(parts), slot.shape[1]

    def body(slot_ref, cot_ref, *refs):
        place = lax.axis_index("dp")
        slots, cots = slot_ref[...], cot_ref[...]
        total = jnp.zeros((rank, rows), jnp.float32)
        for turn in range(count):
            block = lax.rem(place + count - turn, count)
            total = total + pick(slots, block, dot(refs[turn][...], cots, 1, 1), owned, rank)
        refs[count][...] = total

    return call(
        body,
        (1,),
        [full(slot.shape), full(cotangent.shape)] + [full(part.shape) for part in parts],
        full((rank, rows)),
        jax.ShapeDtypeStruct((rank, rows), jnp.float32),
        slot,
        cotangent,
        *parts,
    )


def add_up(parts, last):
    def body(*refs):
        total = refs[0][...]
        for ref in refs[1:-1]:
            total = total + ref[...]
        if last:
            total = narrow(adapter_scale * narrow(total).astype(jnp.float32))
        refs[-1][...] = total

    shape = parts[0].shape
    return call(
        body,
        (1,),
        [full(shape)] * len(parts),
        full(shape),
        jax.ShapeDtypeStruct(shape, jnp.bfloat16 if last else jnp.float32),
        *parts,
    )


def scaled_sum(value, axis):
    count = lax.axis_size(axis)
    if count & (count - 1):
        return add_up([value] + turns(value, axis), True)
    step = 1
    while step < count:
        other = lax.ppermute(value, axis, [(i, i ^ step) for i in range(count)])
        step *= 2
        value = add_up([value, other], step >= count)
    return value


def message(step, count, odd, stream, slot, back, inputs, received, owned, rank):
    rows, width = inputs.shape[0], received.shape[1]
    tile = tile_of(width)
    down_rows = owned * rank
    height = down_rows if only_sums(count, step, odd) else received.shape[0]

    def body(slot_ref, back_ref, in_ref, got_ref, out_ref, factor_ref):
        place = lax.axis_index("dp")
        up = going_up(place, odd)
        along = jnp.where(up, place, count - 1 - place)
        target = along + count - step + 1
        block = jnp.where(up, target, count - 1 - target)

        @pl.when(pl.program_id(0) == 0)
        def prepare():
            factor_ref[...] = spread(slot_ref[...], block, back_ref[...], owned, rank)

        def add():
            value = dot(factor_ref[...], in_ref[...], 1, 0)
            out_ref[:down_rows, :] = narrow(value + got_ref[:down_rows, :].astype(jnp.float32))
            if height > down_rows:
                out_ref[down_rows:, :] = jnp.zeros((height - down_rows, tile), jnp.bfloat16)

        def pass_on():
            out_ref[...] = got_ref[...]

        if height == down_rows:
            add()
        else:
            pl.when(along < step - 1)(add)
            pl.when(along >= step - 1)(pass_on)

    return call(
        body,
        (width // tile,),
        [
            full(slot.shape),
            full(back.shape),
            columns(rows, tile, stream * (width // tile)),
            columns(height, tile),
        ],
        columns(height, tile),
        jax.ShapeDtypeStruct((height, width), jnp.bfloat16),
        slot,
        back,
        inputs,
        received,
        scratch=[pltpu.VMEM((down_rows, rows), jnp.bfloat16)],
    )


def own_sum(stream, slot, back, inputs, received, whole, owned, rank):
    rows, width = inputs.shape[0], received[0].shape[1]
    tile = tile_of(width)
    down_rows = owned * rank
    first = stream * (width // tile)
    given = [] if whole is None else [whole]

    def body(slot_ref, back_ref, in_ref, *refs):
        out_ref, factor_ref = refs[-2:]

        @pl.when(pl.program_id(0) == 0)
        def prepare():
            place = lax.axis_index("dp")
            factor_ref[...] = spread(slot_ref[...], place, back_ref[...], owned, rank)

        value = dot(factor_ref[...], in_ref[...], 1, 0)
        for ref in refs[: len(received)]:
            value = value + ref[...].astype(jnp.float32)
        out_ref[...] = narrow(value)

    return call(
        body,
        (width // tile,),
        [full(slot.shape), full(back.shape), columns(rows, tile, first)]
        + [columns(down_rows, tile)] * len(received)
        + [pl.BlockSpec(memory_space=pl.ANY)] * len(given),
        columns(down_rows, tile, first),
        jax.ShapeDtypeStruct((down_rows, inputs.shape[1]), jnp.bfloat16),
        slot,
        back,
        inputs,
        *received,
        *given,
        scratch=[pltpu.VMEM((down_rows, rows), jnp.bfloat16)],
        aliases={3 + len(received): 0} if given else None,
    )


def use_pieces(step, count, stream, slot, back, inputs, pieces, proj, low, owned, rank):
    rows, width = inputs.shape[0], pieces[0].shape[1]
    tile = tile_of(width)
    down_rows = owned * rank
    total = len(pieces)
    share = pieces[0].shape[0] - down_rows
    merged = one_sided(count, step) and total > 1
    shared = share * (1 if merged else total)
    held = [] if proj is None else [proj], [] if low is None else [low]

    def body(slot_ref, back_ref, in_ref, *refs):
        place = lax.axis_index("dp")
        blocks = [arrived(count, place, step, odd) if step else place for odd in range(total)]
        slots, ins = slot_ref[...], in_ref[...]
        piece_refs, share_refs, refs = refs[:total], refs[total : 2 * total], refs[2 * total :]
        held_refs, (proj_ref, low_ref, share_ref, factor_ref) = refs[:-4], refs[-4:]

        @pl.when(pl.program_id(0) == 0)
        def prepare():
            for at, block in enumerate(blocks):
                factor_ref[at] = spread(slots, block, back_ref[...], owned, rank)

        if merged:
            came = within(count, blocks[0])
            share_ref[...] = jnp.where(came, share_refs[0][...], share_refs[1][...])
        else:
            for at, ref in enumerate(share_refs):
                share_ref[at * share : (at + 1) * share, :] = ref[...]
        sums, lows = None, None
        for at, block in enumerate(blocks):
            value = piece_refs[at][...]
            term = pick(slots, block, dot(value, ins, 1, 1), owned, rank)
            sums = term if sums is None else sums + term
            term = narrow(dot(factor_ref[at], value, 0, 0))
            lows = term if lows is None else lows + term
        low_ref[...] = lows + held_refs[-1][...] if held[1] else lows

        @pl.when(pl.program_id(0) == 0)
        def first():
            proj_ref[...] = sums + held_refs[0][...] if held[0] else sums

        @pl.when(pl.program_id(0) > 0)
        def later():
            proj_ref[...] = proj_ref[...] + sums

    return call(
        body,
        (width // tile,),
        [full(slot.shape), full(back.shape), columns(rows, tile, stream * (width // tile))]
        + [columns(down_rows, tile)] * total
        + [columns(share, tile, 0, down_rows // share)] * total
        + [full((rank, rows))] * len(held[0])
        + [columns(rows, tile)] * len(held[1]),
        [full((rank, rows)), columns(rows, tile), columns(shared, tile)],
        [
            jax.ShapeDtypeStruct((rank, rows), jnp.float32),
            jax.ShapeDtypeStruct((rows, width), jnp.bfloat16),
            jax.ShapeDtypeStruct((shared, width), jnp.bfloat16),
        ],
        slot,
        back,
        inputs,
        *pieces,
        *pieces,
        *held[0],
        *held[1],
        scratch=[pltpu.VMEM((total, down_rows, rows), jnp.bfloat16)],
        flops=piece_flops if step else 1,
    )


def up_parts(targets, slot, proj, cotangent, owned, rank):
    keys = cotangent.shape[1]

    def body(slot_ref, proj_ref, cot_ref, *outs):
        place = lax.axis_index("dp")
        slots, projs, cots = slot_ref[...], proj_ref[...], cot_ref[...]
        for target, out in zip(targets, outs):
            out[...] = narrow(dot(spread(slots, target(place), projs, owned, rank), cots, 1, 0))

    shape = (owned * rank, keys)
    return call(
        body,
        (1,),
        [full(slot.shape), full(proj.shape), full(cotangent.shape)],
        [full(shape)] * len(targets),
        [jax.ShapeDtypeStruct(shape, jnp.bfloat16)] * len(targets),
        slot,
        proj,
        cotangent,
    )


def pack(down_own, weight):
    down_rows, width = down_own.shape
    keys = weight.shape[1]
    half = weight.shape[0] // lax.axis_size("groups")
    streams = width // keys
    chunk = half // streams

    def body(down_ref, weight_ref, *outs):
        group = lax.axis_index("groups")
        for at, out in enumerate(outs):
            rows = pl.ds(pl.multiple_of(group * half + at * chunk, chunk), chunk)
            out[:down_rows, :] = down_ref[:, at * keys : (at + 1) * keys]
            out[down_rows:, :] = weight_ref[rows, :]

    shape = (down_rows + chunk, keys)
    return call(
        body,
        (1,),
        [full(down_own.shape), full(weight.shape)],
        [full(shape)] * streams,
        [jax.ShapeDtypeStruct(shape, jnp.bfloat16)] * streams,
        down_own,
        weight,
    )


def finish(cotangents, weight_own, described, pieces, lows):
    rows, stream_width = lows[0].shape
    streams = len(lows)
    weight_rows, keys = weight_own.shape
    shard = cotangents[0].shape[1]
    count, groups, parts = lax.axis_size("dp"), lax.axis_size("groups"), len(cotangents)
    half = weight_rows // groups
    chunk = half // streams
    some = max(1, 512 // weight_rows)
    tile = some * weight_rows
    tiles = stream_width // tile

    def body(*refs):
        cot_refs, own_ref, refs = refs[:parts], refs[parts], refs[parts + 1 :]
        piece_refs, low_refs = refs[: len(pieces)], refs[len(pieces) : -3]
        out_ref, dy_ref, weight_ref = refs[-3:]
        now = pl.program_id(0)

        @pl.when(now == 0)
        def arrange():
            place, group, part = (lax.axis_index(axis) for axis in ("dp", "groups", "fsdp"))
            for turn, ref in enumerate(cot_refs):
                at = lax.rem(part + parts - turn, parts) * shard
                dy_ref[:, pl.ds(pl.multiple_of(at, shard), shard)] = ref[...]
            weight_ref[place] = own_ref[...]
            for at, ref in enumerate(piece_refs):
                owner = lax.rem(group + groups - at % groups, groups)
                for first, (step, stream, odds) in enumerate(described[at // groups]):
                    for odd in odds:
                        block = arrived(count, place, step, odd)

                        def store(first=first * chunk, stream=stream, block=block):
                            row = pl.multiple_of(owner * half + stream * chunk, chunk)
                            weight_ref[block, pl.ds(row, chunk), :] = ref[first : first + chunk, :]

                        pl.when(within(count, block))(store)

        def add(low_ref):
            for block in range(some):
                at = slice(block * weight_rows, (block + 1) * weight_rows)
                base = dot(dy_ref[...], weight_ref[now * some + block], 1, 1)
                out_ref[:, at] = narrow(base + low_ref[:, at].astype(jnp.float32))

        for stream, low_ref in enumerate(low_refs):
            pl.when(now // tiles == stream)(functools.partial(add, low_ref))

    def low_spec(stream):
        return pl.BlockSpec((rows, tile), lambda at: (0, jnp.clip(at - stream * tiles, 0, tiles - 1)))

    fixed = [*cotangents, weight_own, *pieces]
    return call(
        body,
        (streams * tiles,),
        [full(array.shape) for array in fixed] + [low_spec(stream) for stream in range(streams)],
        columns(rows, tile),
        jax.ShapeDtypeStruct((rows, streams * stream_width), jnp.bfloat16),
        *fixed,
        *lows,
        scratch=[
            pltpu.VMEM((rows, keys), jnp.bfloat16),
            pltpu.VMEM((count, weight_rows, keys), jnp.bfloat16),
        ],
    )


def shards(
    inputs,
    cotangent,
    frozen_key_weight,
    adapter_down_weight,
    adapter_up_weight,
    row_adapter_index,
    adapter_slot_index,
):
    tok_rows, feat_width = inputs.shape
    key_shard = cotangent.shape[1]
    owned, rank, _ = adapter_down_weight.shape
    slots = adapter_slot_index.shape[0]
    data_count, place = lax.axis_size("dp"), lax.axis_index("dp")
    down_rows = owned * rank
    key_at = lax.axis_index("fsdp") * key_shard

    up_own = lax.dynamic_slice_in_dim(adapter_up_weight, key_at, key_shard, 2)
    up_own = up_own.reshape(down_rows, key_shard)
    ups = [up_own] + turns(up_own, "dp")
    down_own = adapter_down_weight.reshape(down_rows, feat_width)
    packed = pack(down_own, frozen_key_weight)

    ids = row_adapter_index[:, 0]
    every = lax.broadcasted_iota(jnp.int32, (slots, tok_rows), 0)
    slot = jnp.sum(jnp.where(ids[None, :] == every, adapter_slot_index[:, None], 0), axis=0)
    slot = slot[None, :]

    def up_swaps(proj):
        targets, routes = [lambda place: place], []
        for step in range(1, data_count):
            for odd in (0, 1):
                ends = [i for i in range(data_count - step) if i // step % 2 == odd]
                if ends:
                    swaps = [(i, i + step) for i in ends] + [(i + step, i) for i in ends]
                    routes.append(swaps)
                    targets.append(
                        lambda place, step=step, odd=odd: jnp.where(
                            lax.rem(lax.div(place, step), 2) == odd, place + step, place - step
                        )
                    )
        parts = up_parts(targets, slot, proj, cotangent, owned, rank)
        got = [lax.ppermute(part, "dp", swaps) for part, swaps in zip(parts[1:], routes)]
        return [parts[0]] + got

    streams = range(len(packed))
    received = [[one, one] for one in after(packed, ups)]
    got, lows = [[one] for one in packed], [None for _ in streams]
    proj, back, exchanged = None, None, []
    cotangents = [cotangent] + turns(after(cotangent, ups), "fsdp")
    last = [cotangents]
    waited = {step: [] for step in range(data_count + 3)}
    for step in range(1, data_count + 1):
        if step == 2:
            back = back_sum(slot, cotangent, after(ups, received[0], last), owned, rank)
            back = scaled_sum(back, "fsdp")
        for stream in streams:
            sent = []
            for odd, other in enumerate(reversed(received[stream])):
                if step > 1:
                    other = after(other, last, waited[step] if stream == streams[-1] else [])
                if not only_blocks(step, odd):
                    other = message(
                        step, data_count, odd, stream, slot, back, inputs, other, owned, rank
                    )
                sent.append(other)
            received[stream] = [
                lax.ppermute(sent[odd], "dp", pairs(data_count, odd)) for odd in (0, 1)
            ]
            if step == 1:
                continue
            pieces = after(got[stream], sent)
            if step == 2:
                proj, lows[stream], _ = use_pieces(
                    0, data_count, stream, slot, back, inputs, [packed[stream]], proj, None,
                    owned, rank,
                )
            proj, lows[stream], share = use_pieces(
                step - 1, data_count, stream, slot, back, inputs, pieces, proj, lows[stream],
                owned, rank,
            )
            last = [proj, lows[stream]]
            share = [share] + turns(share, "groups")
            waited[step + 1].append(share)
            if one_sided(data_count, step - 1):
                described = [(step - 1, stream, odds)]
            else:
                described = [(step - 1, stream, [odd]) for odd in odds]
            exchanged.append((described, share))
        odds = [odd for odd in (0, 1) if not only_sums(data_count, step, odd)]
        got = [[received[stream][odd] for odd in odds] for stream in streams]

    order = [entry for entry, _ in exchanged]
    parts = sum([share for _, share in exchanged], [])
    input_grad = finish(cotangents, frozen_key_weight, order, parts, lows)
    down_grad = None
    for stream in streams:
        if stream == streams[-1]:
            received[stream] = after(received[stream], input_grad)
        down_grad = own_sum(
            stream, slot, back, inputs, received[stream], down_grad, owned, rank
        )
        if stream == 0:
            proj = scaled_sum(after(proj, down_grad), "fsdp")
            up_grads = up_swaps(proj)
    up_grads = after(up_grads, input_grad)
    up_grad = sum(part.astype(jnp.float32) for part in up_grads)
    return (
        input_grad,
        down_grad.reshape(owned, rank, feat_width),
        narrow(up_grad).reshape(owned, rank, key_shard),
    )


def solution(mesh):
    placed = (
        P(("groups", "dp"), "fsdp"),
        P(("groups", "dp"), "fsdp"),
        P(("fsdp", "dp"), None),
        P(("groups", "dp"), None, "fsdp"),
        P(("groups", "dp"), None, None),
        P(("groups", "dp"), None),
        P("groups"),
    )
    return jax.shard_map(
        shards,
        mesh=mesh,
        in_specs=placed,
        out_specs=(
            P(("groups", "dp"), "fsdp"),
            P(("groups", "dp"), None, "fsdp"),
            P(("groups", "dp"), None, "fsdp"),
        ),
        check_vma=False,
    )
```

time: 189 us -> 160 us (0.85)
  waiting for transfers between devices: 76.3 us -> 51.4 us
  starting transfers between devices: 50.3 us -> 69.7 us
  local copies, waits for them, and re-layouts: 14.4 us -> 3.51 us
  Pallas kernels: 43.8 us -> 33.2 us
    ppermute x12, waiting for transfers between devices: 41.2 us -> 16.4 us  [turns(): lax.ppermute(value, axis, [(i, (i + step) % count) for i in range(count)])]
    ppermute x8 -> x16, starting transfers between devices: 20.3 us -> 41.8 us  [shards(): lax.ppermute(sent[odd], 'dp', pairs(data_count, odd))]
    unnamed x50 -> x16, local copies, waits for them, and re-layouts: 14.4 us -> 3.49 us
    ppermute x8, waiting for transfers between devices: 16.2 us -> 7.69 us  [the longest x4 7.24 us: scaled_sum(): other = lax.ppermute(value, axis, [(i, i ^ step) for i in range(count)])]
    ppermute x8 -> x16, waiting for transfers between devices: 18.9 us -> 27.3 us  [shards(): lax.ppermute(sent[odd], 'dp', pairs(data_count, odd))]
    pallas_call x1 -> x0, Pallas kernels: 5.8 us -> none  [finish(): pl.pallas_call(body, grid=(width // tile,), in_specs=[full(array.shape) f...]
    pallas_call x17 -> x28, Pallas kernels: 38 us -> 33.2 us  [call(): pl.pallas_call(body, grid=grid, in_specs=in_specs, out_specs=out_specs, o...]
  transfers between devices with their start and end apart: 28 -> 36, of which waited for: 16 -> 15; matrix products, arithmetic and copies ran while one was open for 1% -> 0% of each run, Pallas kernels for 21% -> 21%
where the time goes in v4:
time: 160 us
  starting transfers between devices  69.7 us (44%)
  waiting for transfers between devices  51.4 us (32%)
  Pallas kernels  33.2 us (21%)
  local copies, waits for them, and re-layouts  3.51 us (2%)
    ppermute x16, starting transfers between devices, shards(): lax.ppermute(sent[odd], 'dp', pairs(data_count, odd))  41.8 us
    pallas_call x28, Pallas kernels, call(): pl.pallas_call(body, grid=grid, in_specs=in_specs, out_specs=out_specs, o...  33.2 us
    ppermute x16, waiting for transfers between devices, shards(): lax.ppermute(sent[odd], 'dp', pairs(data_count, odd))  27.3 us
    ppermute x12, waiting for transfers between devices, turns(): lax.ppermute(value, axis, [(i, (i + step) % count) for i in range(count)])  16.4 us
    ppermute x12, starting transfers between devices, turns(): lax.ppermute(value, axis, [(i, (i + step) % count) for i in range(count)])  15.3 us
    ppermute x4, starting transfers between devices, up_swaps(): lax.ppermute(part, 'dp', swaps)  9.51 us
    ppermute x4, waiting for transfers between devices, scaled_sum(): other = lax.ppermute(value, axis, [(i, i ^ step) for i in range(count)])  7.24 us
    unnamed x16, local copies, waits for them, and re-layouts  3.49 us
  transfers between devices with their start and end apart: 36, of which 15 were waited for; matrix products, arithmetic and copies ran while one was open for 0% of the time, Pallas kernels for 21%

profile of v4, /device:TPU:0, one launch (start us, length us, event | category | flops | bytes accessed | tf_op | source)
XLA Modules:
  0.0 159.8 jit_solution(9907267197254683558)
XLA Ops:
  1.7 5.1 %collective-permute-start.2 = (bf16[256,256]{1,0:T(8,128)(2,1)S(1)}, bf16[256,256]{1,0:T(8,128)(2,1)S(1)}, u32[]{:S(2)}, u32[]{:S(2)}) collective-permute-start(bf16[256,256]{1,0:T(8,128)(2,1)S(1)} %bitcast.29), channel_id=1, source_target_pairs={{0,3},{1,0},{2,1},{3,2},{4,7},{5,4},{6,5},{7,6},{8,11},{9,8},{10,9... | collective-permute-start | bytes 393224 | tf_op jit(solution)/shard_map/ppermute | solution.py:26
  10.7 7.3 %collective-permute-done.1.refs_2_ = bf16[256,256]{1,0:T(8,128)(2,1)S(1)} collective-permute-done((bf16[256,256]{1,0:T(8,128)(2,1)S(1)}, bf16[256,256]{1,0:T(8,128)(2,1)S(1)}, u32[]{:S(2)}, u32[]{:S(2)}) %collective-permute-start.1) | collective-permute-done | bytes 131104 | tf_op jit(solution)/shard_map/ppermute | solution.py:26
  21.2 4.0 %collective-permute-done.5.refs_3_ = bf16[512,256]{1,0:T(8,128)(2,1)S(1)} collective-permute-done((bf16[512,256]{1,0:T(8,128)(2,1)S(1)}, bf16[512,256]{1,0:T(8,128)(2,1)S(1)}, u32[]{:S(2)}, u32[]{:S(2)}) %collective-permute-start.5) | collective-permute-done | bytes 262176 | tf_op jit(solution)/shard_map/ppermute | solution.py:26
  25.2 3.7 %collective-permute-start.11 = (bf16[384,1024]{1,0:T(8,128)(2,1)S(1)}, bf16[384,1024]{1,0:T(8,128)(2,1)S(1)}, u32[]{:S(2)}, u32[]{:S(2)}) collective-permute-start(bf16[384,1024]{1,0:T(8,128)(2,1)S(1)} %get-tuple-element.84.refs_0_.refs_1_), channel_id=1, source_target_pairs={{0,1},{2,3},{1,0},{3,2},{4,5},{6,7},{5,4},{7,6},{8,9},{10,11},{9,8... | collective-permute-start | bytes 2359304 | tf_op jit(solution)/shard_map/ppermute | solution.py:528
  28.9 4.7 %collective-permute-done.4.refs_2_ = bf16[512,256]{1,0:T(8,128)(2,1)S(1)} collective-permute-done((bf16[512,256]{1,0:T(8,128)(2,1)S(1)}, bf16[512,256]{1,0:T(8,128)(2,1)S(1)}, u32[]{:S(2)}, u32[]{:S(2)}) %collective-permute-start.4) | collective-permute-done | bytes 262176 | tf_op jit(solution)/shard_map/ppermute | solution.py:26
  34.4 4.1 %collective-permute-done.6.refs_0_.refs_2_ = bf16[384,1024]{1,0:T(8,128)(2,1)S(1)} collective-permute-done((bf16[384,1024]{1,0:T(8,128)(2,1)S(1)}, bf16[384,1024]{1,0:T(8,128)(2,1)S(1)}, u32[]{:S(2)}, u32[]{:S(2)}) %collective-permute-start.6) | collective-permute-done | bytes 786464 | tf_op jit(solution)/shard_map/ppermute | solution.py:528
  42.6 2.4 %collective-permute-done.9.refs_1_ = f32[16,512]{1,0:T(8,128)S(1)} collective-permute-done((f32[16,512]{1,0:T(8,128)S(1)}, f32[16,512]{1,0:T(8,128)S(1)}, u32[]{:S(2)}, u32[]{:S(2)}) %collective-permute-start.9) | collective-permute-done | bytes 32800 | tf_op jit(solution)/shard_map/ppermute | solution.py:182
  46.0 3.9 %collective-permute-start.14 = (bf16[384,1024]{1,0:T(8,128)(2,1)S(1)}, bf16[384,1024]{1,0:T(8,128)(2,1)S(1)}, u32[]{:S(2)}, u32[]{:S(2)}) collective-permute-start(bf16[384,1024]{1,0:T(8,128)(2,1)S(1)} %shard_map.98), channel_id=1, source_target_pairs={{0,1},{2,3},{1,0},{3,2},{4,5},{6,7},{5,4},{7,6},{8,9},{10,11},{9,8... | collective-permute-start | bytes 2359304 | tf_op jit(solution)/shard_map/ppermute | solution.py:528
  51.9 2.1 %shard_map.100 = (f32[16,512]{1,0:T(8,128)S(1)}, bf16[512,1024]{1,0:T(8,128)(2,1)S(1)}, bf16[256,1024]{1,0:T(8,128)(2,1)S(1)}) custom-call(s32[1,512]{1,0:T(1,128)S(1)} %bitcast.9, bf16[16,512]{1,0:T(8,128)(2,1)S(1)} %shard_map.97.back_ref, bf16[512,2048]{1,0:T(8,128)(2,1)S(1)} %copy-done.1, bf16[384,1024]{1,0:T(8,128)(2,1)S(1)} %collective-permute-done.6.refs_0_.refs_2_, ...), custom_call_target="tpu_custom_call" | custom-call | flops 1 | bytes 1 | tf_op jit(solution)/shard_map/pallas_call | solution.py:119
  58.6 3.9 %collective-permute-start.17 = (bf16[384,1024]{1,0:T(8,128)(2,1)S(1)}, bf16[384,1024]{1,0:T(8,128)(2,1)S(1)}, u32[]{:S(2)}, u32[]{:S(2)}) collective-permute-start(bf16[384,1024]{1,0:T(8,128)(2,1)S(1)} %shard_map.101), channel_id=1, source_target_pairs={{0,1},{2,3},{1,0},{3,2},{4,5},{6,7},{5,4},{7,6},{8,9},{10,11},{9,8... | collective-permute-start | bytes 2359304 | tf_op jit(solution)/shard_map/ppermute | solution.py:528
  64.5 2.1 %shard_map.103 = (f32[16,512]{1,0:T(8,128)S(1)}, bf16[512,1024]{1,0:T(8,128)(2,1)S(1)}, bf16[256,1024]{1,0:T(8,128)(2,1)S(1)}) custom-call(s32[1,512]{1,0:T(1,128)S(1)} %bitcast.12, bf16[16,512]{1,0:T(8,128)(2,1)S(1)} %shard_map.97.back_ref, bf16[512,2048]{1,0:T(8,128)(2,1)S(1)} %copy-done.1, bf16[384,1024]{1,0:T(8,128)(2,1)S(1)} %collective-permute-done.11.refs_0_.refs_2_, ...), custom_call_target="tpu_custom_call" | custom-call | flops 1 | bytes 1 | tf_op jit(solution)/shard_map/pallas_call | solution.py:119
  68.1 4.0 %collective-permute-done.14.got_ref.refs_0_.refs_2_ = bf16[384,1024]{1,0:T(8,128)(2,1)S(1)} collective-permute-done((bf16[384,1024]{1,0:T(8,128)(2,1)S(1)}, bf16[384,1024]{1,0:T(8,128)(2,1)S(1)}, u32[]{:S(2)}, u32[]{:S(2)}) %collective-permute-start.14) | collective-permute-done | bytes 786464 | tf_op jit(solution)/shard_map/ppermute | solution.py:528
  72.2 6.4 %collective-permute-start.20 = (bf16[384,1024]{1,0:T(8,128)(2,1)S(1)}, bf16[384,1024]{1,0:T(8,128)(2,1)S(1)}, u32[]{:S(2)}, u32[]{:S(2)}) collective-permute-start(bf16[384,1024]{1,0:T(8,128)(2,1)S(1)} %shard_map.104), channel_id=1, source_target_pairs={{0,1},{2,3},{1,0},{3,2},{4,5},{6,7},{5,4},{7,6},{8,9},{10,11},{9,8... | collective-permute-start | bytes 2359304 | tf_op jit(solution)/shard_map/ppermute | solution.py:528
  80.1 2.1 %shard_map.106 = (f32[16,512]{1,0:T(8,128)S(1)}, bf16[512,1024]{1,0:T(8,128)(2,1)S(1)}, bf16[128,1024]{1,0:T(8,128)(2,1)S(1)}) custom-call(s32[1,512]{1,0:T(1,128)S(1)} %bitcast.15, bf16[16,512]{1,0:T(8,128)(2,1)S(1)} %shard_map.97.back_ref, bf16[512,2048]{1,0:T(8,128)(2,1)S(1)} %copy-done.1, ...), custom_call_target="tpu_custom_call" | custom-call | flops 1 | bytes 1 | tf_op jit(solution)/shard_map/pallas_call | solution.py:119
  83.2 10.7 %collective-permute-start.23 = (bf16[384,1024]{1,0:T(8,128)(2,1)S(1)}, bf16[384,1024]{1,0:T(8,128)(2,1)S(1)}, u32[]{:S(2)}, u32[]{:S(2)}) collective-permute-start(bf16[384,1024]{1,0:T(8,128)(2,1)S(1)} %shard_map.107), channel_id=1, source_target_pairs={{0,1},{2,3},{1,0},{3,2},{4,5},{6,7},{5,4},{7,6},{8,9},{10,11},{9,8... | collective-permute-start | bytes 2359304 | tf_op jit(solution)/shard_map/ppermute | solution.py:528
  97.0 2.1 %shard_map.109 = (f32[16,512]{1,0:T(8,128)S(1)}, bf16[512,1024]{1,0:T(8,128)(2,1)S(1)}, bf16[128,1024]{1,0:T(8,128)(2,1)S(1)}) custom-call(s32[1,512]{1,0:T(1,128)S(1)} %bitcast.18, bf16[16,512]{1,0:T(8,128)(2,1)S(1)} %shard_map.97.back_ref, bf16[512,2048]{1,0:T(8,128)(2,1)S(1)} %copy-done.1, ...), custom_call_target="tpu_custom_call" | custom-call | flops 1 | bytes 1 | tf_op jit(solution)/shard_map/pallas_call | solution.py:119
  100.6 5.3 %collective-permute-done.20.got_ref.refs_0_.refs_1_ = bf16[384,1024]{1,0:T(8,128)(2,1)S(1)} collective-permute-done((bf16[384,1024]{1,0:T(8,128)(2,1)S(1)}, bf16[384,1024]{1,0:T(8,128)(2,1)S(1)}, u32[]{:S(2)}, u32[]{:S(2)}) %collective-permute-start.20) | collective-permute-done | bytes 786464 | tf_op jit(solution)/shard_map/ppermute | solution.py:528
  111.2 5.6 %collective-permute-start.26 = (bf16[256,1024]{1,0:T(8,128)(2,1)S(1)}, bf16[256,1024]{1,0:T(8,128)(2,1)S(1)}, u32[]{:S(2)}, u32[]{:S(2)}) collective-permute-start(bf16[256,1024]{1,0:T(8,128)(2,1)S(1)} %shard_map.113), channel_id=1, source_target_pairs={{0,1},{2,3},{1,0},{3,2},{4,5},{6,7},{5,4},{7,6},{8,9},{10,11},{9,8... | collective-permute-start | bytes 1572872 | tf_op jit(solution)/shard_map/ppermute | solution.py:528
  116.8 5.9 %collective-permute-done.23.got_ref.refs_0_.refs_1_ = bf16[384,1024]{1,0:T(8,128)(2,1)S(1)} collective-permute-done((bf16[384,1024]{1,0:T(8,128)(2,1)S(1)}, bf16[384,1024]{1,0:T(8,128)(2,1)S(1)}, u32[]{:S(2)}, u32[]{:S(2)}) %collective-permute-start.23) | collective-permute-done | bytes 786464 | tf_op jit(solution)/shard_map/ppermute | solution.py:528
  127.4 6.6 %collective-permute-done.28.refs_0_ = bf16[256,1024]{1,0:T(8,128)(2,1)S(1)} collective-permute-done((bf16[256,1024]{1,0:T(8,128)(2,1)S(1)}, bf16[256,1024]{1,0:T(8,128)(2,1)S(1)}, u32[]{:S(2)}, u32[]{:S(2)}) %collective-permute-start.28) | collective-permute-done | bytes 524320 | tf_op jit(solution)/shard_map/ppermute | solution.py:528
  139.8 2.4 %collective-permute-done.31.refs_1_ = f32[16,512]{1,0:T(8,128)S(1)} collective-permute-done((f32[16,512]{1,0:T(8,128)S(1)}, f32[16,512]{1,0:T(8,128)S(1)}, u32[]{:S(2)}, u32[]{:S(2)}) %collective-permute-start.31) | collective-permute-done | bytes 32800 | tf_op jit(solution)/shard_map/ppermute | solution.py:182
  144.2 4.1 %collective-permute-start.34 = (bf16[256,256]{1,0:T(8,128)(2,1)S(1)}, bf16[256,256]{1,0:T(8,128)(2,1)S(1)}, u32[]{:S(2)}, u32[]{:S(2)}) collective-permute-start(bf16[256,256]{1,0:T(8,128)(2,1)S(1)} %get-tuple-element.128), channel_id=1, source_target_pairs={{0,2},{1,3},{2,0},{3,1},{4,6},{5,7},{6,4},{7,5},{8,10},{9,11},{10,... | collective-permute-start | bytes 393224 | tf_op jit(solution)/shard_map/ppermute | solution.py:503
  148.3 4.0 %collective-permute-start.35 = (bf16[256,256]{1,0:T(8,128)(2,1)S(1)}, bf16[256,256]{1,0:T(8,128)(2,1)S(1)}, u32[]{:S(2)}, u32[]{:S(2)}) collective-permute-start(bf16[256,256]{1,0:T(8,128)(2,1)S(1)} %get-tuple-element.129), channel_id=1, source_target_pairs={{0,3},{3,0},{4,7},{7,4},{8,11},{11,8},{12,15},{15,12},{16,19},{19,... | collective-permute-start | bytes 393224 | tf_op jit(solution)/shard_map/ppermute | solution.py:503
  152.3 4.7 %shard_map.116 = bf16[512,2048]{1,0:T(8,128)(2,1)} custom-call(bf16[512,256]{1,0:T(8,128)(2,1)S(1)} %copy-done.4, bf16[512,256]{1,0:T(8,128)(2,1)S(1)} %collective-permute-done.3.refs_1_, bf16[512,256]{1,0:T(8,128)(2,1)S(1)} %collective-permute-done.4.refs_2_, bf16[512,256]{1,0:T(8,128)(2,1)S(1)} %collective-permute-done.5.refs_3_, ...), custom_call_target="tpu_custom_call" | custom-call | flops 1 | bytes 1 | tf_op jit(solution)/shard_map/pallas_call | solution.py:119
  (95 shorter events, 51.4 us)
Async XLA Ops:
  18.0 20.5 %collective-permute-start.6 = (bf16[384,1024]{1,0:T(8,128)(2,1)S(1)}, bf16[384,1024]{1,0:T(8,128)(2,1)S(1)}, u32[]{:S(2)}, u32[]{:S(2)}) collective-permute-start(bf16[384,1024]{1,0:T(8,128)(2,1)S(1)} %get-tuple-element.72.refs_0_.refs_1_), channel_id=1, source_target_pairs={{0,1},{2,3},{1,0},{3,2},{4,5},{6,7},{5,4},{7,6},{8,9},{10,11},{9,8... | collective-permute-start | bytes 2359304 | tf_op jit(solution)/shard_map/ppermute | solution.py:528
  18.7 20.6 %collective-permute-start.7 = (bf16[384,1024]{1,0:T(8,128)(2,1)S(1)}, bf16[384,1024]{1,0:T(8,128)(2,1)S(1)}, u32[]{:S(2)}, u32[]{:S(2)}) collective-permute-start(bf16[384,1024]{1,0:T(8,128)(2,1)S(1)} %get-tuple-element.72.refs_0_.refs_1_), channel_id=1, source_target_pairs={{1,2},{2,1},{5,6},{6,5},{9,10},{10,9},{13,14},{14,13},{17,18},{18,... | collective-permute-start | bytes 2359304 | tf_op jit(solution)/shard_map/ppermute | solution.py:528
  19.5 14.1 %collective-permute-start.4 = (bf16[512,256]{1,0:T(8,128)(2,1)S(1)}, bf16[512,256]{1,0:T(8,128)(2,1)S(1)}, u32[]{:S(2)}, u32[]{:S(2)}) collective-permute-start(bf16[512,256]{1,0:T(8,128)(2,1)S(1)} %copy-done.4), channel_id=1, source_target_pairs={{0,8},{4,12},{8,0},{12,4},{1,9},{5,13},{9,1},{13,5},{2,10},{6,14},... | collective-permute-start | bytes 786440 | tf_op jit(solution)/shard_map/ppermute | solution.py:26
  21.1 13.3 %collective-permute-start.3 = (bf16[512,256]{1,0:T(8,128)(2,1)S(1)}, bf16[512,256]{1,0:T(8,128)(2,1)S(1)}, u32[]{:S(2)}, u32[]{:S(2)}) collective-permute-start(bf16[512,256]{1,0:T(8,128)(2,1)S(1)} %copy-done.4), channel_id=1, source_target_pairs={{0,4},{4,8},{8,12},{12,0},{1,5},{5,9},{9,13},{13,1},{2,6},{6,10},{... | collective-permute-start | bytes 786440 | tf_op jit(solution)/shard_map/ppermute | solution.py:26
  25.2 30.1 %collective-permute-start.11 = (bf16[384,1024]{1,0:T(8,128)(2,1)S(1)}, bf16[384,1024]{1,0:T(8,128)(2,1)S(1)}, u32[]{:S(2)}, u32[]{:S(2)}) collective-permute-start(bf16[384,1024]{1,0:T(8,128)(2,1)S(1)} %get-tuple-element.84.refs_0_.refs_1_), channel_id=1, source_target_pairs={{0,1},{2,3},{1,0},{3,2},{4,5},{6,7},{5,4},{7,6},{8,9},{10,11},{9,8... | collective-permute-start | bytes 2359304 | tf_op jit(solution)/shard_map/ppermute | solution.py:528
  33.7 24.0 %collective-permute-start.12 = (bf16[384,1024]{1,0:T(8,128)(2,1)S(1)}, bf16[384,1024]{1,0:T(8,128)(2,1)S(1)}, u32[]{:S(2)}, u32[]{:S(2)}) collective-permute-start(bf16[384,1024]{1,0:T(8,128)(2,1)S(1)} %get-tuple-element.84.refs_0_.refs_1_), channel_id=1, source_target_pairs={{1,2},{2,1},{5,6},{6,5},{9,10},{10,9},{13,14},{14,13},{17,18},{18,... | collective-permute-start | bytes 2359304 | tf_op jit(solution)/shard_map/ppermute | solution.py:528
  38.5 28.1 %collective-permute-start.15 = (bf16[384,1024]{1,0:T(8,128)(2,1)S(1)}, bf16[384,1024]{1,0:T(8,128)(2,1)S(1)}, u32[]{:S(2)}, u32[]{:S(2)}) collective-permute-start(bf16[384,1024]{1,0:T(8,128)(2,1)S(1)} %collective-permute-done.6.refs_0_.refs_2_), channel_id=1, source_target_pairs={{1,2},{2,1},{5,6},{6,5},{9,10},{10,9},{13,14},{14,13},{17,18},{18,... | collective-permute-start | bytes 2359304 | tf_op jit(solution)/shard_map/ppermute | solution.py:528
  46.0 26.2 %collective-permute-start.14 = (bf16[384,1024]{1,0:T(8,128)(2,1)S(1)}, bf16[384,1024]{1,0:T(8,128)(2,1)S(1)}, u32[]{:S(2)}, u32[]{:S(2)}) collective-permute-start(bf16[384,1024]{1,0:T(8,128)(2,1)S(1)} %shard_map.98), channel_id=1, source_target_pairs={{0,1},{2,3},{1,0},{3,2},{4,5},{6,7},{5,4},{7,6},{8,9},{10,11},{9,8... | collective-permute-start | bytes 2359304 | tf_op jit(solution)/shard_map/ppermute | solution.py:528
  55.3 26.9 %collective-permute-start.18 = (bf16[384,1024]{1,0:T(8,128)(2,1)S(1)}, bf16[384,1024]{1,0:T(8,128)(2,1)S(1)}, u32[]{:S(2)}, u32[]{:S(2)}) collective-permute-start(bf16[384,1024]{1,0:T(8,128)(2,1)S(1)} %collective-permute-done.11.refs_0_.refs_2_), channel_id=1, source_target_pairs={{1,2},{2,1},{5,6},{6,5},{9,10},{10,9},{13,14},{14,13},{17,18},{18,... | collective-permute-start | bytes 2359304 | tf_op jit(solution)/shard_map/ppermute | solution.py:528
  56.0 23.4 %collective-permute-start.10 = (bf16[256,1024]{1,0:T(8,128)(2,1)S(1)}, bf16[256,1024]{1,0:T(8,128)(2,1)S(1)}, u32[]{:S(2)}, u32[]{:S(2)}) collective-permute-start(bf16[256,1024]{1,0:T(8,128)(2,1)S(1)} %get-tuple-element.83.refs_5_), channel_id=1, source_target_pairs={{0,16},{16,0},{1,17},{17,1},{2,18},{18,2},{3,19},{19,3},{4,20},{20... | collective-permute-start | bytes 1572872 | tf_op jit(solution)/shard_map/ppermute | solution.py:26
  58.6 35.3 %collective-permute-start.17 = (bf16[384,1024]{1,0:T(8,128)(2,1)S(1)}, bf16[384,1024]{1,0:T(8,128)(2,1)S(1)}, u32[]{:S(2)}, u32[]{:S(2)}) collective-permute-start(bf16[384,1024]{1,0:T(8,128)(2,1)S(1)} %shard_map.101), channel_id=1, source_target_pairs={{0,1},{2,3},{1,0},{3,2},{4,5},{6,7},{5,4},{7,6},{8,9},{10,11},{9,8... | collective-permute-start | bytes 2359304 | tf_op jit(solution)/shard_map/ppermute | solution.py:528
  66.6 15.6 %collective-permute-start.13 = (bf16[256,1024]{1,0:T(8,128)(2,1)S(1)}, bf16[256,1024]{1,0:T(8,128)(2,1)S(1)}, u32[]{:S(2)}, u32[]{:S(2)}) collective-permute-start(bf16[256,1024]{1,0:T(8,128)(2,1)S(1)} %get-tuple-element.93.refs_7_), channel_id=1, source_target_pairs={{0,16},{16,0},{1,17},{17,1},{2,18},{18,2},{3,19},{19,3},{4,20},{20... | collective-permute-start | bytes 1572872 | tf_op jit(solution)/shard_map/ppermute | solution.py:26
  72.2 33.7 %collective-permute-start.20 = (bf16[384,1024]{1,0:T(8,128)(2,1)S(1)}, bf16[384,1024]{1,0:T(8,128)(2,1)S(1)}, u32[]{:S(2)}, u32[]{:S(2)}) collective-permute-start(bf16[384,1024]{1,0:T(8,128)(2,1)S(1)} %shard_map.104), channel_id=1, source_target_pairs={{0,1},{2,3},{1,0},{3,2},{4,5},{6,7},{5,4},{7,6},{8,9},{10,11},{9,8... | collective-permute-start | bytes 2359304 | tf_op jit(solution)/shard_map/ppermute | solution.py:528
  79.4 19.8 %collective-permute-start.21 = (bf16[256,1024]{1,0:T(8,128)(2,1)S(1)}, bf16[256,1024]{1,0:T(8,128)(2,1)S(1)}, u32[]{:S(2)}, u32[]{:S(2)}) collective-permute-start(bf16[256,1024]{1,0:T(8,128)(2,1)S(1)} %shard_map.105), channel_id=1, source_target_pairs={{1,2},{2,1},{5,6},{6,5},{9,10},{10,9},{13,14},{14,13},{17,18},{18,... | collective-permute-start | bytes 1572872 | tf_op jit(solution)/shard_map/ppermute | solution.py:528
  83.2 39.5 %collective-permute-start.23 = (bf16[384,1024]{1,0:T(8,128)(2,1)S(1)}, bf16[384,1024]{1,0:T(8,128)(2,1)S(1)}, u32[]{:S(2)}, u32[]{:S(2)}) collective-permute-start(bf16[384,1024]{1,0:T(8,128)(2,1)S(1)} %shard_map.107), channel_id=1, source_target_pairs={{0,1},{2,3},{1,0},{3,2},{4,5},{6,7},{5,4},{7,6},{8,9},{10,11},{9,8... | collective-permute-start | bytes 2359304 | tf_op jit(solution)/shard_map/ppermute | solution.py:528
  94.8 15.6 %collective-permute-start.24 = (bf16[256,1024]{1,0:T(8,128)(2,1)S(1)}, bf16[256,1024]{1,0:T(8,128)(2,1)S(1)}, u32[]{:S(2)}, u32[]{:S(2)}) collective-permute-start(bf16[256,1024]{1,0:T(8,128)(2,1)S(1)} %shard_map.108), channel_id=1, source_target_pairs={{1,2},{2,1},{5,6},{6,5},{9,10},{10,9},{13,14},{14,13},{17,18},{18,... | collective-permute-start | bytes 1572872 | tf_op jit(solution)/shard_map/ppermute | solution.py:528
  105.9 28.1 %collective-permute-start.28 = (bf16[256,1024]{1,0:T(8,128)(2,1)S(1)}, bf16[256,1024]{1,0:T(8,128)(2,1)S(1)}, u32[]{:S(2)}, u32[]{:S(2)}) collective-permute-start(bf16[256,1024]{1,0:T(8,128)(2,1)S(1)} %shard_map.110), channel_id=1, source_target_pairs={{0,1},{2,3},{1,0},{3,2},{4,5},{6,7},{5,4},{7,6},{8,9},{10,11},{9,8... | collective-permute-start | bytes 1572872 | tf_op jit(solution)/shard_map/ppermute | solution.py:528
  108.0 27.5 %collective-permute-start.29 = (bf16[256,1024]{1,0:T(8,128)(2,1)S(1)}, bf16[256,1024]{1,0:T(8,128)(2,1)S(1)}, u32[]{:S(2)}, u32[]{:S(2)}) collective-permute-start(bf16[256,1024]{1,0:T(8,128)(2,1)S(1)} %shard_map.111), channel_id=1, source_target_pairs={{1,2},{2,1},{5,6},{6,5},{9,10},{10,9},{13,14},{14,13},{17,18},{18,... | collective-permute-start | bytes 1572872 | tf_op jit(solution)/shard_map/ppermute | solution.py:528
  111.2 37.1 %collective-permute-start.26 = (bf16[256,1024]{1,0:T(8,128)(2,1)S(1)}, bf16[256,1024]{1,0:T(8,128)(2,1)S(1)}, u32[]{:S(2)}, u32[]{:S(2)}) collective-permute-start(bf16[256,1024]{1,0:T(8,128)(2,1)S(1)} %shard_map.113), channel_id=1, source_target_pairs={{0,1},{2,3},{1,0},{3,2},{4,5},{6,7},{5,4},{7,6},{8,9},{10,11},{9,8... | collective-permute-start | bytes 1572872 | tf_op jit(solution)/shard_map/ppermute | solution.py:528
  123.6 33.4 %collective-permute-start.27 = (bf16[256,1024]{1,0:T(8,128)(2,1)S(1)}, bf16[256,1024]{1,0:T(8,128)(2,1)S(1)}, u32[]{:S(2)}, u32[]{:S(2)}) collective-permute-start(bf16[256,1024]{1,0:T(8,128)(2,1)S(1)} %shard_map.114), channel_id=1, source_target_pairs={{1,2},{2,1},{5,6},{6,5},{9,10},{10,9},{13,14},{14,13},{17,18},{18,... | collective-permute-start | bytes 1572872 | tf_op jit(solution)/shard_map/ppermute | solution.py:528
  124.3 19.2 %collective-permute-start.22 = (bf16[128,1024]{1,0:T(8,128)(2,1)S(1)}, bf16[128,1024]{1,0:T(8,128)(2,1)S(1)}, u32[]{:S(2)}, u32[]{:S(2)}) collective-permute-start(bf16[128,1024]{1,0:T(8,128)(2,1)S(1)} %get-tuple-element.113.refs_13_), channel_id=1, source_target_pairs={{0,16},{16,0},{1,17},{17,1},{2,18},{18,2},{3,19},{19,3},{4,20},{20... | collective-permute-start | bytes 786440 | tf_op jit(solution)/shard_map/ppermute | solution.py:26
  142.8 15.8 %collective-permute-start.32 = (bf16[256,256]{1,0:T(8,128)(2,1)S(1)}, bf16[256,256]{1,0:T(8,128)(2,1)S(1)}, u32[]{:S(2)}, u32[]{:S(2)}) collective-permute-start(bf16[256,256]{1,0:T(8,128)(2,1)S(1)} %get-tuple-element.126), channel_id=1, source_target_pairs={{0,1},{2,3},{1,0},{3,2},{4,5},{6,7},{5,4},{7,6},{8,9},{10,11},{9,8... | collective-permute-start | bytes 393224 | tf_op jit(solution)/shard_map/ppermute | solution.py:503
  143.5 15.0 %collective-permute-start.33 = (bf16[256,256]{1,0:T(8,128)(2,1)S(1)}, bf16[256,256]{1,0:T(8,128)(2,1)S(1)}, u32[]{:S(2)}, u32[]{:S(2)}) collective-permute-start(bf16[256,256]{1,0:T(8,128)(2,1)S(1)} %get-tuple-element.127), channel_id=1, source_target_pairs={{1,2},{2,1},{5,6},{6,5},{9,10},{10,9},{13,14},{14,13},{17,18},{18,... | collective-permute-start | bytes 393224 | tf_op jit(solution)/shard_map/ppermute | solution.py:503
  144.2 14.8 %collective-permute-start.34 = (bf16[256,256]{1,0:T(8,128)(2,1)S(1)}, bf16[256,256]{1,0:T(8,128)(2,1)S(1)}, u32[]{:S(2)}, u32[]{:S(2)}) collective-permute-start(bf16[256,256]{1,0:T(8,128)(2,1)S(1)} %get-tuple-element.128), channel_id=1, source_target_pairs={{0,2},{1,3},{2,0},{3,1},{4,6},{5,7},{6,4},{7,5},{8,10},{9,11},{10,... | collective-permute-start | bytes 393224 | tf_op jit(solution)/shard_map/ppermute | solution.py:503
  (20 other events, 225.3 us)

commit v5 on v4

--- a/solution.py
+++ b/solution.py
@@ -185,13 +185,18 @@
     return value
 
 
-def message(step, count, odd, stream, slot, back, inputs, received, owned, rank):
+def message(step, count, odd, stream, slot, back, inputs, received, extra, owned, rank):
     rows, width = inputs.shape[0], received.shape[1]
     tile = tile_of(width)
     down_rows = owned * rank
     height = down_rows if only_sums(count, step, odd) else received.shape[0]
-
-    def body(slot_ref, back_ref, in_ref, got_ref, out_ref, factor_ref):
+    given, below, across = [], 0, 1
+    if extra is not None:
+        given, across = [extra], tile // extra.shape[1]
+        below = down_rows * extra.shape[1] // width
+
+    def body(slot_ref, back_ref, in_ref, got_ref, *refs):
+        out_ref, factor_ref = refs[-2:]
         place = lax.axis_index("dp")
         up = going_up(place, odd)
         along = jnp.where(up, place, count - 1 - place)
@@ -205,6 +210,9 @@
         def add():
             value = dot(factor_ref[...], in_ref[...], 1, 0)
             out_ref[:down_rows, :] = narrow(value + got_ref[:down_rows, :].astype(jnp.float32))
+            for at in range(across if given else 0):
+                lanes = slice(at * extra.shape[1], (at + 1) * extra.shape[1])
+                out_ref[down_rows:, lanes] = refs[0][at * below : (at + 1) * below, :]
             if height > down_rows:
                 out_ref[down_rows:, :] = jnp.zeros((height - down_rows, tile), jnp.bfloat16)
 
@@ -225,13 +233,15 @@
             full(back.shape),
             columns(rows, tile, stream * (width // tile)),
             columns(height, tile),
-        ],
-        columns(height, tile),
-        jax.ShapeDtypeStruct((height, width), jnp.bfloat16),
+        ]
+        + [pl.BlockSpec((below * across, one.shape[1]), lambda at: (at, 0)) for one in given],
+        columns(height + below, tile),
+        jax.ShapeDtypeStruct((height + below, width), jnp.bfloat16),
         slot,
         back,
         inputs,
         received,
+        *given,
         scratch=[pltpu.VMEM((down_rows, rows), jnp.bfloat16)],
     )
 
@@ -274,7 +284,7 @@
     )
 
 
-def use_pieces(step, count, stream, slot, back, inputs, pieces, proj, low, owned, rank):
+def use_pieces(step, count, stream, slot, back, inputs, pieces, proj, low, prior, owned, rank):
     rows, width = inputs.shape[0], pieces[0].shape[1]
     tile = tile_of(width)
     down_rows = owned * rank
@@ -283,6 +293,8 @@
     merged = one_sided(count, step) and total > 1
     shared = share * (1 if merged else total)
     held = [] if proj is None else [proj], [] if low is None else [low]
+    given = [] if prior is None else [prior]
+    above = 0 if prior is None else prior.shape[0]
 
     def body(slot_ref, back_ref, in_ref, *refs):
         place = lax.axis_index("dp")
@@ -290,6 +302,9 @@
         slots, ins = slot_ref[...], in_ref[...]
         piece_refs, share_refs, refs = refs[:total], refs[total : 2 * total], refs[2 * total :]
         held_refs, (proj_ref, low_ref, share_ref, factor_ref) = refs[:-4], refs[-4:]
+        if given:
+            share_ref[:above, :] = held_refs[-1][...]
+            held_refs = held_refs[:-1]
 
         @pl.when(pl.program_id(0) == 0)
         def prepare():
@@ -298,10 +313,10 @@
 
         if merged:
             came = within(count, blocks[0])
-            share_ref[...] = jnp.where(came, share_refs[0][...], share_refs[1][...])
+            share_ref[above:, :] = jnp.where(came, share_refs[0][...], share_refs[1][...])
         else:
             for at, ref in enumerate(share_refs):
-                share_ref[at * share : (at + 1) * share, :] = ref[...]
+                share_ref[above + at * share : above + (at + 1) * share, :] = ref[...]
         sums, lows = None, None
         for at, block in enumerate(blocks):
             value = piece_refs[at][...]
@@ -326,12 +341,13 @@
         + [columns(down_rows, tile)] * total
         + [columns(share, tile, 0, down_rows // share)] * total
         + [full((rank, rows))] * len(held[0])
-        + [columns(rows, tile)] * len(held[1]),
-        [full((rank, rows)), columns(rows, tile), columns(shared, tile)],
+        + [columns(rows, tile)] * len(held[1])
+        + [columns(above, tile)] * len(given),
+        [full((rank, rows)), columns(rows, tile), columns(above + shared, tile)],
         [
             jax.ShapeDtypeStruct((rank, rows), jnp.float32),
             jax.ShapeDtypeStruct((rows, width), jnp.bfloat16),
-            jax.ShapeDtypeStruct((shared, width), jnp.bfloat16),
+            jax.ShapeDtypeStruct((above + shared, width), jnp.bfloat16),
         ],
         slot,
         back,
@@ -340,6 +356,7 @@
         *pieces,
         *held[0],
         *held[1],
+        *given,
         scratch=[pltpu.VMEM((total, down_rows, rows), jnp.bfloat16)],
         flops=piece_flops if step else 1,
     )
@@ -364,6 +381,37 @@
         slot,
         proj,
         cotangent,
+    )
+
+
+def up_total(own, swapped, others):
+    height, keys = own.shape
+    width = swapped[0].shape[1]
+    across = width // keys
+    below = height // across
+
+    def body(*refs):
+        own_ref, swapped_refs, other_refs = refs[0], refs[1 : 1 + len(swapped)], refs[1 + len(swapped) : -1]
+        for at in range(across):
+            rows, lanes = slice(at * below, (at + 1) * below), slice(at * keys, (at + 1) * keys)
+            total = own_ref[rows, :].astype(jnp.float32)
+            for ref in swapped_refs:
+                total = total + ref[:, lanes].astype(jnp.float32)
+            for ref in other_refs:
+                total = total + ref[rows, :].astype(jnp.float32)
+            refs[-1][rows, :] = narrow(total)
+
+    return call(
+        body,
+        (1,),
+        [full(own.shape)]
+        + [pl.BlockSpec((below, width), lambda at: (height // below, 0))] * len(swapped)
+        + [full(own.shape)] * len(others),
+        full(own.shape),
+        jax.ShapeDtypeStruct(own.shape, jnp.bfloat16),
+        own,
+        *swapped,
+        *others,
     )
 
 
@@ -486,27 +534,27 @@
     slot = jnp.sum(jnp.where(ids[None, :] == every, adapter_slot_index[:, None], 0), axis=0)
     slot = slot[None, :]
 
-    def up_swaps(proj):
-        targets, routes = [lambda place: place], []
-        for step in range(1, data_count):
-            for odd in (0, 1):
-                ends = [i for i in range(data_count - step) if i // step % 2 == odd]
-                if ends:
-                    swaps = [(i, i + step) for i in ends] + [(i + step, i) for i in ends]
-                    routes.append(swaps)
-                    targets.append(
-                        lambda place, step=step, odd=odd: jnp.where(
-                            lax.rem(lax.div(place, step), 2) == odd, place + step, place - step
-                        )
-                    )
-        parts = up_parts(targets, slot, proj, cotangent, owned, rank)
-        got = [lax.ppermute(part, "dp", swaps) for part, swaps in zip(parts[1:], routes)]
-        return [parts[0]] + got
+    def up_ways(step):
+        ways = []
+        for odd in (0, 1):
+            ends = [i for i in range(data_count - step) if i // step % 2 == odd]
+
+            def other(place, odd=odd):
+                mine = lax.rem(lax.div(place, step), 2) == odd
+                return jnp.where(mine, place + step, place - step)
+
+            if ends:
+                swaps = [(i, i + step) for i in ends] + [(i + step, i) for i in ends]
+                ways.append((other, swaps))
+        return ways
+
+    def own_block(place):
+        return place
 
     streams = range(len(packed))
     received = [[one, one] for one in after(packed, ups)]
     got, lows = [[one] for one in packed], [None for _ in streams]
-    proj, back, exchanged = None, None, []
+    proj, back, exchanged, extras = None, None, [], [None, None]
     cotangents = [cotangent] + turns(after(cotangent, ups), "fsdp")
     last = [cotangents]
     waited = {step: [] for step in range(data_count + 3)}
@@ -520,8 +568,9 @@
                 if step > 1:
                     other = after(other, last, waited[step] if stream == streams[-1] else [])
                 if not only_blocks(step, odd):
+                    extra = extras[odd] if stream == streams[-1] else None
                     other = message(
-                        step, data_count, odd, stream, slot, back, inputs, other, owned, rank
+                        step, data_count, odd, stream, slot, back, inputs, other, extra, owned, rank
                     )
                 sent.append(other)
             received[stream] = [
@@ -533,20 +582,30 @@
             if step == 2:
                 proj, lows[stream], _ = use_pieces(
                     0, data_count, stream, slot, back, inputs, [packed[stream]], proj, None,
-                    owned, rank,
+                    None, owned, rank,
                 )
+            merged = one_sided(data_count, step - 1)
+            if stream == 0 or not merged:
+                prior, described = None, []
             proj, lows[stream], share = use_pieces(
                 step - 1, data_count, stream, slot, back, inputs, pieces, proj, lows[stream],
-                owned, rank,
+                prior, owned, rank,
             )
             last = [proj, lows[stream]]
-            share = [share] + turns(share, "groups")
-            waited[step + 1].append(share)
-            if one_sided(data_count, step - 1):
-                described = [(step - 1, stream, odds)]
-            else:
-                described = [(step - 1, stream, [odd]) for odd in odds]
-            exchanged.append((described, share))
+            described += [(step - 1, stream, some) for some in ([odds] if merged else [[odd] for odd in odds])]
+            prior = share
+            if stream == streams[-1] or not merged:
+                share = [share] + turns(share, "groups")
+                waited[step + 1].append(share)
+                exchanged.append((described, share))
+        if step == data_count - 1:
+            near = scaled_sum(proj, "fsdp")
+            ways = sum([up_ways(away) for away in range(1, step)], [])
+            targets = [own_block] + [other for other, _ in ways]
+            up_own, *parts = up_parts(targets, slot, near, cotangent, owned, rank)
+            extras = parts[:2]
+            waiting = [(part, way) for part, (_, way) in zip(parts[2:], ways[2:])]
+            proj = None
         odds = [odd for odd in (0, 1) if not only_sums(data_count, step, odd)]
         got = [[received[stream][odd] for odd in odds] for stream in streams]
 
@@ -561,14 +620,17 @@
             stream, slot, back, inputs, received[stream], down_grad, owned, rank
         )
         if stream == 0:
-            proj = scaled_sum(after(proj, down_grad), "fsdp")
-            up_grads = up_swaps(proj)
-    up_grads = after(up_grads, input_grad)
-    up_grad = sum(part.astype(jnp.float32) for part in up_grads)
+            others = [lax.ppermute(after(part, down_grad), "dp", way) for part, way in waiting]
+            far = scaled_sum(after(proj, down_grad), "fsdp")
+            ways = up_ways(data_count - 1)
+            parts = up_parts([other for other, _ in ways], slot, far, cotangent, owned, rank)
+            others += [lax.ppermute(part, "dp", way) for part, (_, way) in zip(parts, ways)]
+    others = after(others, input_grad)
+    up_grad = up_total(up_own, received[streams[-1]], others)
     return (
         input_grad,
         down_grad.reshape(owned, rank, feat_width),
-        narrow(up_grad).reshape(owned, rank, key_shard),
+        up_grad.reshape(owned, rank, key_shard),
     )
 
 

time: 160 us -> 155 us (0.969)
  starting transfers between devices: 69.7 us -> 61.9 us
  waiting for transfers between devices: 51.4 us -> 53.8 us
    ppermute x12 -> x10, waiting for transfers between devices: 16.4 us -> 22 us  [turns(): lax.ppermute(value, axis, [(i, (i + step) % count) for i in range(count)])]
    ppermute x16, waiting for transfers between devices: 27.3 us -> 22.4 us  [shards(): lax.ppermute(sent[odd], 'dp', pairs(data_count, odd))]
    ppermute x4 -> x2, starting transfers between devices: 9.51 us -> 5.05 us  [the longest x1 2.69 us: shards(): lax.ppermute(after(part, down_grad), 'dp', way)]
    ppermute x16, starting transfers between devices: 41.8 us -> 39.1 us  [shards(): lax.ppermute(sent[odd], 'dp', pairs(data_count, odd))]
    ppermute x12 -> x10, starting transfers between devices: 15.3 us -> 13.1 us  [turns(): lax.ppermute(value, axis, [(i, (i + step) % count) for i in range(count)])]
    ppermute x4 -> x6, starting transfers between devices: 3.06 us -> 4.69 us  [scaled_sum(): other = lax.ppermute(value, axis, [(i, i ^ step) for i in range(count)])]
    pallas_call x28 -> x32, Pallas kernels: 33.2 us -> 34.3 us  [call(): pl.pallas_call(body, grid=grid, in_specs=in_specs, out_specs=out_specs, o...]
    ppermute x4 -> x6, waiting for transfers between devices: 7.24 us -> 7.74 us  [scaled_sum(): other = lax.ppermute(value, axis, [(i, i ^ step) for i in range(count)])]
  transfers between devices with their start and end apart: 36 -> 34, of which waited for: 15 -> 18; matrix products, arithmetic and copies ran while one was open for 0% -> 0% of each run, Pallas kernels for 21% -> 22%
where the time goes in v5:
time: 155 us
  starting transfers between devices  61.9 us (40%)
  waiting for transfers between devices  53.8 us (35%)
  Pallas kernels  34.3 us (22%)
  local copies, waits for them, and re-layouts  3.51 us (2%)
    ppermute x16, starting transfers between devices, shards(): lax.ppermute(sent[odd], 'dp', pairs(data_count, odd))  39.1 us
    pallas_call x32, Pallas kernels, call(): pl.pallas_call(body, grid=grid, in_specs=in_specs, out_specs=out_specs, o...  34.3 us
    ppermute x16, waiting for transfers between devices, shards(): lax.ppermute(sent[odd], 'dp', pairs(data_count, odd))  22.4 us
    ppermute x10, waiting for transfers between devices, turns(): lax.ppermute(value, axis, [(i, (i + step) % count) for i in range(count)])  22 us
    ppermute x10, starting transfers between devices, turns(): lax.ppermute(value, axis, [(i, (i + step) % count) for i in range(count)])  13.1 us
    ppermute x6, waiting for transfers between devices, scaled_sum(): other = lax.ppermute(value, axis, [(i, i ^ step) for i in range(count)])  7.74 us
    ppermute x6, starting transfers between devices, scaled_sum(): other = lax.ppermute(value, axis, [(i, i ^ step) for i in range(count)])  4.69 us
    unnamed x16, local copies, waits for them, and re-layouts  3.5 us
  transfers between devices with their start and end apart: 34, of which 18 were waited for; matrix products, arithmetic and copies ran while one was open for 0% of the time, Pallas kernels for 22%

profile of v5, /device:TPU:0, one launch (start us, length us, event | category | flops | bytes accessed | tf_op | source)
XLA Modules:
  0.0 154.7 jit_solution(8274346697048352752)
XLA Ops:
  1.7 5.1 %collective-permute-start.2 = (bf16[256,256]{1,0:T(8,128)(2,1)S(1)}, bf16[256,256]{1,0:T(8,128)(2,1)S(1)}, u32[]{:S(2)}, u32[]{:S(2)}) collective-permute-start(bf16[256,256]{1,0:T(8,128)(2,1)S(1)} %bitcast.30), channel_id=1, source_target_pairs={{0,3},{1,0},{2,1},{3,2},{4,7},{5,4},{6,5},{7,6},{8,11},{9,8},{10,9... | collective-permute-start | bytes 393224 | tf_op jit(solution)/shard_map/ppermute | solution.py:26
  10.7 7.3 %collective-permute-done.1.refs_2_ = bf16[256,256]{1,0:T(8,128)(2,1)S(1)} collective-permute-done((bf16[256,256]{1,0:T(8,128)(2,1)S(1)}, bf16[256,256]{1,0:T(8,128)(2,1)S(1)}, u32[]{:S(2)}, u32[]{:S(2)}) %collective-permute-start.1) | collective-permute-done | bytes 131104 | tf_op jit(solution)/shard_map/ppermute | solution.py:26
  21.2 2.4 %collective-permute-done.5.refs_3_ = bf16[512,256]{1,0:T(8,128)(2,1)S(1)} collective-permute-done((bf16[512,256]{1,0:T(8,128)(2,1)S(1)}, bf16[512,256]{1,0:T(8,128)(2,1)S(1)}, u32[]{:S(2)}, u32[]{:S(2)}) %collective-permute-start.5) | collective-permute-done | bytes 262176 | tf_op jit(solution)/shard_map/ppermute | solution.py:26
  24.7 7.5 %collective-permute-done.4.refs_2_ = bf16[512,256]{1,0:T(8,128)(2,1)S(1)} collective-permute-done((bf16[512,256]{1,0:T(8,128)(2,1)S(1)}, bf16[512,256]{1,0:T(8,128)(2,1)S(1)}, u32[]{:S(2)}, u32[]{:S(2)}) %collective-permute-start.4) | collective-permute-done | bytes 262176 | tf_op jit(solution)/shard_map/ppermute | solution.py:26
  33.0 5.5 %collective-permute-done.6.refs_0_.refs_2_ = bf16[384,1024]{1,0:T(8,128)(2,1)S(1)} collective-permute-done((bf16[384,1024]{1,0:T(8,128)(2,1)S(1)}, bf16[384,1024]{1,0:T(8,128)(2,1)S(1)}, u32[]{:S(2)}, u32[]{:S(2)}) %collective-permute-start.6) | collective-permute-done | bytes 786464 | tf_op jit(solution)/shard_map/ppermute | solution.py:577
  42.6 2.4 %collective-permute-done.9.refs_1_ = f32[16,512]{1,0:T(8,128)S(1)} collective-permute-done((f32[16,512]{1,0:T(8,128)S(1)}, f32[16,512]{1,0:T(8,128)S(1)}, u32[]{:S(2)}, u32[]{:S(2)}) %collective-permute-start.9) | collective-permute-done | bytes 32800 | tf_op jit(solution)/shard_map/ppermute | solution.py:182
  46.0 3.9 %collective-permute-start.16 = (bf16[384,1024]{1,0:T(8,128)(2,1)S(1)}, bf16[384,1024]{1,0:T(8,128)(2,1)S(1)}, u32[]{:S(2)}, u32[]{:S(2)}) collective-permute-start(bf16[384,1024]{1,0:T(8,128)(2,1)S(1)} %shard_map.98), channel_id=1, source_target_pairs={{0,1},{2,3},{1,0},{3,2},{4,5},{6,7},{5,4},{7,6},{8,9},{10,11},{9,8... | collective-permute-start | bytes 2359304 | tf_op jit(solution)/shard_map/ppermute | solution.py:577
  51.8 2.1 %shard_map.100 = (f32[16,512]{1,0:T(8,128)S(1)}, bf16[512,1024]{1,0:T(8,128)(2,1)S(1)}, bf16[256,1024]{1,0:T(8,128)(2,1)S(1)}) custom-call(s32[1,512]{1,0:T(1,128)S(1)} %bitcast.9, bf16[16,512]{1,0:T(8,128)(2,1)S(1)} %shard_map.97.back_ref, bf16[512,2048]{1,0:T(8,128)(2,1)S(1)} %copy-done.1, bf16[384,1024]{1,0:T(8,128)(2,1)S(1)} %collective-permute-done.6.refs_0_.refs_2_, ...), custom_call_target="tpu_custom_call" | custom-call | flops 1 | bytes 1 | tf_op jit(solution)/shard_map/pallas_call | solution.py:119
  57.0 3.9 %collective-permute-start.14 = (bf16[384,1024]{1,0:T(8,128)(2,1)S(1)}, bf16[384,1024]{1,0:T(8,128)(2,1)S(1)}, u32[]{:S(2)}, u32[]{:S(2)}) collective-permute-start(bf16[384,1024]{1,0:T(8,128)(2,1)S(1)} %shard_map.101), channel_id=1, source_target_pairs={{0,1},{2,3},{1,0},{3,2},{4,5},{6,7},{5,4},{7,6},{8,9},{10,11},{9,8... | collective-permute-start | bytes 2359304 | tf_op jit(solution)/shard_map/ppermute | solution.py:577
  64.4 2.1 %shard_map.103 = (f32[16,512]{1,0:T(8,128)S(1)}, bf16[512,1024]{1,0:T(8,128)(2,1)S(1)}, bf16[256,1024]{1,0:T(8,128)(2,1)S(1)}) custom-call(s32[1,512]{1,0:T(1,128)S(1)} %bitcast.12, bf16[16,512]{1,0:T(8,128)(2,1)S(1)} %shard_map.97.back_ref, bf16[512,2048]{1,0:T(8,128)(2,1)S(1)} %copy-done.1, bf16[384,1024]{1,0:T(8,128)(2,1)S(1)} %collective-permute-done.11.refs_0_.refs_2_, ...), custom_call_target="tpu_custom_call" | custom-call | flops 1 | bytes 1 | tf_op jit(solution)/shard_map/pallas_call | solution.py:119
  68.1 4.1 %collective-permute-done.16.got_ref.refs_0_.refs_2_ = bf16[384,1024]{1,0:T(8,128)(2,1)S(1)} collective-permute-done((bf16[384,1024]{1,0:T(8,128)(2,1)S(1)}, bf16[384,1024]{1,0:T(8,128)(2,1)S(1)}, u32[]{:S(2)}, u32[]{:S(2)}) %collective-permute-start.16) | collective-permute-done | bytes 786464 | tf_op jit(solution)/shard_map/ppermute | solution.py:577
  72.2 5.9 %collective-permute-start.21 = (bf16[384,1024]{1,0:T(8,128)(2,1)S(1)}, bf16[384,1024]{1,0:T(8,128)(2,1)S(1)}, u32[]{:S(2)}, u32[]{:S(2)}) collective-permute-start(bf16[384,1024]{1,0:T(8,128)(2,1)S(1)} %shard_map.104), channel_id=1, source_target_pairs={{0,1},{2,3},{1,0},{3,2},{4,5},{6,7},{5,4},{7,6},{8,9},{10,11},{9,8... | collective-permute-start | bytes 2359304 | tf_op jit(solution)/shard_map/ppermute | solution.py:577
  79.0 2.1 %shard_map.106 = (f32[16,512]{1,0:T(8,128)S(1)}, bf16[512,1024]{1,0:T(8,128)(2,1)S(1)}, bf16[128,1024]{1,0:T(8,128)(2,1)S(1)}) custom-call(s32[1,512]{1,0:T(1,128)S(1)} %bitcast.15, bf16[16,512]{1,0:T(8,128)(2,1)S(1)} %shard_map.97.back_ref, bf16[512,2048]{1,0:T(8,128)(2,1)S(1)} %copy-done.1, ...), custom_call_target="tpu_custom_call" | custom-call | flops 1 | bytes 1 | tf_op jit(solution)/shard_map/pallas_call | solution.py:119
  81.1 4.4 %collective-permute-done.13.refs_8_ = bf16[256,1024]{1,0:T(8,128)(2,1)S(1)} collective-permute-done((bf16[256,1024]{1,0:T(8,128)(2,1)S(1)}, bf16[256,1024]{1,0:T(8,128)(2,1)S(1)}, u32[]{:S(2)}, u32[]{:S(2)}) %collective-permute-start.13) | collective-permute-done | bytes 524320 | tf_op jit(solution)/shard_map/ppermute | solution.py:26
  86.4 6.4 %collective-permute-start.19 = (bf16[384,1024]{1,0:T(8,128)(2,1)S(1)}, bf16[384,1024]{1,0:T(8,128)(2,1)S(1)}, u32[]{:S(2)}, u32[]{:S(2)}) collective-permute-start(bf16[384,1024]{1,0:T(8,128)(2,1)S(1)} %shard_map.107), channel_id=1, source_target_pairs={{0,1},{2,3},{1,0},{3,2},{4,5},{6,7},{5,4},{7,6},{8,9},{10,11},{9,8... | collective-permute-start | bytes 2359304 | tf_op jit(solution)/shard_map/ppermute | solution.py:577
  94.5 2.2 %shard_map.109 = (f32[16,512]{1,0:T(8,128)S(1)}, bf16[512,1024]{1,0:T(8,128)(2,1)S(1)}, bf16[256,1024]{1,0:T(8,128)(2,1)S(1)}) custom-call(s32[1,512]{1,0:T(1,128)S(1)} %bitcast.18, bf16[16,512]{1,0:T(8,128)(2,1)S(1)} %shard_map.97.back_ref, bf16[512,2048]{1,0:T(8,128)(2,1)S(1)} %copy-done.1, ...), custom_call_target="tpu_custom_call" | custom-call | flops 1 | bytes 1 | tf_op jit(solution)/shard_map/pallas_call | solution.py:119
  101.9 4.0 %collective-permute-done.21.got_ref.refs_0_.refs_1_ = bf16[384,1024]{1,0:T(8,128)(2,1)S(1)} collective-permute-done((bf16[384,1024]{1,0:T(8,128)(2,1)S(1)}, bf16[384,1024]{1,0:T(8,128)(2,1)S(1)}, u32[]{:S(2)}, u32[]{:S(2)}) %collective-permute-start.21) | collective-permute-done | bytes 786464 | tf_op jit(solution)/shard_map/ppermute | solution.py:577
  105.9 6.2 %collective-permute-start.28 = (bf16[256,1024]{1,0:T(8,128)(2,1)S(1)}, bf16[256,1024]{1,0:T(8,128)(2,1)S(1)}, u32[]{:S(2)}, u32[]{:S(2)}) collective-permute-start(bf16[256,1024]{1,0:T(8,128)(2,1)S(1)} %shard_map.110), channel_id=1, source_target_pairs={{0,1},{2,3},{1,0},{3,2},{4,5},{6,7},{5,4},{7,6},{8,9},{10,11},{9,8... | collective-permute-start | bytes 1572872 | tf_op jit(solution)/shard_map/ppermute | solution.py:577
  116.7 5.2 %collective-permute-start.26 = (bf16[320,1024]{1,0:T(8,128)(2,1)S(1)}, bf16[320,1024]{1,0:T(8,128)(2,1)S(1)}, u32[]{:S(2)}, u32[]{:S(2)}) collective-permute-start(bf16[320,1024]{1,0:T(8,128)(2,1)S(1)} %shard_map.116), channel_id=1, source_target_pairs={{0,1},{2,3},{1,0},{3,2},{4,5},{6,7},{5,4},{7,6},{8,9},{10,11},{9,8... | collective-permute-start | bytes 1966088 | tf_op jit(solution)/shard_map/ppermute | solution.py:577
  127.5 6.5 %collective-permute-done.28.refs_0_ = bf16[256,1024]{1,0:T(8,128)(2,1)S(1)} collective-permute-done((bf16[256,1024]{1,0:T(8,128)(2,1)S(1)}, bf16[256,1024]{1,0:T(8,128)(2,1)S(1)}, u32[]{:S(2)}, u32[]{:S(2)}) %collective-permute-start.28) | collective-permute-done | bytes 524320 | tf_op jit(solution)/shard_map/ppermute | solution.py:577
  138.3 2.4 %collective-permute-done.32.refs_1_ = f32[16,512]{1,0:T(8,128)S(1)} collective-permute-done((f32[16,512]{1,0:T(8,128)S(1)}, f32[16,512]{1,0:T(8,128)S(1)}, u32[]{:S(2)}, u32[]{:S(2)}) %collective-permute-start.32) | collective-permute-done | bytes 32800 | tf_op jit(solution)/shard_map/ppermute | solution.py:182
  140.7 2.7 %collective-permute-start.30 = (bf16[256,256]{1,0:T(8,128)(2,1)S(1)}, bf16[256,256]{1,0:T(8,128)(2,1)S(1)}, u32[]{:S(2)}, u32[]{:S(2)}) collective-permute-start(bf16[256,256]{1,0:T(8,128)(2,1)S(1)} %get-tuple-element.124), channel_id=1, source_target_pairs={{0,2},{1,3},{2,0},{3,1},{4,6},{5,7},{6,4},{7,5},{8,10},{9,11},{10,... | collective-permute-start | bytes 393224 | tf_op jit(solution)/shard_map/ppermute | solution.py:623
  143.6 2.4 %collective-permute-start.33 = (bf16[256,256]{1,0:T(8,128)(2,1)S(1)}, bf16[256,256]{1,0:T(8,128)(2,1)S(1)}, u32[]{:S(2)}, u32[]{:S(2)}) collective-permute-start(bf16[256,256]{1,0:T(8,128)(2,1)S(1)} %shard_map.124), channel_id=1, source_target_pairs={{0,3},{3,0},{4,7},{7,4},{8,11},{11,8},{12,15},{15,12},{16,19},{19,... | collective-permute-start | bytes 393224 | tf_op jit(solution)/shard_map/ppermute | solution.py:627
  146.0 4.6 %shard_map.119 = bf16[512,2048]{1,0:T(8,128)(2,1)} custom-call(bf16[512,256]{1,0:T(8,128)(2,1)S(1)} %copy-done.4, bf16[512,256]{1,0:T(8,128)(2,1)S(1)} %collective-permute-done.3.refs_1_, bf16[512,256]{1,0:T(8,128)(2,1)S(1)} %collective-permute-done.4.refs_2_, bf16[512,256]{1,0:T(8,128)(2,1)S(1)} %collective-permute-done.5.refs_3_, ...), custom_call_target="tpu_custom_call" | custom-call | flops 1 | bytes 1 | tf_op jit(solution)/shard_map/pallas_call | solution.py:119
  (94 shorter events, 52.2 us)
Async XLA Ops:
  6.8 11.2 %collective-permute-start.1 = (bf16[256,256]{1,0:T(8,128)(2,1)S(1)}, bf16[256,256]{1,0:T(8,128)(2,1)S(1)}, u32[]{:S(2)}, u32[]{:S(2)}) collective-permute-start(bf16[256,256]{1,0:T(8,128)(2,1)S(1)} %bitcast.31), channel_id=1, source_target_pairs={{0,2},{1,3},{2,0},{3,1},{4,6},{5,7},{6,4},{7,5},{8,10},{9,11},{10,... | collective-permute-start | bytes 393224 | tf_op jit(solution)/shard_map/ppermute | solution.py:26
  18.0 20.5 %collective-permute-start.6 = (bf16[384,1024]{1,0:T(8,128)(2,1)S(1)}, bf16[384,1024]{1,0:T(8,128)(2,1)S(1)}, u32[]{:S(2)}, u32[]{:S(2)}) collective-permute-start(bf16[384,1024]{1,0:T(8,128)(2,1)S(1)} %get-tuple-element.69.refs_0_.refs_1_), channel_id=1, source_target_pairs={{0,1},{2,3},{1,0},{3,2},{4,5},{6,7},{5,4},{7,6},{8,9},{10,11},{9,8... | collective-permute-start | bytes 2359304 | tf_op jit(solution)/shard_map/ppermute | solution.py:577
  18.8 20.5 %collective-permute-start.7 = (bf16[384,1024]{1,0:T(8,128)(2,1)S(1)}, bf16[384,1024]{1,0:T(8,128)(2,1)S(1)}, u32[]{:S(2)}, u32[]{:S(2)}) collective-permute-start(bf16[384,1024]{1,0:T(8,128)(2,1)S(1)} %get-tuple-element.69.refs_0_.refs_1_), channel_id=1, source_target_pairs={{1,2},{2,1},{5,6},{6,5},{9,10},{10,9},{13,14},{14,13},{17,18},{18,... | collective-permute-start | bytes 2359304 | tf_op jit(solution)/shard_map/ppermute | solution.py:577
  19.5 12.7 %collective-permute-start.4 = (bf16[512,256]{1,0:T(8,128)(2,1)S(1)}, bf16[512,256]{1,0:T(8,128)(2,1)S(1)}, u32[]{:S(2)}, u32[]{:S(2)}) collective-permute-start(bf16[512,256]{1,0:T(8,128)(2,1)S(1)} %copy-done.4), channel_id=1, source_target_pairs={{0,8},{4,12},{8,0},{12,4},{1,9},{5,13},{9,1},{13,5},{2,10},{6,14},... | collective-permute-start | bytes 786440 | tf_op jit(solution)/shard_map/ppermute | solution.py:26
  21.0 12.0 %collective-permute-start.3 = (bf16[512,256]{1,0:T(8,128)(2,1)S(1)}, bf16[512,256]{1,0:T(8,128)(2,1)S(1)}, u32[]{:S(2)}, u32[]{:S(2)}) collective-permute-start(bf16[512,256]{1,0:T(8,128)(2,1)S(1)} %copy-done.4), channel_id=1, source_target_pairs={{0,4},{4,8},{8,12},{12,0},{1,5},{5,9},{9,13},{13,1},{2,6},{6,10},{... | collective-permute-start | bytes 786440 | tf_op jit(solution)/shard_map/ppermute | solution.py:26
  23.7 31.7 %collective-permute-start.11 = (bf16[384,1024]{1,0:T(8,128)(2,1)S(1)}, bf16[384,1024]{1,0:T(8,128)(2,1)S(1)}, u32[]{:S(2)}, u32[]{:S(2)}) collective-permute-start(bf16[384,1024]{1,0:T(8,128)(2,1)S(1)} %get-tuple-element.81.refs_0_.refs_1_), channel_id=1, source_target_pairs={{0,1},{2,3},{1,0},{3,2},{4,5},{6,7},{5,4},{7,6},{8,9},{10,11},{9,8... | collective-permute-start | bytes 2359304 | tf_op jit(solution)/shard_map/ppermute | solution.py:577
  32.2 23.9 %collective-permute-start.12 = (bf16[384,1024]{1,0:T(8,128)(2,1)S(1)}, bf16[384,1024]{1,0:T(8,128)(2,1)S(1)}, u32[]{:S(2)}, u32[]{:S(2)}) collective-permute-start(bf16[384,1024]{1,0:T(8,128)(2,1)S(1)} %get-tuple-element.81.refs_0_.refs_1_), channel_id=1, source_target_pairs={{1,2},{2,1},{5,6},{6,5},{9,10},{10,9},{13,14},{14,13},{17,18},{18,... | collective-permute-start | bytes 2359304 | tf_op jit(solution)/shard_map/ppermute | solution.py:577
  38.5 28.1 %collective-permute-start.17 = (bf16[384,1024]{1,0:T(8,128)(2,1)S(1)}, bf16[384,1024]{1,0:T(8,128)(2,1)S(1)}, u32[]{:S(2)}, u32[]{:S(2)}) collective-permute-start(bf16[384,1024]{1,0:T(8,128)(2,1)S(1)} %collective-permute-done.6.refs_0_.refs_2_), channel_id=1, source_target_pairs={{1,2},{2,1},{5,6},{6,5},{9,10},{10,9},{13,14},{14,13},{17,18},{18,... | collective-permute-start | bytes 2359304 | tf_op jit(solution)/shard_map/ppermute | solution.py:577
  46.0 26.2 %collective-permute-start.16 = (bf16[384,1024]{1,0:T(8,128)(2,1)S(1)}, bf16[384,1024]{1,0:T(8,128)(2,1)S(1)}, u32[]{:S(2)}, u32[]{:S(2)}) collective-permute-start(bf16[384,1024]{1,0:T(8,128)(2,1)S(1)} %shard_map.98), channel_id=1, source_target_pairs={{0,1},{2,3},{1,0},{3,2},{4,5},{6,7},{5,4},{7,6},{8,9},{10,11},{9,8... | collective-permute-start | bytes 2359304 | tf_op jit(solution)/shard_map/ppermute | solution.py:577
  55.3 30.2 %collective-permute-start.15 = (bf16[384,1024]{1,0:T(8,128)(2,1)S(1)}, bf16[384,1024]{1,0:T(8,128)(2,1)S(1)}, u32[]{:S(2)}, u32[]{:S(2)}) collective-permute-start(bf16[384,1024]{1,0:T(8,128)(2,1)S(1)} %collective-permute-done.11.refs_0_.refs_2_), channel_id=1, source_target_pairs={{1,2},{2,1},{5,6},{6,5},{9,10},{10,9},{13,14},{14,13},{17,18},{18,... | collective-permute-start | bytes 2359304 | tf_op jit(solution)/shard_map/ppermute | solution.py:577
  57.0 36.6 %collective-permute-start.14 = (bf16[384,1024]{1,0:T(8,128)(2,1)S(1)}, bf16[384,1024]{1,0:T(8,128)(2,1)S(1)}, u32[]{:S(2)}, u32[]{:S(2)}) collective-permute-start(bf16[384,1024]{1,0:T(8,128)(2,1)S(1)} %shard_map.101), channel_id=1, source_target_pairs={{0,1},{2,3},{1,0},{3,2},{4,5},{6,7},{5,4},{7,6},{8,9},{10,11},{9,8... | collective-permute-start | bytes 2359304 | tf_op jit(solution)/shard_map/ppermute | solution.py:577
  62.9 18.2 %collective-permute-start.10 = (bf16[256,1024]{1,0:T(8,128)(2,1)S(1)}, bf16[256,1024]{1,0:T(8,128)(2,1)S(1)}, u32[]{:S(2)}, u32[]{:S(2)}) collective-permute-start(bf16[256,1024]{1,0:T(8,128)(2,1)S(1)} %get-tuple-element.80.refs_5_), channel_id=1, source_target_pairs={{0,16},{16,0},{1,17},{17,1},{2,18},{18,2},{3,19},{19,3},{4,20},{20... | collective-permute-start | bytes 1572872 | tf_op jit(solution)/shard_map/ppermute | solution.py:26
  66.6 18.9 %collective-permute-start.13 = (bf16[256,1024]{1,0:T(8,128)(2,1)S(1)}, bf16[256,1024]{1,0:T(8,128)(2,1)S(1)}, u32[]{:S(2)}, u32[]{:S(2)}) collective-permute-start(bf16[256,1024]{1,0:T(8,128)(2,1)S(1)} %get-tuple-element.90.refs_7_), channel_id=1, source_target_pairs={{0,16},{16,0},{1,17},{17,1},{2,18},{18,2},{3,19},{19,3},{4,20},{20... | collective-permute-start | bytes 1572872 | tf_op jit(solution)/shard_map/ppermute | solution.py:26
  72.2 33.7 %collective-permute-start.21 = (bf16[384,1024]{1,0:T(8,128)(2,1)S(1)}, bf16[384,1024]{1,0:T(8,128)(2,1)S(1)}, u32[]{:S(2)}, u32[]{:S(2)}) collective-permute-start(bf16[384,1024]{1,0:T(8,128)(2,1)S(1)} %shard_map.104), channel_id=1, source_target_pairs={{0,1},{2,3},{1,0},{3,2},{4,5},{6,7},{5,4},{7,6},{8,9},{10,11},{9,8... | collective-permute-start | bytes 2359304 | tf_op jit(solution)/shard_map/ppermute | solution.py:577
  86.4 36.3 %collective-permute-start.19 = (bf16[384,1024]{1,0:T(8,128)(2,1)S(1)}, bf16[384,1024]{1,0:T(8,128)(2,1)S(1)}, u32[]{:S(2)}, u32[]{:S(2)}) collective-permute-start(bf16[384,1024]{1,0:T(8,128)(2,1)S(1)} %shard_map.107), channel_id=1, source_target_pairs={{0,1},{2,3},{1,0},{3,2},{4,5},{6,7},{5,4},{7,6},{8,9},{10,11},{9,8... | collective-permute-start | bytes 2359304 | tf_op jit(solution)/shard_map/ppermute | solution.py:577
  96.8 19.0 %collective-permute-start.20 = (bf16[256,1024]{1,0:T(8,128)(2,1)S(1)}, bf16[256,1024]{1,0:T(8,128)(2,1)S(1)}, u32[]{:S(2)}, u32[]{:S(2)}) collective-permute-start(bf16[256,1024]{1,0:T(8,128)(2,1)S(1)} %shard_map.108), channel_id=1, source_target_pairs={{1,2},{2,1},{5,6},{6,5},{9,10},{10,9},{13,14},{14,13},{17,18},{18,... | collective-permute-start | bytes 1572872 | tf_op jit(solution)/shard_map/ppermute | solution.py:577
  98.0 17.8 %collective-permute-start.18 = (bf16[256,1024]{1,0:T(8,128)(2,1)S(1)}, bf16[256,1024]{1,0:T(8,128)(2,1)S(1)}, u32[]{:S(2)}, u32[]{:S(2)}) collective-permute-start(bf16[256,1024]{1,0:T(8,128)(2,1)S(1)} %get-tuple-element.104.refs_9_), channel_id=1, source_target_pairs={{0,16},{16,0},{1,17},{17,1},{2,18},{18,2},{3,19},{19,3},{4,20},{20... | collective-permute-start | bytes 1572872 | tf_op jit(solution)/shard_map/ppermute | solution.py:26
  99.5 13.4 %collective-permute-start.24 = (f32[16,512]{1,0:T(8,128)S(1)}, f32[16,512]{1,0:T(8,128)S(1)}, u32[]{:S(2)}, u32[]{:S(2)}) collective-permute-start(f32[16,512]{1,0:T(8,128)S(1)} %shard_map.113.refs_0_), channel_id=1, source_target_pairs={{0,8},{4,12},{8,0},{12,4},{1,9},{5,13},{9,1},{13,5},{2,10},{6,14},... | collective-permute-start | bytes 98312 | tf_op jit(solution)/shard_map/ppermute | solution.py:182
  105.9 28.1 %collective-permute-start.28 = (bf16[256,1024]{1,0:T(8,128)(2,1)S(1)}, bf16[256,1024]{1,0:T(8,128)(2,1)S(1)}, u32[]{:S(2)}, u32[]{:S(2)}) collective-permute-start(bf16[256,1024]{1,0:T(8,128)(2,1)S(1)} %shard_map.110), channel_id=1, source_target_pairs={{0,1},{2,3},{1,0},{3,2},{4,5},{6,7},{5,4},{7,6},{8,9},{10,11},{9,8... | collective-permute-start | bytes 1572872 | tf_op jit(solution)/shard_map/ppermute | solution.py:577
  112.9 21.1 %collective-permute-start.29 = (bf16[256,1024]{1,0:T(8,128)(2,1)S(1)}, bf16[256,1024]{1,0:T(8,128)(2,1)S(1)}, u32[]{:S(2)}, u32[]{:S(2)}) collective-permute-start(bf16[256,1024]{1,0:T(8,128)(2,1)S(1)} %shard_map.111), channel_id=1, source_target_pairs={{1,2},{2,1},{5,6},{6,5},{9,10},{10,9},{13,14},{14,13},{17,18},{18,... | collective-permute-start | bytes 1572872 | tf_op jit(solution)/shard_map/ppermute | solution.py:577
  116.7 34.0 %collective-permute-start.26 = (bf16[320,1024]{1,0:T(8,128)(2,1)S(1)}, bf16[320,1024]{1,0:T(8,128)(2,1)S(1)}, u32[]{:S(2)}, u32[]{:S(2)}) collective-permute-start(bf16[320,1024]{1,0:T(8,128)(2,1)S(1)} %shard_map.116), channel_id=1, source_target_pairs={{0,1},{2,3},{1,0},{3,2},{4,5},{6,7},{5,4},{7,6},{8,9},{10,11},{9,8... | collective-permute-start | bytes 1966088 | tf_op jit(solution)/shard_map/ppermute | solution.py:577
  123.6 27.0 %collective-permute-start.27 = (bf16[320,1024]{1,0:T(8,128)(2,1)S(1)}, bf16[320,1024]{1,0:T(8,128)(2,1)S(1)}, u32[]{:S(2)}, u32[]{:S(2)}) collective-permute-start(bf16[320,1024]{1,0:T(8,128)(2,1)S(1)} %shard_map.117), channel_id=1, source_target_pairs={{1,2},{2,1},{5,6},{6,5},{9,10},{10,9},{13,14},{14,13},{17,18},{18,... | collective-permute-start | bytes 1966088 | tf_op jit(solution)/shard_map/ppermute | solution.py:577
  125.9 20.1 %collective-permute-start.25 = (bf16[256,1024]{1,0:T(8,128)(2,1)S(1)}, bf16[256,1024]{1,0:T(8,128)(2,1)S(1)}, u32[]{:S(2)}, u32[]{:S(2)}) collective-permute-start(bf16[256,1024]{1,0:T(8,128)(2,1)S(1)} %get-tuple-element.118.refs_11_), channel_id=1, source_target_pairs={{0,16},{16,0},{1,17},{17,1},{2,18},{18,2},{3,19},{19,3},{4,20},{20... | collective-permute-start | bytes 1572872 | tf_op jit(solution)/shard_map/ppermute | solution.py:26
  140.7 11.6 %collective-permute-start.30 = (bf16[256,256]{1,0:T(8,128)(2,1)S(1)}, bf16[256,256]{1,0:T(8,128)(2,1)S(1)}, u32[]{:S(2)}, u32[]{:S(2)}) collective-permute-start(bf16[256,256]{1,0:T(8,128)(2,1)S(1)} %get-tuple-element.124), channel_id=1, source_target_pairs={{0,2},{1,3},{2,0},{3,1},{4,6},{5,7},{6,4},{7,5},{8,10},{9,11},{10,... | collective-permute-start | bytes 393224 | tf_op jit(solution)/shard_map/ppermute | solution.py:623
  (18 other events, 187.9 us)

commit v6 on v5

--- a/solution.py
+++ b/solution.py
@@ -9,6 +9,7 @@
 
 adapter_scale = 2.0
 piece_flops = 1
+back_flops = 10**10
 vmem_bytes = 24 * 1024 * 1024
 
 
@@ -150,6 +151,7 @@
         slot,
         cotangent,
         *parts,
+        flops=back_flops,
     )
 
 
@@ -183,6 +185,46 @@
         step *= 2
         value = add_up([value, other], step >= count)
     return value
+
+
+def stacked(arrays):
+    heights = [array.shape[0] for array in arrays]
+    shape = (sum(heights), arrays[0].shape[1])
+
+    def body(*refs):
+        at = 0
+        for ref, height in zip(refs, heights):
+            refs[-1][at : at + height, :] = ref[...]
+            at += height
+
+    return call(
+        body,
+        (1,),
+        [full(array.shape) for array in arrays],
+        full(shape),
+        jax.ShapeDtypeStruct(shape, arrays[0].dtype),
+        *arrays,
+    )
+
+
+def gathered(value, axis):
+    count = lax.axis_size(axis)
+    found = [(value, [lambda part: part])]
+    if count & (count - 1):
+        for turn, other in enumerate(turns(value, axis), 1):
+            found.append((other, [lambda part, turn=turn: lax.rem(part + count - turn, count)]))
+        return found
+    step = 1
+    while step < count:
+        whole = stacked([array for array, _ in found]) if step > 1 else value
+        other = lax.ppermute(whole, axis, [(i, i ^ step) for i in range(count)])
+        owners = [
+            lambda part, far=step + near: lax.bitwise_xor(part, jnp.int32(far))
+            for near in range(step)
+        ]
+        found.append((other, owners))
+        step *= 2
+    return found
 
 
 def message(step, count, odd, stream, slot, back, inputs, received, extra, owned, rank):
@@ -445,7 +487,7 @@
     rows, stream_width = lows[0].shape
     streams = len(lows)
     weight_rows, keys = weight_own.shape
-    shard = cotangents[0].shape[1]
+    shard = cotangents[0][0].shape[1]
     count, groups, parts = lax.axis_size("dp"), lax.axis_size("groups"), len(cotangents)
     half = weight_rows // groups
     chunk = half // streams
@@ -462,9 +504,10 @@
         @pl.when(now == 0)
         def arrange():
             place, group, part = (lax.axis_index(axis) for axis in ("dp", "groups", "fsdp"))
-            for turn, ref in enumerate(cot_refs):
-                at = lax.rem(part + parts - turn, parts) * shard
-                dy_ref[:, pl.ds(pl.multiple_of(at, shard), shard)] = ref[...]
+            for ref, (_, owners) in zip(cot_refs, cotangents):
+                for at, owner in enumerate(owners):
+                    lanes = pl.ds(pl.multiple_of(owner(part) * shard, shard), shard)
+                    dy_ref[:, lanes] = ref[at * rows : (at + 1) * rows, :]
             weight_ref[place] = own_ref[...]
             for at, ref in enumerate(piece_refs):
                 owner = lax.rem(group + groups - at % groups, groups)
@@ -490,7 +533,7 @@
     def low_spec(stream):
         return pl.BlockSpec((rows, tile), lambda at: (0, jnp.clip(at - stream * tiles, 0, tiles - 1)))
 
-    fixed = [*cotangents, weight_own, *pieces]
+    fixed = [*[array for array, _ in cotangents], weight_own, *pieces]
     return call(
         body,
         (streams * tiles,),
@@ -552,16 +595,17 @@
         return place
 
     streams = range(len(packed))
-    received = [[one, one] for one in after(packed, ups)]
+    received = [[one, one] for one in packed]
     got, lows = [[one] for one in packed], [None for _ in streams]
     proj, back, exchanged, extras = None, None, [], [None, None]
-    cotangents = [cotangent] + turns(after(cotangent, ups), "fsdp")
-    last = [cotangents]
+    last = []
     waited = {step: [] for step in range(data_count + 3)}
     for step in range(1, data_count + 1):
         if step == 2:
-            back = back_sum(slot, cotangent, after(ups, received[0], last), owned, rank)
+            back = back_sum(slot, cotangent, ups, owned, rank)
             back = scaled_sum(back, "fsdp")
+            cotangents = gathered(after(cotangent, back), "fsdp")
+            waited[3] += [array for array, _ in cotangents]
         for stream in streams:
             sent = []
             for odd, other in enumerate(reversed(received[stream])):

time: 155 us -> 149 us (0.961)
  starting transfers between devices: 61.9 us -> 53.6 us
  waiting for transfers between devices: 53.8 us -> 56 us
    ppermute x16, waiting for transfers between devices: 22.4 us -> 41.1 us  [shards(): lax.ppermute(sent[odd], 'dp', pairs(data_count, odd))]
    ppermute x10 -> x7, waiting for transfers between devices: 22 us -> 8.28 us  [turns(): lax.ppermute(value, axis, [(i, (i + step) % count) for i in range(count)])]
    ppermute x16, starting transfers between devices: 39.1 us -> 29.3 us  [shards(): lax.ppermute(sent[odd], 'dp', pairs(data_count, odd))]
    ppermute x0 -> x2, starting transfers between devices: none -> 1.75 us  [gathered(): other = lax.ppermute(whole, axis, [(i, i ^ step) for i in range(count)])]
    ppermute x6, waiting for transfers between devices: 7.74 us -> 6.15 us  [scaled_sum(): other = lax.ppermute(value, axis, [(i, i ^ step) for i in range(count)])]
    ppermute x10 -> x7, starting transfers between devices: 13.1 us -> 12.3 us  [turns(): lax.ppermute(value, axis, [(i, (i + step) % count) for i in range(count)])]
    pallas_call x32 -> x33, Pallas kernels: 34.3 us -> 34.4 us  [call(): pl.pallas_call(body, grid=grid, in_specs=in_specs, out_specs=out_specs, o...]
  transfers between devices with their start and end apart: 34 -> 33, of which waited for: 18 -> 15; matrix products, arithmetic and copies ran while one was open for 0% -> 0% of each run, Pallas kernels for 22% -> 23%
where the time goes in v6:
time: 149 us
  waiting for transfers between devices  56 us (38%)
  starting transfers between devices  53.6 us (36%)
  Pallas kernels  34.4 us (23%)
  local copies, waits for them, and re-layouts  3.49 us (2%)
    ppermute x16, waiting for transfers between devices, shards(): lax.ppermute(sent[odd], 'dp', pairs(data_count, odd))  41.1 us
    pallas_call x33, Pallas kernels, call(): pl.pallas_call(body, grid=grid, in_specs=in_specs, out_specs=out_specs, o...  34.4 us
    ppermute x16, starting transfers between devices, shards(): lax.ppermute(sent[odd], 'dp', pairs(data_count, odd))  29.3 us
    ppermute x7, starting transfers between devices, turns(): lax.ppermute(value, axis, [(i, (i + step) % count) for i in range(count)])  12.3 us
    ppermute x7, waiting for transfers between devices, turns(): lax.ppermute(value, axis, [(i, (i + step) % count) for i in range(count)])  8.28 us
    ppermute x6, waiting for transfers between devices, scaled_sum(): other = lax.ppermute(value, axis, [(i, i ^ step) for i in range(count)])  6.15 us
    ppermute x6, starting transfers between devices, scaled_sum(): other = lax.ppermute(value, axis, [(i, i ^ step) for i in range(count)])  4.94 us
    ppermute x1, starting transfers between devices, shards(): lax.ppermute(part, 'dp', way)  3.84 us
  transfers between devices with their start and end apart: 33, of which 15 were waited for; matrix products, arithmetic and copies ran while one was open for 0% of the time, Pallas kernels for 23%

profile of v6, /device:TPU:0, one launch (start us, length us, event | category | flops | bytes accessed | tf_op | source)
XLA Modules:
  0.0 148.7 jit_solution(14089790521417981337)
XLA Ops:
  1.7 3.1 %collective-permute-start = (bf16[256,256]{1,0:T(8,128)(2,1)S(1)}, bf16[256,256]{1,0:T(8,128)(2,1)S(1)}, u32[]{:S(2)}, u32[]{:S(2)}) collective-permute-start(bf16[256,256]{1,0:T(8,128)(2,1)S(1)} %bitcast.30), channel_id=1, source_target_pairs={{0,1},{1,2},{2,3},{3,0},{4,5},{5,6},{6,7},{7,4},{8,9},{9,10},{10,1... | collective-permute-start | bytes 393224 | tf_op jit(solution)/shard_map/ppermute | solution.py:27
  4.8 2.6 %collective-permute-start.1 = (bf16[256,256]{1,0:T(8,128)(2,1)S(1)}, bf16[256,256]{1,0:T(8,128)(2,1)S(1)}, u32[]{:S(2)}, u32[]{:S(2)}) collective-permute-start(bf16[256,256]{1,0:T(8,128)(2,1)S(1)} %bitcast.31), channel_id=1, source_target_pairs={{0,2},{1,3},{2,0},{3,1},{4,6},{5,7},{6,4},{7,5},{8,10},{9,11},{10,... | collective-permute-start | bytes 393224 | tf_op jit(solution)/shard_map/ppermute | solution.py:27
  12.8 2.8 %collective-permute-start.10 = (bf16[384,1024]{1,0:T(8,128)(2,1)S(1)}, bf16[384,1024]{1,0:T(8,128)(2,1)S(1)}, u32[]{:S(2)}, u32[]{:S(2)}) collective-permute-start(bf16[384,1024]{1,0:T(8,128)(2,1)S(1)} %get-tuple-element.65.refs_0_.refs_1_), channel_id=1, source_target_pairs={{0,1},{2,3},{1,0},{3,2},{4,5},{6,7},{5,4},{7,6},{8,9},{10,11},{9,8... | collective-permute-start | bytes 2359304 | tf_op jit(solution)/shard_map/ppermute | solution.py:621
  19.8 2.3 %collective-permute-done.4.refs_1_ = f32[16,512]{1,0:T(8,128)S(1)} collective-permute-done((f32[16,512]{1,0:T(8,128)S(1)}, f32[16,512]{1,0:T(8,128)S(1)}, u32[]{:S(2)}, u32[]{:S(2)}) %collective-permute-start.4) | collective-permute-done | bytes 32800 | tf_op jit(solution)/shard_map/ppermute | solution.py:184
  22.1 11.1 %collective-permute-done.7.refs_0_.refs_2_ = bf16[384,1024]{1,0:T(8,128)(2,1)S(1)} collective-permute-done((bf16[384,1024]{1,0:T(8,128)(2,1)S(1)}, bf16[384,1024]{1,0:T(8,128)(2,1)S(1)}, u32[]{:S(2)}, u32[]{:S(2)}) %collective-permute-start.7) | collective-permute-done | bytes 786464 | tf_op jit(solution)/shard_map/ppermute | solution.py:621
  36.6 2.5 %collective-permute-start.15 = (bf16[384,1024]{1,0:T(8,128)(2,1)S(1)}, bf16[384,1024]{1,0:T(8,128)(2,1)S(1)}, u32[]{:S(2)}, u32[]{:S(2)}) collective-permute-start(bf16[384,1024]{1,0:T(8,128)(2,1)S(1)} %shard_map.99), channel_id=1, source_target_pairs={{0,1},{2,3},{1,0},{3,2},{4,5},{6,7},{5,4},{7,6},{8,9},{10,11},{9,8... | collective-permute-start | bytes 2359304 | tf_op jit(solution)/shard_map/ppermute | solution.py:621
  41.1 2.1 %shard_map.101 = (f32[16,512]{1,0:T(8,128)S(1)}, bf16[512,1024]{1,0:T(8,128)(2,1)S(1)}, bf16[256,1024]{1,0:T(8,128)(2,1)S(1)}) custom-call(s32[1,512]{1,0:T(1,128)S(1)} %bitcast.9, bf16[16,512]{1,0:T(8,128)(2,1)S(1)} %shard_map.96.back_ref, bf16[512,2048]{1,0:T(8,128)(2,1)S(1)} %copy-done.1, bf16[384,1024]{1,0:T(8,128)(2,1)S(1)} %collective-permute-done.7.refs_0_.refs_2_, ...), custom_call_target="tpu_custom_call" | custom-call | flops 1 | bytes 1 | tf_op jit(solution)/shard_map/pallas_call | solution.py:120
  43.2 6.8 %collective-permute-done.10.refs_0_.refs_2_ = bf16[384,1024]{1,0:T(8,128)(2,1)S(1)} collective-permute-done((bf16[384,1024]{1,0:T(8,128)(2,1)S(1)}, bf16[384,1024]{1,0:T(8,128)(2,1)S(1)}, u32[]{:S(2)}, u32[]{:S(2)}) %collective-permute-start.10) | collective-permute-done | bytes 786464 | tf_op jit(solution)/shard_map/ppermute | solution.py:621
  51.7 2.6 %collective-permute-start.13 = (bf16[384,1024]{1,0:T(8,128)(2,1)S(1)}, bf16[384,1024]{1,0:T(8,128)(2,1)S(1)}, u32[]{:S(2)}, u32[]{:S(2)}) collective-permute-start(bf16[384,1024]{1,0:T(8,128)(2,1)S(1)} %shard_map.102), channel_id=1, source_target_pairs={{0,1},{2,3},{1,0},{3,2},{4,5},{6,7},{5,4},{7,6},{8,9},{10,11},{9,8... | collective-permute-start | bytes 2359304 | tf_op jit(solution)/shard_map/ppermute | solution.py:621
  54.4 2.0 %shard_map.103 = (f32[16,512]{1,0:T(8,128)S(1)}, bf16[512,1024]{1,0:T(8,128)(2,1)S(1)}, bf16[128,1024]{1,0:T(8,128)(2,1)}) custom-call(s32[1,512]{1,0:T(1,128)S(1)} %bitcast.11, bf16[16,512]{1,0:T(8,128)(2,1)S(1)} %shard_map.96.back_ref, bf16[512,2048]{1,0:T(8,128)(2,1)S(1)} %copy-done.1, bf16[384,1024]{1,0:T(8,128)(2,1)S(1)} %get-tuple-element.65.refs_0_.refs_1_, ...), custom_call_target="tpu_custom_call" | custom-call | flops 1 | bytes 1 | tf_op jit(solution)/shard_map/pallas_call | solution.py:120
  56.4 2.1 %shard_map.104 = (f32[16,512]{1,0:T(8,128)S(1)}, bf16[512,1024]{1,0:T(8,128)(2,1)S(1)}, bf16[256,1024]{1,0:T(8,128)(2,1)S(1)}) custom-call(s32[1,512]{1,0:T(1,128)S(1)} %bitcast.12, bf16[16,512]{1,0:T(8,128)(2,1)S(1)} %shard_map.96.back_ref, bf16[512,2048]{1,0:T(8,128)(2,1)S(1)} %copy-done.1, bf16[384,1024]{1,0:T(8,128)(2,1)S(1)} %collective-permute-done.10.refs_0_.refs_2_, ...), custom_call_target="tpu_custom_call" | custom-call | flops 1 | bytes 1 | tf_op jit(solution)/shard_map/pallas_call | solution.py:120
  61.6 5.3 %collective-permute-done.15.got_ref.refs_0_.refs_2_ = bf16[384,1024]{1,0:T(8,128)(2,1)S(1)} collective-permute-done((bf16[384,1024]{1,0:T(8,128)(2,1)S(1)}, bf16[384,1024]{1,0:T(8,128)(2,1)S(1)}, u32[]{:S(2)}, u32[]{:S(2)}) %collective-permute-start.15) | collective-permute-done | bytes 786464 | tf_op jit(solution)/shard_map/ppermute | solution.py:621
  66.9 5.0 %collective-permute-start.20 = (bf16[384,1024]{1,0:T(8,128)(2,1)S(1)}, bf16[384,1024]{1,0:T(8,128)(2,1)S(1)}, u32[]{:S(2)}, u32[]{:S(2)}) collective-permute-start(bf16[384,1024]{1,0:T(8,128)(2,1)S(1)} %shard_map.105), channel_id=1, source_target_pairs={{0,1},{2,3},{1,0},{3,2},{4,5},{6,7},{5,4},{7,6},{8,9},{10,11},{9,8... | collective-permute-start | bytes 2359304 | tf_op jit(solution)/shard_map/ppermute | solution.py:621
  72.8 2.1 %shard_map.107 = (f32[16,512]{1,0:T(8,128)S(1)}, bf16[512,1024]{1,0:T(8,128)(2,1)S(1)}, bf16[128,1024]{1,0:T(8,128)(2,1)S(1)}) custom-call(s32[1,512]{1,0:T(1,128)S(1)} %bitcast.15, bf16[16,512]{1,0:T(8,128)(2,1)S(1)} %shard_map.96.back_ref, bf16[512,2048]{1,0:T(8,128)(2,1)S(1)} %copy-done.1, ...), custom_call_target="tpu_custom_call" | custom-call | flops 1 | bytes 1 | tf_op jit(solution)/shard_map/pallas_call | solution.py:120
  75.0 7.6 %collective-permute-done.12.refs_7_ = bf16[256,1024]{1,0:T(8,128)(2,1)S(1)} collective-permute-done((bf16[256,1024]{1,0:T(8,128)(2,1)S(1)}, bf16[256,1024]{1,0:T(8,128)(2,1)S(1)}, u32[]{:S(2)}, u32[]{:S(2)}) %collective-permute-start.12) | collective-permute-done | bytes 524320 | tf_op jit(solution)/shard_map/ppermute | solution.py:27
  83.5 3.7 %collective-permute-start.18 = (bf16[384,1024]{1,0:T(8,128)(2,1)S(1)}, bf16[384,1024]{1,0:T(8,128)(2,1)S(1)}, u32[]{:S(2)}, u32[]{:S(2)}) collective-permute-start(bf16[384,1024]{1,0:T(8,128)(2,1)S(1)} %shard_map.108), channel_id=1, source_target_pairs={{0,1},{2,3},{1,0},{3,2},{4,5},{6,7},{5,4},{7,6},{8,9},{10,11},{9,8... | collective-permute-start | bytes 2359304 | tf_op jit(solution)/shard_map/ppermute | solution.py:621
  88.8 2.2 %shard_map.110 = (f32[16,512]{1,0:T(8,128)S(1)}, bf16[512,1024]{1,0:T(8,128)(2,1)S(1)}, bf16[256,1024]{1,0:T(8,128)(2,1)S(1)}) custom-call(s32[1,512]{1,0:T(1,128)S(1)} %bitcast.18, bf16[16,512]{1,0:T(8,128)(2,1)S(1)} %shard_map.96.back_ref, bf16[512,2048]{1,0:T(8,128)(2,1)S(1)} %copy-done.1, ...), custom_call_target="tpu_custom_call" | custom-call | flops 1 | bytes 1 | tf_op jit(solution)/shard_map/pallas_call | solution.py:120
  95.8 4.8 %collective-permute-done.20.got_ref.refs_0_.refs_1_ = bf16[384,1024]{1,0:T(8,128)(2,1)S(1)} collective-permute-done((bf16[384,1024]{1,0:T(8,128)(2,1)S(1)}, bf16[384,1024]{1,0:T(8,128)(2,1)S(1)}, u32[]{:S(2)}, u32[]{:S(2)}) %collective-permute-start.20) | collective-permute-done | bytes 786464 | tf_op jit(solution)/shard_map/ppermute | solution.py:621
  100.6 5.7 %collective-permute-start.27 = (bf16[256,1024]{1,0:T(8,128)(2,1)S(1)}, bf16[256,1024]{1,0:T(8,128)(2,1)S(1)}, u32[]{:S(2)}, u32[]{:S(2)}) collective-permute-start(bf16[256,1024]{1,0:T(8,128)(2,1)S(1)} %shard_map.111), channel_id=1, source_target_pairs={{0,1},{2,3},{1,0},{3,2},{4,5},{6,7},{5,4},{7,6},{8,9},{10,11},{9,8... | collective-permute-start | bytes 1572872 | tf_op jit(solution)/shard_map/ppermute | solution.py:621
  110.9 6.6 %collective-permute-done.18.got_ref.refs_0_.refs_1_ = bf16[384,1024]{1,0:T(8,128)(2,1)S(1)} collective-permute-done((bf16[384,1024]{1,0:T(8,128)(2,1)S(1)}, bf16[384,1024]{1,0:T(8,128)(2,1)S(1)}, u32[]{:S(2)}, u32[]{:S(2)}) %collective-permute-start.18) | collective-permute-done | bytes 786464 | tf_op jit(solution)/shard_map/ppermute | solution.py:621
  122.5 6.2 %collective-permute-done.27.refs_0_ = bf16[256,1024]{1,0:T(8,128)(2,1)S(1)} collective-permute-done((bf16[256,1024]{1,0:T(8,128)(2,1)S(1)}, bf16[256,1024]{1,0:T(8,128)(2,1)S(1)}, u32[]{:S(2)}, u32[]{:S(2)}) %collective-permute-start.27) | collective-permute-done | bytes 524320 | tf_op jit(solution)/shard_map/ppermute | solution.py:621
  133.1 2.3 %collective-permute-done.31.refs_1_ = f32[16,512]{1,0:T(8,128)S(1)} collective-permute-done((f32[16,512]{1,0:T(8,128)S(1)}, f32[16,512]{1,0:T(8,128)S(1)}, u32[]{:S(2)}, u32[]{:S(2)}) %collective-permute-start.31) | collective-permute-done | bytes 32800 | tf_op jit(solution)/shard_map/ppermute | solution.py:184
  137.1 3.8 %collective-permute-start.32 = (bf16[256,256]{1,0:T(8,128)(2,1)S(1)}, bf16[256,256]{1,0:T(8,128)(2,1)S(1)}, u32[]{:S(2)}, u32[]{:S(2)}) collective-permute-start(bf16[256,256]{1,0:T(8,128)(2,1)S(1)} %shard_map.125), channel_id=1, source_target_pairs={{0,3},{3,0},{4,7},{7,4},{8,11},{11,8},{12,15},{15,12},{16,19},{19,... | collective-permute-start | bytes 393224 | tf_op jit(solution)/shard_map/ppermute | solution.py:671
  141.0 4.7 %shard_map.120 = bf16[512,2048]{1,0:T(8,128)(2,1)} custom-call(bf16[512,256]{1,0:T(8,128)(2,1)S(1)} %copy-done.4, bf16[512,256]{1,0:T(8,128)(2,1)S(1)} %collective-permute-done.5.refs_1_, bf16[1024,256]{1,0:T(8,128)(2,1)S(1)} %collective-permute-done.6.refs_2_, bf16[512,1024]{1,0:T(8,128)(2,1)S(1)} %copy-done.3, ...), custom_call_target="tpu_custom_call" | custom-call | flops 1 | bytes 1 | tf_op jit(solution)/shard_map/pallas_call | solution.py:120
  (93 shorter events, 47.3 us)
Async XLA Ops:
  4.8 11.3 %collective-permute-start.1 = (bf16[256,256]{1,0:T(8,128)(2,1)S(1)}, bf16[256,256]{1,0:T(8,128)(2,1)S(1)}, u32[]{:S(2)}, u32[]{:S(2)}) collective-permute-start(bf16[256,256]{1,0:T(8,128)(2,1)S(1)} %bitcast.31), channel_id=1, source_target_pairs={{0,2},{1,3},{2,0},{3,1},{4,6},{5,7},{6,4},{7,5},{8,10},{9,11},{10,... | collective-permute-start | bytes 393224 | tf_op jit(solution)/shard_map/ppermute | solution.py:27
  11.3 22.0 %collective-permute-start.7 = (bf16[384,1024]{1,0:T(8,128)(2,1)S(1)}, bf16[384,1024]{1,0:T(8,128)(2,1)S(1)}, u32[]{:S(2)}, u32[]{:S(2)}) collective-permute-start(bf16[384,1024]{1,0:T(8,128)(2,1)S(1)} %get-tuple-element.59.refs_0_.refs_1_), channel_id=1, source_target_pairs={{0,1},{2,3},{1,0},{3,2},{4,5},{6,7},{5,4},{7,6},{8,9},{10,11},{9,8... | collective-permute-start | bytes 2359304 | tf_op jit(solution)/shard_map/ppermute | solution.py:621
  12.0 23.7 %collective-permute-start.8 = (bf16[384,1024]{1,0:T(8,128)(2,1)S(1)}, bf16[384,1024]{1,0:T(8,128)(2,1)S(1)}, u32[]{:S(2)}, u32[]{:S(2)}) collective-permute-start(bf16[384,1024]{1,0:T(8,128)(2,1)S(1)} %get-tuple-element.59.refs_0_.refs_1_), channel_id=1, source_target_pairs={{1,2},{2,1},{5,6},{6,5},{9,10},{10,9},{13,14},{14,13},{17,18},{18,... | collective-permute-start | bytes 2359304 | tf_op jit(solution)/shard_map/ppermute | solution.py:621
  12.8 37.2 %collective-permute-start.10 = (bf16[384,1024]{1,0:T(8,128)(2,1)S(1)}, bf16[384,1024]{1,0:T(8,128)(2,1)S(1)}, u32[]{:S(2)}, u32[]{:S(2)}) collective-permute-start(bf16[384,1024]{1,0:T(8,128)(2,1)S(1)} %get-tuple-element.65.refs_0_.refs_1_), channel_id=1, source_target_pairs={{0,1},{2,3},{1,0},{3,2},{4,5},{6,7},{5,4},{7,6},{8,9},{10,11},{9,8... | collective-permute-start | bytes 2359304 | tf_op jit(solution)/shard_map/ppermute | solution.py:621
  16.9 33.9 %collective-permute-start.11 = (bf16[384,1024]{1,0:T(8,128)(2,1)S(1)}, bf16[384,1024]{1,0:T(8,128)(2,1)S(1)}, u32[]{:S(2)}, u32[]{:S(2)}) collective-permute-start(bf16[384,1024]{1,0:T(8,128)(2,1)S(1)} %get-tuple-element.65.refs_0_.refs_1_), channel_id=1, source_target_pairs={{1,2},{2,1},{5,6},{6,5},{9,10},{10,9},{13,14},{14,13},{17,18},{18,... | collective-permute-start | bytes 2359304 | tf_op jit(solution)/shard_map/ppermute | solution.py:621
  22.1 11.9 %collective-permute-start.5 = (bf16[512,256]{1,0:T(8,128)(2,1)S(1)}, bf16[512,256]{1,0:T(8,128)(2,1)S(1)}, u32[]{:S(2)}, u32[]{:S(2)}) collective-permute-start(bf16[512,256]{1,0:T(8,128)(2,1)S(1)} %copy-done.4), channel_id=1, source_target_pairs={{0,4},{4,0},{8,12},{12,8},{1,5},{5,1},{9,13},{13,9},{2,6},{6,2},{1... | collective-permute-start | bytes 786440 | tf_op jit(solution)/shard_map/ppermute | solution.py:220
  33.2 26.9 %collective-permute-start.16 = (bf16[384,1024]{1,0:T(8,128)(2,1)S(1)}, bf16[384,1024]{1,0:T(8,128)(2,1)S(1)}, u32[]{:S(2)}, u32[]{:S(2)}) collective-permute-start(bf16[384,1024]{1,0:T(8,128)(2,1)S(1)} %collective-permute-done.7.refs_0_.refs_2_), channel_id=1, source_target_pairs={{1,2},{2,1},{5,6},{6,5},{9,10},{10,9},{13,14},{14,13},{17,18},{18,... | collective-permute-start | bytes 2359304 | tf_op jit(solution)/shard_map/ppermute | solution.py:621
  34.0 24.6 %collective-permute-start.6 = (bf16[1024,256]{1,0:T(8,128)(2,1)S(1)}, bf16[1024,256]{1,0:T(8,128)(2,1)S(1)}, u32[]{:S(2)}, u32[]{:S(2)}) collective-permute-start(bf16[1024,256]{1,0:T(8,128)(2,1)S(1)} %shard_map.97), channel_id=1, source_target_pairs={{0,8},{4,12},{8,0},{12,4},{1,9},{5,13},{9,1},{13,5},{2,10},{6,14},... | collective-permute-start | bytes 1572872 | tf_op jit(solution)/shard_map/ppermute | solution.py:220
  36.6 30.3 %collective-permute-start.15 = (bf16[384,1024]{1,0:T(8,128)(2,1)S(1)}, bf16[384,1024]{1,0:T(8,128)(2,1)S(1)}, u32[]{:S(2)}, u32[]{:S(2)}) collective-permute-start(bf16[384,1024]{1,0:T(8,128)(2,1)S(1)} %shard_map.99), channel_id=1, source_target_pairs={{0,1},{2,3},{1,0},{3,2},{4,5},{6,7},{5,4},{7,6},{8,9},{10,11},{9,8... | collective-permute-start | bytes 2359304 | tf_op jit(solution)/shard_map/ppermute | solution.py:621
  50.1 32.5 %collective-permute-start.14 = (bf16[384,1024]{1,0:T(8,128)(2,1)S(1)}, bf16[384,1024]{1,0:T(8,128)(2,1)S(1)}, u32[]{:S(2)}, u32[]{:S(2)}) collective-permute-start(bf16[384,1024]{1,0:T(8,128)(2,1)S(1)} %collective-permute-done.10.refs_0_.refs_2_), channel_id=1, source_target_pairs={{1,2},{2,1},{5,6},{6,5},{9,10},{10,9},{13,14},{14,13},{17,18},{18,... | collective-permute-start | bytes 2359304 | tf_op jit(solution)/shard_map/ppermute | solution.py:621
  51.7 36.1 %collective-permute-start.13 = (bf16[384,1024]{1,0:T(8,128)(2,1)S(1)}, bf16[384,1024]{1,0:T(8,128)(2,1)S(1)}, u32[]{:S(2)}, u32[]{:S(2)}) collective-permute-start(bf16[384,1024]{1,0:T(8,128)(2,1)S(1)} %shard_map.102), channel_id=1, source_target_pairs={{0,1},{2,3},{1,0},{3,2},{4,5},{6,7},{5,4},{7,6},{8,9},{10,11},{9,8... | collective-permute-start | bytes 2359304 | tf_op jit(solution)/shard_map/ppermute | solution.py:621
  58.6 16.4 %collective-permute-start.9 = (bf16[256,1024]{1,0:T(8,128)(2,1)S(1)}, bf16[256,1024]{1,0:T(8,128)(2,1)S(1)}, u32[]{:S(2)}, u32[]{:S(2)}) collective-permute-start(bf16[256,1024]{1,0:T(8,128)(2,1)S(1)} %get-tuple-element.64.refs_4_), channel_id=1, source_target_pairs={{0,16},{16,0},{1,17},{17,1},{2,18},{18,2},{3,19},{19,3},{4,20},{20... | collective-permute-start | bytes 1572872 | tf_op jit(solution)/shard_map/ppermute | solution.py:27
  60.2 22.4 %collective-permute-start.12 = (bf16[256,1024]{1,0:T(8,128)(2,1)S(1)}, bf16[256,1024]{1,0:T(8,128)(2,1)S(1)}, u32[]{:S(2)}, u32[]{:S(2)}) collective-permute-start(bf16[256,1024]{1,0:T(8,128)(2,1)S(1)} %get-tuple-element.74.refs_6_), channel_id=1, source_target_pairs={{0,16},{16,0},{1,17},{17,1},{2,18},{18,2},{3,19},{19,3},{4,20},{20... | collective-permute-start | bytes 1572872 | tf_op jit(solution)/shard_map/ppermute | solution.py:27
  66.9 33.7 %collective-permute-start.20 = (bf16[384,1024]{1,0:T(8,128)(2,1)S(1)}, bf16[384,1024]{1,0:T(8,128)(2,1)S(1)}, u32[]{:S(2)}, u32[]{:S(2)}) collective-permute-start(bf16[384,1024]{1,0:T(8,128)(2,1)S(1)} %shard_map.105), channel_id=1, source_target_pairs={{0,1},{2,3},{1,0},{3,2},{4,5},{6,7},{5,4},{7,6},{8,9},{10,11},{9,8... | collective-permute-start | bytes 2359304 | tf_op jit(solution)/shard_map/ppermute | solution.py:621
  83.5 34.0 %collective-permute-start.18 = (bf16[384,1024]{1,0:T(8,128)(2,1)S(1)}, bf16[384,1024]{1,0:T(8,128)(2,1)S(1)}, u32[]{:S(2)}, u32[]{:S(2)}) collective-permute-start(bf16[384,1024]{1,0:T(8,128)(2,1)S(1)} %shard_map.108), channel_id=1, source_target_pairs={{0,1},{2,3},{1,0},{3,2},{4,5},{6,7},{5,4},{7,6},{8,9},{10,11},{9,8... | collective-permute-start | bytes 2359304 | tf_op jit(solution)/shard_map/ppermute | solution.py:621
  91.1 18.9 %collective-permute-start.17 = (bf16[256,1024]{1,0:T(8,128)(2,1)S(1)}, bf16[256,1024]{1,0:T(8,128)(2,1)S(1)}, u32[]{:S(2)}, u32[]{:S(2)}) collective-permute-start(bf16[256,1024]{1,0:T(8,128)(2,1)S(1)} %get-tuple-element.88.refs_8_), channel_id=1, source_target_pairs={{0,16},{16,0},{1,17},{17,1},{2,18},{18,2},{3,19},{19,3},{4,20},{20... | collective-permute-start | bytes 1572872 | tf_op jit(solution)/shard_map/ppermute | solution.py:27
  92.7 17.3 %collective-permute-start.19 = (bf16[256,1024]{1,0:T(8,128)(2,1)S(1)}, bf16[256,1024]{1,0:T(8,128)(2,1)S(1)}, u32[]{:S(2)}, u32[]{:S(2)}) collective-permute-start(bf16[256,1024]{1,0:T(8,128)(2,1)S(1)} %shard_map.109), channel_id=1, source_target_pairs={{1,2},{2,1},{5,6},{6,5},{9,10},{10,9},{13,14},{14,13},{17,18},{18,... | collective-permute-start | bytes 1572872 | tf_op jit(solution)/shard_map/ppermute | solution.py:621
  93.4 13.8 %collective-permute-start.23 = (f32[16,512]{1,0:T(8,128)S(1)}, f32[16,512]{1,0:T(8,128)S(1)}, u32[]{:S(2)}, u32[]{:S(2)}) collective-permute-start(f32[16,512]{1,0:T(8,128)S(1)} %shard_map.114.refs_0_), channel_id=1, source_target_pairs={{0,8},{4,12},{8,0},{12,4},{1,9},{5,13},{9,1},{13,5},{2,10},{6,14},... | collective-permute-start | bytes 98312 | tf_op jit(solution)/shard_map/ppermute | solution.py:184
  100.6 28.1 %collective-permute-start.27 = (bf16[256,1024]{1,0:T(8,128)(2,1)S(1)}, bf16[256,1024]{1,0:T(8,128)(2,1)S(1)}, u32[]{:S(2)}, u32[]{:S(2)}) collective-permute-start(bf16[256,1024]{1,0:T(8,128)(2,1)S(1)} %shard_map.111), channel_id=1, source_target_pairs={{0,1},{2,3},{1,0},{3,2},{4,5},{6,7},{5,4},{7,6},{8,9},{10,11},{9,8... | collective-permute-start | bytes 1572872 | tf_op jit(solution)/shard_map/ppermute | solution.py:621
  107.2 21.5 %collective-permute-start.28 = (bf16[256,1024]{1,0:T(8,128)(2,1)S(1)}, bf16[256,1024]{1,0:T(8,128)(2,1)S(1)}, u32[]{:S(2)}, u32[]{:S(2)}) collective-permute-start(bf16[256,1024]{1,0:T(8,128)(2,1)S(1)} %shard_map.112), channel_id=1, source_target_pairs={{1,2},{2,1},{5,6},{6,5},{9,10},{10,9},{13,14},{14,13},{17,18},{18,... | collective-permute-start | bytes 1572872 | tf_op jit(solution)/shard_map/ppermute | solution.py:621
  117.5 28.4 %collective-permute-start.25 = (bf16[320,1024]{1,0:T(8,128)(2,1)S(1)}, bf16[320,1024]{1,0:T(8,128)(2,1)S(1)}, u32[]{:S(2)}, u32[]{:S(2)}) collective-permute-start(bf16[320,1024]{1,0:T(8,128)(2,1)S(1)} %shard_map.117), channel_id=1, source_target_pairs={{0,1},{2,3},{1,0},{3,2},{4,5},{6,7},{5,4},{7,6},{8,9},{10,11},{9,8... | collective-permute-start | bytes 1966088 | tf_op jit(solution)/shard_map/ppermute | solution.py:621
  118.7 27.3 %collective-permute-start.26 = (bf16[320,1024]{1,0:T(8,128)(2,1)S(1)}, bf16[320,1024]{1,0:T(8,128)(2,1)S(1)}, u32[]{:S(2)}, u32[]{:S(2)}) collective-permute-start(bf16[320,1024]{1,0:T(8,128)(2,1)S(1)} %shard_map.118), channel_id=1, source_target_pairs={{1,2},{2,1},{5,6},{6,5},{9,10},{10,9},{13,14},{14,13},{17,18},{18,... | collective-permute-start | bytes 1966088 | tf_op jit(solution)/shard_map/ppermute | solution.py:621
  120.9 20.1 %collective-permute-start.24 = (bf16[256,1024]{1,0:T(8,128)(2,1)S(1)}, bf16[256,1024]{1,0:T(8,128)(2,1)S(1)}, u32[]{:S(2)}, u32[]{:S(2)}) collective-permute-start(bf16[256,1024]{1,0:T(8,128)(2,1)S(1)} %get-tuple-element.102.refs_10_), channel_id=1, source_target_pairs={{0,16},{16,0},{1,17},{17,1},{2,18},{18,2},{3,19},{19,3},{4,20},{20... | collective-permute-start | bytes 1572872 | tf_op jit(solution)/shard_map/ppermute | solution.py:27
  135.5 12.0 %collective-permute-start.29 = (bf16[256,256]{1,0:T(8,128)(2,1)S(1)}, bf16[256,256]{1,0:T(8,128)(2,1)S(1)}, u32[]{:S(2)}, u32[]{:S(2)}) collective-permute-start(bf16[256,256]{1,0:T(8,128)(2,1)S(1)} %get-tuple-element.108), channel_id=1, source_target_pairs={{0,2},{1,3},{2,0},{3,1},{4,6},{5,7},{6,4},{7,5},{8,10},{9,11},{10,... | collective-permute-start | bytes 393224 | tf_op jit(solution)/shard_map/ppermute | solution.py:667
  (17 other events, 131.9 us)
